TPU v7x, 128 devices: a whole 4x4x4 slice. The times are simulated.
128 devices in a mesh: scan: 32 (over y, z, x_lo), beam: 4 (over x_hi, core).
Axes of the slice: x: 4 (x_hi: 2, x_lo: 2; x = x_hi * 2 + x_lo), y: 4, z: 4, core: 2. Of those that a mesh axis runs over, the one named last changes fastest.
Arguments:
- smatrix: bfloat16 [2, 1024, 2048, 128], P(None, 'beam', 'scan'), may hold values from -6 to 6
- beam_freq: int32 [2, 1024], P(None, 'beam'), may hold values from -32 to 31
- beam_amp: float32 [2, 1024], P(None, 'beam'), may hold values from -0.1875 to 0.1875
- row_offset: int32 [2048], P('scan'), may hold values from 0 to 63
- col_offset: int32 [2048], P('scan'), may hold values from 0 to 127
- counts: int32 [32], P('scan'), may hold values from 16 to 64, as said below
- amplitude: float32 [2048, 128, 128], P('scan'), may hold values from 0.25 to 2
Outputs:
- grad_smatrix: bfloat16 [2, 1024, 2048, 128], P(None, 'beam', 'scan')
Inputs may be any that keep to these rules, and one draw needn't show every extreme that they name: `counts`: slots of a tile at or past its count are unused; some tile holds exactly 64 live positions.
All inputs are finite; a program needn't handle non-finite values.
Results may differ from a plain program's by a relative error of at most 0.0063.
Values may be sent and summed in bfloat16 or wider, within the bound.
No kernel may reach another device: no remote copies, remote signals or barrier semaphores. Data moves between devices by JAX's collectives and lax.ppermute only.
A program may use at most 192 MiB of HBM per device.

v0:
```python
import math

import jax
import jax.numpy as jnp
from jax import lax
from jax.sharding import PartitionSpec as P

TWO_PI = 6.283185307179586
ETA = 0.1


def passed_along(value, axis, by):
    devices = lax.axis_size(axis)
    return lax.ppermute(value, axis, [(i, (i + by) % devices) for i in range(devices)])


def coefficients(
    tile_rows, tile_cols, tile_ids, beam_freq, beam_amp, strip_rows, field_rows, window
):
    global_rows = tile_ids * strip_rows + tile_rows
    along_rows = beam_freq[0][None, :] * global_rows[:, None] % field_rows
    along_cols = beam_freq[1][None, :] * tile_cols[:, None] % window
    phase_turns = (
        along_rows.astype(jnp.float32) / field_rows + along_cols.astype(jnp.float32) / window
    )
    phase_angle = -TWO_PI * phase_turns
    cos_part = jnp.cos(phase_angle)
    sin_part = jnp.sin(phase_angle)
    coef_re = beam_amp[0][None, :] * cos_part - beam_amp[1][None, :] * sin_part
    coef_im = beam_amp[0][None, :] * sin_part + beam_amp[1][None, :] * cos_part
    return (coef_re.astype(jnp.bfloat16), coef_im.astype(jnp.bfloat16))


def forward_matrix(coef_re, coef_im):
    real_rows = jnp.concatenate([coef_re, -coef_im], axis=1)
    imag_rows = jnp.concatenate([coef_im, coef_re], axis=1)
    return jnp.concatenate([real_rows, imag_rows], axis=0)


def backward_matrix(coef_re, coef_im):
    real_rows = jnp.concatenate([coef_re.T, coef_im.T], axis=1)
    imag_rows = jnp.concatenate([-coef_im.T, coef_re.T], axis=1)
    return jnp.concatenate([real_rows, imag_rows], axis=0)


def dft_tables(window):
    counter = jnp.arange(window, dtype=jnp.int32)
    product = counter[:, None] * counter[None, :] % window
    turn_angle = product.astype(jnp.float32) * (TWO_PI / window)
    norm_scale = 1.0 / math.sqrt(window)
    return (jnp.cos(turn_angle) * norm_scale, -jnp.sin(turn_angle) * norm_scale)


def transform(real_in, imag_in, table_re, table_im):
    highest = lax.Precision.HIGHEST
    left_re = jnp.einsum("jk,qkl->qjl", table_re, real_in, precision=highest) - jnp.einsum(
        "jk,qkl->qjl", table_im, imag_in, precision=highest
    )
    left_im = jnp.einsum("jk,qkl->qjl", table_re, imag_in, precision=highest) + jnp.einsum(
        "jk,qkl->qjl", table_im, real_in, precision=highest
    )
    out_re = jnp.einsum("qjk,kl->qjl", left_re, table_re, precision=highest) - jnp.einsum(
        "qjk,kl->qjl", left_im, table_im, precision=highest
    )
    out_im = jnp.einsum("qjk,kl->qjl", left_re, table_im, precision=highest) + jnp.einsum(
        "qjk,kl->qjl", left_im, table_re, precision=highest
    )
    return (out_re, out_im)


def far_field_gradient(wave_re, wave_im, measured, live_rows, tables):
    table_re, table_im = tables
    far_re, far_im = transform(wave_re, wave_im, table_re, table_im)
    modulus = jnp.sqrt(far_re * far_re + far_im * far_im + ETA)
    keep_share = 1.0 - measured / modulus
    back_re, back_im = transform(far_re * keep_share, far_im * keep_share, table_re, -table_im)
    live_mask = live_rows[:, None, None]
    return jnp.stack([back_re * live_mask, back_im * live_mask], axis=0).astype(jnp.bfloat16)


def selection(tile_rows, window, total_rows, dtype):
    field_index = jnp.arange(total_rows, dtype=jnp.int32)
    window_index = jnp.arange(window, dtype=jnp.int32)
    target = tile_rows[:, None, None] + window_index[None, None, :]
    return (field_index[None, :, None] == target).astype(dtype)


def take_window(strip_waves, tile_rows, window):
    picker = selection(tile_rows, window, strip_waves.shape[2], jnp.float32)
    return jnp.einsum("pyj,cpyx->cpjx", picker, strip_waves, precision=lax.Precision.HIGHEST)


def place_rows(wave_grads, tile_rows, total_rows):
    picker = selection(tile_rows, wave_grads.shape[2], total_rows, jnp.bfloat16)
    placed = jnp.einsum("pyj,cpjx->cpyx", picker, wave_grads, preferred_element_type=jnp.float32)
    return placed.astype(jnp.bfloat16)


def beam_fourier(strip_waves, row_offset, amplitude, live_rows, tables, window):
    windows = take_window(strip_waves, row_offset, window)
    summed = lax.psum(windows, "beam")
    return far_field_gradient(summed[0], summed[1], amplitude, live_rows, tables)


def body(smatrix, beam_freq, beam_amp, row_offset, col_offset, counts, amplitude):
    beam_dev = smatrix.shape[1]
    strip_rows = smatrix.shape[2]
    window = smatrix.shape[3]
    per_tile = row_offset.shape[0]
    scan_size = lax.axis_size("scan")
    field_rows = strip_rows * scan_size
    my_tile = lax.axis_index("scan")
    tables = dft_tables(window)
    rows_list = [row_offset]
    cols_list = [col_offset]
    ids_list = [jnp.full((per_tile,), my_tile, jnp.int32)]
    for distance in (1, 2):
        moved_rows, moved_cols = passed_along((row_offset, col_offset), "scan", distance)
        rows_list.append(moved_rows)
        cols_list.append(moved_cols)
        ids_list.append(jnp.full((per_tile,), (my_tile - distance) % scan_size, jnp.int32))
    coef_re, coef_im = coefficients(
        jnp.concatenate(rows_list),
        jnp.concatenate(cols_list),
        jnp.concatenate(ids_list),
        beam_freq,
        beam_amp,
        strip_rows,
        field_rows,
        window,
    )
    live_rows = (jnp.arange(per_tile, dtype=jnp.int32) < counts[0]).astype(jnp.float32)
    pieces = [smatrix]
    for distance in (1, 2):
        pieces.append(passed_along(smatrix, "scan", -distance))
    extended = jnp.concatenate(pieces, axis=2).reshape(2 * beam_dev, 3 * strip_rows * window)
    own_matrix = forward_matrix(coef_re[:per_tile], coef_im[:per_tile])
    strip_waves = jnp.dot(own_matrix, extended, preferred_element_type=jnp.float32).reshape(
        2, per_tile, 3 * strip_rows, window
    )
    wave_grads = beam_fourier(strip_waves, row_offset, amplitude, live_rows, tables, window)
    placed = place_rows(wave_grads, row_offset, 3 * strip_rows)
    grad_parts = [placed[:, :, 0:strip_rows]]
    for distance in (1, 2):
        grad_parts.append(
            passed_along(
                placed[:, :, distance * strip_rows : (distance + 1) * strip_rows], "scan", distance
            )
        )
    gathered = jnp.stack(grad_parts, axis=1).reshape(6 * per_tile, strip_rows * window)
    gradient = jnp.dot(
        backward_matrix(coef_re, coef_im), gathered, preferred_element_type=jnp.float32
    )
    return gradient.astype(jnp.bfloat16).reshape(2, beam_dev, strip_rows, window)


def solution(mesh):
    return jax.shard_map(
        body,
        mesh=mesh,
        in_specs=(
            P(None, "beam", "scan", None),
            P(None, "beam"),
            P(None, "beam"),
            P("scan"),
            P("scan"),
            P("scan"),
            P("scan", None, None),
        ),
        out_specs=P(None, "beam", "scan", None),
        check_vma=False,
    )
```

profile of v0, /device:TPU:1, one launch (start us, length us, event | category | flops | bytes accessed | tf_op | source)
XLA Modules:
  0.0 901.0 jit_solution(504833085663088691)
XLA Ops:
  6.5 8.0 collective-permute-start.4
  19.4 175.1 %collective-permute-done.2 = s32[64]{0:T(128)S(1)} collective-permute-done((s32[64]{0:T(128)}, s32[64]{0:T(128)S(1)}, u32[]{:S(2)}, u32[]{:S(2)}) %collective-permute-start.2) | collective-permute-done | bytes 288 | tf_op jit(solution)/shard_map/ppermute | solution.py:14
  195.3 5.1 collective-permute-done.1
  202.1 20.6 %pad_maximum_fusion = bf16[2,256,192,128]{3,2,1,0:T(8,128)(2,1)} fusion(bf16[2,256,64,128]{3,2,1,0:T(8,128)(2,1)} %collective-permute-done.5, bf16[2,256,64,128]{3,2,1,0:T(8,128)(2,1)} %collective-permute-done.4, bf16[2,256,64,128]{3,2,1,0:T(8,128)(2,1)} %param.7), kind=kLoop, calls=%fused_computation.1 | loop fusion | flops 75497472 | bytes 50331648 | tf_op jit(solution)/shard_map/concatenate | solution.py:136
  222.7 25.7 %copy.72 = bf16[64,8,192,128]{3,1,2,0:T(8,128)(2,1)S(1)} copy(bf16[64,8,192,128]{3,2,1,0:T(8,128)(2,1)} %bitcast.138) | data formatting | bytes 50331648
  248.4 9.1 %copy.52 = bf16[64,8,192,128]{3,2,1,0:T(8,128)(2,1)} copy(bf16[64,8,192,128]{3,1,2,0:T(8,128)(2,1)S(1)} %copy.72) | data formatting | bytes 50331648
  257.5 36.5 %fusion = f32[2,64,192,128]{3,1,2,0:T(8,128)} fusion(bf16[2,64,512,1]{2,1,3,0:T(8,128)(2,1)S(1)} %bitcast.142, bf16[192,128,512,1]{1,0,2,3:T(8,128)(2,1)} %bitcast.137), kind=kOutput, calls=%fused_computation.2 | convolution fusion | flops 3221225472 | bytes 37879808 | tf_op jit(solution)/shard_map/dot_general | solution.py:138
  293.9 27.2 %fusion.40 = f32[2,64,128,128]{2,3,0,1:T(8,128)} fusion(f32[2,64,192,128]{3,1,2,0:T(8,128)} %fusion, s32[64,128]{1,0:T(8,128)S(1)} %iota_add_fusion), kind=kOutput, calls=%fused_computation.44 | convolution fusion | flops 4833411072 | bytes 21004288 | tf_op jit(solution)/shard_map/pyj,cpyx->cpjx/dot_general | solution.py:90
  321.8 333.5 %all-reduce.2.cloned.1.call-done = f32[2,64,128,128]{2,3,0,1:T(8,128)} async-done(((f32[2,64,128,128]{2,3,0,1:T(8,128)}), f32[2,64,128,128]{2,3,0,1:T(8,128)}) %all-reduce.2.cloned.1.call-update) | async-done | bytes 8388624 | tf_op jit(solution)/shard_map/psum | solution.py:101
  655.3 6.2 fusion.32
  661.5 3.8 fusion.48
  665.3 6.9 fusion.23
  672.2 7.3 fusion.21
  679.5 3.8 fusion.33
  683.3 4.3 fusion.47
  687.7 7.1 fusion.49
  694.8 7.4 fusion.52
  702.2 7.6 fusion.107
  709.9 8.0 fusion.104
  717.9 8.1 convolution_add_fusion
  726.0 6.9 fusion.15
  732.8 7.0 fusion.13
  739.9 8.3 convolution_subtract_fusion
  748.2 7.9 fusion.59
  756.1 7.9 fusion.62
  764.0 2.0 convert_bitcast_fusion
  766.0 2.0 slice_bitcast_fusion.10
  772.7 46.5 %collective-permute-done.6 = bf16[2,64,64,128]{3,2,0,1:T(8,128)(2,1)S(1)} collective-permute-done((bf16[2,64,64,128]{3,2,0,1:T(8,128)(2,1)S(1)}, bf16[2,64,64,128]{3,2,0,1:T(8,128)(2,1)S(1)}, u32[]{:S(2)}, u32[]{:S(2)}) %collective-permute-start.6) | collective-permute-done | bytes 2097184 | tf_op jit(solution)/shard_map/ppermute | solution.py:14
  819.3 44.8 %collective-permute-done.7 = bf16[2,64,64,128]{3,2,0,1:T(8,128)(2,1)S(1)} collective-permute-done((bf16[2,64,64,128]{3,2,0,1:T(8,128)(2,1)S(1)}, bf16[2,64,64,128]{3,2,0,1:T(8,128)(2,1)S(1)}, u32[]{:S(2)}, u32[]{:S(2)}) %collective-permute-start.7) | collective-permute-done | bytes 2097184 | tf_op jit(solution)/shard_map/ppermute | solution.py:14
  865.0 2.1 copy.34
  867.1 17.4 %fusion.10 = bf16[64,8,64,128]{3,1,2,0:T(8,128)(2,1)} fusion(bf16[48,8,64,128]{3,2,1,0:T(8,128)(2,1)S(1)} %bitcast.139, bf16[256,192]{1,0:T(8,128)(2,1)S(1)} %get-tuple-element.11, bf16[256,192]{1,0:T(8,128)(2,1)S(1)} %fusion.202, bf16[256,192]{1,0:T(8,128)(2,1)S(1)} %get-tuple-element.10), kind=kOutput, calls=%fused_computation.14 | convolution fusion | flops 3226992640 | bytes 14974976 | tf_op jit(solution)/shard_map/dot_general | solution.py:151
  884.5 9.5 %copy.54 = bf16[64,8,64,128]{3,2,1,0:T(8,128)(2,1)} copy(bf16[64,8,64,128]{3,1,2,0:T(8,128)(2,1)} %fusion.10) | data formatting | bytes 16777216
  (33 shorter events, 13.0 us)
Async XLA Ops:
  6.5 648.8 %all-reduce.2.cloned.1.call-start = ((), (), s32[]{:S(2)}) async-start(), calls=%async_computation | async-start | bytes 16777216 | tf_op jit(solution)/shard_map/psum | solution.py:101
  6.5 195.6 %collective-permute-start.4 = (bf16[2,256,64,128]{3,2,1,0:T(8,128)(2,1)}, bf16[2,256,64,128]{3,2,1,0:T(8,128)(2,1)}, u32[]{:S(2)}, u32[]{:S(2)}) collective-permute-start(bf16[2,256,64,128]{3,2,1,0:T(8,128)(2,1)} %param.7), channel_id=1, source_target_pairs={{0,124},{4,0},{8,4},{12,8},{16,12},{20,16},{24,20},{28,24},{32,28}... | collective-permute-start | bytes 25165832 | tf_op jit(solution)/shard_map/ppermute | solution.py:14
  14.5 187.6 %collective-permute-start.5 = (bf16[2,256,64,128]{3,2,1,0:T(8,128)(2,1)}, bf16[2,256,64,128]{3,2,1,0:T(8,128)(2,1)}, u32[]{:S(2)}, u32[]{:S(2)}) collective-permute-start(bf16[2,256,64,128]{3,2,1,0:T(8,128)(2,1)} %param.7), channel_id=1, source_target_pairs={{0,120},{4,124},{8,0},{12,4},{16,8},{20,12},{24,16},{28,20},{32,24... | collective-permute-start | bytes 25165832 | tf_op jit(solution)/shard_map/ppermute | solution.py:14
  14.6 179.9 %collective-permute-start.2 = (s32[64]{0:T(128)}, s32[64]{0:T(128)S(1)}, u32[]{:S(2)}, u32[]{:S(2)}) collective-permute-start(s32[64]{0:T(128)} %param.11), channel_id=1, source_target_pairs={{0,4},{4,8},{8,12},{12,16},{16,20},{20,24},{24,28},{28,32},{32,36}... | collective-permute-start | bytes 776 | tf_op jit(solution)/shard_map/ppermute | solution.py:14
  15.0 179.5 %collective-permute-start.3 = (s32[64]{0:T(128)}, s32[64]{0:T(128)S(1)}, u32[]{:S(2)}, u32[]{:S(2)}) collective-permute-start(s32[64]{0:T(128)} %param.11), channel_id=1, source_target_pairs={{0,8},{4,12},{8,16},{12,20},{16,24},{20,28},{24,32},{28,36},{32,40... | collective-permute-start | bytes 776 | tf_op jit(solution)/shard_map/ppermute | solution.py:14
  16.0 179.3 %collective-permute-start = (s32[64]{0:T(128)}, s32[64]{0:T(128)S(1)}, u32[]{:S(2)}, u32[]{:S(2)}) collective-permute-start(s32[64]{0:T(128)} %param.10), channel_id=1, source_target_pairs={{0,4},{4,8},{8,12},{12,16},{16,20},{20,24},{24,28},{28,32},{32,36}... | collective-permute-start | bytes 776 | tf_op jit(solution)/shard_map/ppermute | solution.py:14
  194.5 5.8 collective-permute-start.1
  655.3 6.2 copy-start.1
  694.8 7.4 copy-start
  768.0 51.3 %collective-permute-start.6 = (bf16[2,64,64,128]{3,2,0,1:T(8,128)(2,1)S(1)}, bf16[2,64,64,128]{3,2,0,1:T(8,128)(2,1)S(1)}, u32[]{:S(2)}, u32[]{:S(2)}) collective-permute-start(bf16[2,64,64,128]{3,2,0,1:T(8,128)(2,1)S(1)} %get-tuple-element.9), channel_id=1, source_target_pairs={{0,4},{4,8},{8,12},{12,16},{16,20},{20,24},{24,28},{28,32},{32,36}... | collective-permute-start | bytes 6291464 | tf_op jit(solution)/shard_map/ppermute | solution.py:14
  768.4 95.8 %collective-permute-start.7 = (bf16[2,64,64,128]{3,2,0,1:T(8,128)(2,1)S(1)}, bf16[2,64,64,128]{3,2,0,1:T(8,128)(2,1)S(1)}, u32[]{:S(2)}, u32[]{:S(2)}) collective-permute-start(bf16[2,64,64,128]{3,2,0,1:T(8,128)(2,1)S(1)} %get-tuple-element.8), channel_id=1, source_target_pairs={{0,8},{4,12},{8,16},{12,20},{16,24},{20,28},{24,32},{28,36},{32,40... | collective-permute-start | bytes 6291464 | tf_op jit(solution)/shard_map/ppermute | solution.py:14
Sparse Core Ops, SparseCore 0:
  321.3 333.9 all-reduce.1
where the time goes:
time: 906 us; the launch traced here: 901 us
  waiting for transfers between devices  605 us (67%)
  matrix products  192 us (21%)
  local copies, waits for them, and re-layouts  49.8 us (5%)
  other arithmetic  27.6 us (3%)
  between operations  14.5 us (2%)
  starting transfers between devices  12.4 us (1%)
    psum x1, waiting for transfers between devices, beam_fourier(): summed = lax.psum(windows, 'beam')  333 us
    ppermute x8, waiting for transfers between devices, passed_along(): lax.ppermute(value, axis, [(i, (i + by) % devices) for i in range(devices)])  272 us
    unnamed x7, local copies, waits for them, and re-layouts  44.2 us
    dot_general x1, matrix products, body(): jnp.dot(own_matrix, extended, preferred_element_type=jnp.float32)  36.5 us
    dot_general x1, matrix products, take_window(): jnp.einsum('pyj,cpyx->cpjx', picker, strip_waves, precision=lax.Precision...  27.2 us
    concatenate x1, other arithmetic, body(): jnp.concatenate(pieces, axis=2)  20.6 us
  transfers between devices with their start and end apart: 9, of which 5 were waited for; matrix products, arithmetic and copies ran while one was open for 1% of the time, Pallas kernels for 0%

commit v1 on v0

v1 whole, which is shorter than its diff:
```python
import math

import jax
import jax.numpy as jnp
import ml_dtypes
import numpy as np
from jax import lax
from jax.experimental import pallas as pl
from jax.experimental.pallas import tpu as pltpu
from jax.sharding import PartitionSpec as P

TWO_PI = 6.283185307179586
ETA = 0.1
BF16 = jnp.bfloat16
F32 = jnp.float32
AXES = ("scan", "beam")
Y_BLOCK = 16


def permutation(scan_size, target):
    pairs = []
    for s in range(scan_size):
        for hi in range(2):
            for core in range(2):
                ts, th, tc = target(s, hi, core)
                pairs.append(((s * 2 + hi) * 2 + core, ((ts % scan_size) * 2 + th) * 2 + tc))
    return pairs


def coefficients(rows, cols, ids, beam_freq, beam_amp, strip_rows, field_rows, window):
    global_rows = ids * strip_rows + rows
    along_rows = beam_freq[0][None, :] * global_rows[:, None] % field_rows
    along_cols = beam_freq[1][None, :] * cols[:, None] % window
    phase_turns = (
        along_rows.astype(F32) / field_rows + along_cols.astype(F32) / window
    )
    phase_angle = -TWO_PI * phase_turns
    cos_part = jnp.cos(phase_angle)
    sin_part = jnp.sin(phase_angle)
    coef_re = beam_amp[0][None, :] * cos_part - beam_amp[1][None, :] * sin_part
    coef_im = beam_amp[0][None, :] * sin_part + beam_amp[1][None, :] * cos_part
    return (coef_re.astype(BF16), coef_im.astype(BF16))


def dft_matrices(window):
    counter = np.arange(window)
    angle = (counter[:, None] * counter[None, :] % window) * (2.0 * math.pi / window)
    re = np.cos(angle) / math.sqrt(window)
    im = -np.sin(angle) / math.sqrt(window)
    full = np.block([[re, im], [-im, re]])
    high = full.astype(ml_dtypes.bfloat16)
    low = (full - high.astype(np.float64)).astype(ml_dtypes.bfloat16)
    return np.stack([high, low, high.T, low.T])


def split(value):
    high = value.astype(BF16)
    return high, (value - high.astype(F32)).astype(BF16)


def dot(left, right):
    return jnp.dot(left, right, preferred_element_type=F32)


def right_product(value, high, low):
    value_hi, value_lo = split(value)
    return dot(value_hi, high) + (dot(value_lo, high) + dot(value_hi, low))


def left_product(high, low, value):
    value_hi, value_lo = split(value)
    return dot(high, value_hi) + (dot(high, value_lo) + dot(low, value_hi))


def forward_kernel(coef_ref, field_ref, *out_refs):
    parts = field_ref.shape[0]
    beams = field_ref.shape[1]
    field = field_ref[...].reshape(parts * beams, Y_BLOCK, field_ref.shape[3])
    by_row = jnp.swapaxes(field, 0, 1)
    for y in range(Y_BLOCK):
        waves = dot(coef_ref[...], by_row[y]).astype(BF16)
        start = 0
        for out_ref in out_refs:
            rows = out_ref.shape[1]
            out_ref[y] = waves[start : start + rows]
            start += rows


def forward_waves(coef, smatrix, groups):
    parts, beams, strip_rows, window = smatrix.shape
    total = coef.shape[0]
    rows = total // groups
    return pl.pallas_call(
        forward_kernel,
        grid=(strip_rows // Y_BLOCK,),
        in_specs=[
            pl.BlockSpec((total, parts * beams), lambda i: (0, 0)),
            pl.BlockSpec((parts, beams, Y_BLOCK, window), lambda i: (0, 0, i, 0)),
        ],
        out_specs=[pl.BlockSpec((Y_BLOCK, rows, window), lambda i: (i, 0, 0))] * groups,
        out_shape=[jax.ShapeDtypeStruct((strip_rows, rows, window), BF16)] * groups,
        compiler_params=pltpu.CompilerParams(vmem_limit_bytes=50 << 20),
        cost_estimate=pl.CostEstimate(
            flops=2 * total * parts * beams * strip_rows * window,
            bytes_accessed=2 * (parts * beams + total) * strip_rows * window,
            transcendentals=0,
        ),
        name="forward_waves",
    )(coef, smatrix)


def backward_kernel(coef_ref, low_ref, high_ref, *refs):
    wave_refs, out_ref = refs[:-1], refs[-1]
    parts, beams = out_ref.shape[0], out_ref.shape[1]
    first = pl.program_id(0) * Y_BLOCK
    low, high = low_ref[...], high_ref[...]
    rows = []
    for y in range(Y_BLOCK):
        waves = jnp.concatenate([ref[y] for ref in wave_refs], axis=0)
        row = (first + y).astype(F32)
        keep = jnp.logical_and(low <= row, row < high)
        waves = jnp.where(keep, waves, jnp.zeros_like(waves))
        rows.append(dot(coef_ref[...], waves).astype(BF16))
    by_row = jnp.stack(rows, axis=0)
    out_ref[...] = jnp.swapaxes(by_row, 0, 1).reshape(parts, beams, Y_BLOCK, by_row.shape[2])


def backward_gradient(coef_t, low, high, pieces, parts, beams):
    strip_rows, rows, window = pieces[0].shape
    total = coef_t.shape[1]
    return pl.pallas_call(
        backward_kernel,
        grid=(strip_rows // Y_BLOCK,),
        in_specs=[
            pl.BlockSpec((parts * beams, total), lambda i: (0, 0)),
            pl.BlockSpec((total, window), lambda i: (0, 0)),
            pl.BlockSpec((total, window), lambda i: (0, 0)),
        ]
        + [pl.BlockSpec((Y_BLOCK, rows, window), lambda i: (i, 0, 0))] * len(pieces),
        out_specs=pl.BlockSpec((parts, beams, Y_BLOCK, window), lambda i: (0, 0, i, 0)),
        out_shape=jax.ShapeDtypeStruct((parts, beams, strip_rows, window), BF16),
        compiler_params=pltpu.CompilerParams(vmem_limit_bytes=50 << 20),
        cost_estimate=pl.CostEstimate(
            flops=2 * total * parts * beams * strip_rows * window,
            bytes_accessed=2 * (parts * beams + total) * strip_rows * window,
            transcendentals=0,
        ),
        name="backward_gradient",
    )(coef_t, low, high, *pieces)


def far_kernel(table_ref, amp_ref, live_ref, a0_ref, a1_ref, b0_ref, b1_ref, ga_ref, gb_ref, mid, back):
    half, both, window = a0_ref.shape
    count = both // 2
    fwd_hi, fwd_lo = table_ref[0], table_ref[1]
    inv_hi, inv_lo = table_ref[2], table_ref[3]
    for k, (x_ref, y_ref) in enumerate(((a0_ref, a1_ref), (b0_ref, b1_ref))):
        total = x_ref[...].astype(F32) + y_ref[...].astype(F32)
        pair = jnp.concatenate([total[:, :count], total[:, count:]], axis=2)
        out = right_product(pair.reshape(half * count, 2 * window), fwd_hi, fwd_lo)
        out = jnp.swapaxes(out.reshape(half, count, 2 * window), 0, 1)
        mid[:, k * half : (k + 1) * half, :] = out

    def one_pair(step, carry):
        first = step * 2
        stacked = []
        for p in range(2):
            rows = mid[first + p]
            stacked.append(jnp.concatenate([rows[:, :window], rows[:, window:]], axis=0))
        far = left_product(inv_hi, inv_lo, jnp.concatenate(stacked, axis=1))
        far_re, far_im = far[: 2 * half], far[2 * half :]
        measured = jnp.concatenate([amp_ref[first], amp_ref[first + 1]], axis=1).astype(F32)
        keep = 1.0 - measured * lax.rsqrt(far_re * far_re + far_im * far_im + ETA)
        residual = jnp.concatenate([far_re * keep, far_im * keep], axis=0)
        grad = left_product(fwd_hi, fwd_lo, residual)
        for p in range(2):
            lanes = slice(p * window, (p + 1) * window)
            pair = jnp.concatenate([grad[: 2 * half, lanes], grad[2 * half :, lanes]], axis=1)
            back[first + p] = pair
        return carry

    lax.fori_loop(0, count // 2, one_pair, 0, unroll=2)
    for k, g_ref in enumerate((ga_ref, gb_ref)):
        rows = back[:, k * half : (k + 1) * half, :]
        out = right_product(rows.reshape(count * half, 2 * window), inv_hi, inv_lo)
        out = out.reshape(count, half, 2 * window) * live_ref[...][:, :, :1]
        out = jnp.swapaxes(out, 0, 1)
        g_ref[:, :count, :] = out[:, :, :window].astype(BF16)
        g_ref[:, count:, :] = out[:, :, window:].astype(BF16)


def far_gradient(tables, amplitude, live, pieces):
    half, both, window = pieces[0].shape
    count = both // 2
    shape = jax.ShapeDtypeStruct((half, both, window), BF16)
    return pl.pallas_call(
        far_kernel,
        out_shape=[shape, shape],
        scratch_shapes=[
            pltpu.VMEM((count, 2 * half, 2 * window), F32),
            pltpu.VMEM((count, 2 * half, 2 * window), F32),
        ],
        compiler_params=pltpu.CompilerParams(vmem_limit_bytes=50 << 20),
        cost_estimate=pl.CostEstimate(
            flops=12 * 2 * count * 2 * half * 4 * window * window,
            bytes_accessed=16 * half * both * window,
            transcendentals=count * window * window,
        ),
        name="far_gradient",
    )(tables, amplitude, live, *pieces)


def body(smatrix, beam_freq, beam_amp, row_offset, col_offset, counts, amplitude):
    parts, beams, strip_rows, window = smatrix.shape
    per_tile = row_offset.shape[0]
    quarter = per_tile // 4
    scan_size = lax.axis_size("scan")
    field_rows = strip_rows * scan_size
    me = lax.axis_index("scan")
    beam_at = lax.axis_index("beam")
    hi, core = beam_at // 2, beam_at % 2
    odd = me % 2 == 1

    def send(value, target):
        return lax.ppermute(value, AXES, permutation(scan_size, target))

    def to_core(value):
        return send(value, lambda s, h, c: (s, h, 1 - c))

    def to_hi(value):
        return send(value, lambda s, h, c: (s, 1 - h, c))

    def to_near(value):
        return send(value, lambda s, h, c: (s ^ 1, h, c))

    def to_cross(value):
        return send(value, lambda s, h, c: (s ^ 1, 1 - h, c))

    def to_owner(value):
        return send(value, lambda s, h, c: (s + 2 if s % 2 else s - 2, h, c))

    def to_strip(value):
        return send(value, lambda s, h, c: (s - 2 if s % 2 else s + 2, h, c))

    packed = jnp.concatenate([row_offset, col_offset, jnp.broadcast_to(counts, (per_tile,))])
    before_1 = send(packed, lambda s, h, c: (s + 1, h, c))
    before_2 = send(packed, lambda s, h, c: (s + 2, h, c))
    first = core * (2 * quarter) + hi * quarter
    own_amp = lax.dynamic_slice_in_dim(amplitude, first, quarter, 0)
    odd_pairs = [
        pair
        for pair in permutation(scan_size, lambda s, h, c: (s + 2, h, c))
        if (pair[0] // 4) % 2
    ]
    moved_amp = lax.ppermute(own_amp.astype(BF16), AXES, odd_pairs)
    my_amp = jnp.where(odd, moved_amp.astype(F32), own_amp)

    local = jnp.where(odd, before_2, packed)
    remote = jnp.where(odd, packed, before_2)
    middle = before_1
    local_id = jnp.where(odd, me - 2, me) % scan_size
    remote_id = jnp.where(odd, me, me - 2) % scan_size
    middle_id = (me - 1) % scan_size

    def ordered(values):
        grid = values.reshape(2, 2, quarter)
        grid = jnp.where(core == 1, grid[::-1], grid)
        return jnp.where(hi == 1, grid[:, ::-1], grid)

    rows, cols, ids = [], [], []
    for tile, tile_id in ((remote, remote_id), (local, local_id), (middle, middle_id)):
        rows.append(ordered(tile[:per_tile]))
        cols.append(ordered(tile[per_tile : 2 * per_tile]))
        ids.append(jnp.full((2, 2, quarter), tile_id, jnp.int32))
    rows = jnp.stack(rows, axis=1)
    cols = jnp.stack(cols, axis=1)
    ids = jnp.stack(ids, axis=1)
    flat = 3 * per_tile
    coef_re, coef_im = coefficients(
        rows.reshape(flat), cols.reshape(flat), ids.reshape(flat),
        beam_freq, beam_amp, strip_rows, field_rows, window,
    )
    blocks = flat // quarter
    coef_re = coef_re.reshape(blocks, 1, quarter, beams)
    coef_im = coef_im.reshape(blocks, 1, quarter, beams)
    coef = jnp.concatenate(
        [
            jnp.concatenate([coef_re, -coef_im], axis=3),
            jnp.concatenate([coef_im, coef_re], axis=3),
        ],
        axis=1,
    ).reshape(2 * flat, parts * beams)

    zero = jnp.zeros_like(rows[:, 0])
    top = jnp.full_like(zero, strip_rows)
    low = jnp.stack(
        [jnp.where(odd, rows[:, 0], zero), jnp.where(odd, zero, rows[:, 1]), zero], axis=1
    )
    high = jnp.stack(
        [jnp.where(odd, top, rows[:, 0]), jnp.where(odd, rows[:, 1], top), top], axis=1
    )

    def per_row(values):
        values = jnp.broadcast_to(values[:, :, :, None, :], (2, 3, 2, 2, quarter))
        return values.reshape(2 * flat)

    low, high = per_row(low), per_row(high)

    mine_rem, mine_loc, mine_mid, other_rem, other_loc, other_mid = forward_waves(coef, smatrix, 6)
    unit = 2 * quarter

    def joined(mine, other):
        return mine.astype(F32) + to_core(other).astype(F32)

    sum_rem = joined(mine_rem, other_rem).astype(BF16)
    from_rem = to_owner(sum_rem)
    sum_mid = joined(mine_mid, other_mid).astype(BF16)
    near_mid = to_near(sum_mid[:, :unit])
    cross_mid = to_cross(sum_mid[:, unit:])
    sum_loc = joined(mine_loc, other_loc)
    y_index = jnp.arange(strip_rows, dtype=jnp.int32)[:, None]
    inside = jnp.logical_and(
        low[None, 2 * unit : 4 * unit] <= y_index, y_index < high[None, 2 * unit : 4 * unit]
    )
    window_a = jnp.where(inside[:, :, None], sum_loc, from_rem.astype(F32)).astype(BF16)
    other_a = to_hi(window_a[:, unit:])
    own_a = window_a[:, :unit]

    own_count = local[2 * per_tile]
    live = (first + jnp.arange(quarter, dtype=jnp.int32) < own_count).astype(F32)
    live = jnp.broadcast_to(live[:, None, None], (quarter, 1, window))
    tables = jnp.asarray(dft_matrices(window))
    grad_a, grad_b = far_gradient(tables, my_amp, live, (own_a, other_a, near_mid, cross_mid))

    grad_a_hi = to_hi(grad_a)
    pieces = [
        to_strip(grad_a), to_strip(grad_a_hi),
        grad_a, grad_a_hi,
        to_near(grad_b), to_cross(grad_b),
    ]
    pieces = pieces + [to_core(piece) for piece in pieces]
    low = jnp.broadcast_to(low.astype(F32)[:, None], (2 * flat, window))
    high = jnp.broadcast_to(high.astype(F32)[:, None], (2 * flat, window))
    return backward_gradient(coef.T, low, high, pieces, parts, beams)


def solution(mesh):
    return jax.shard_map(
        body,
        mesh=mesh,
        in_specs=(
            P(None, "beam", "scan", None),
            P(None, "beam"),
            P(None, "beam"),
            P("scan"),
            P("scan"),
            P("scan"),
            P("scan", None, None),
        ),
        out_specs=P(None, "beam", "scan", None),
        check_vma=False,
    )
```

time: 906 us -> 144 us (0.16)
  waiting for transfers between devices: 605 us -> 58.4 us
  matrix products: 192 us -> 0 us
  local copies, waits for them, and re-layouts: 49.8 us -> 6.62 us
  Pallas kernels: 0 us -> 30 us
  starting transfers between devices: 12.4 us -> 33.9 us
  between operations: 14.5 us -> 0.9 us
  other arithmetic: 27.6 us -> 14.1 us
    psum x1 -> x0, waiting for transfers between devices: 333 us -> none  [beam_fourier(): summed = lax.psum(windows, 'beam')]
    ppermute x8 -> x21, waiting for transfers between devices: 272 us -> 58.4 us  [the longest x20 58.4 us: send(): return lax.ppermute(value, AXES, permutation(scan_size, target))]
    dot_general x20 -> x0, matrix products: 192 us -> none  [the longest x1 36.5 us: body(): jnp.dot(own_matrix, extended, preferred_element_type=jnp.float32)]
    unnamed x7 -> x8, local copies, waits for them, and re-layouts: 44.2 us -> 0.41 us
    pallas_call x0 -> x3, Pallas kernels: none -> 30 us  [the longest x1 12.5 us: backward_gradient(): pl.pallas_call(backward_kernel, grid=(strip_rows // Y_BLOCK,), in_specs=[...]
    ppermute x8 -> x21, starting transfers between devices: 12.4 us -> 33.9 us  [the longest x20 32.4 us: send(): return lax.ppermute(value, AXES, permutation(scan_size, target))]
    concatenate x3 -> x2, other arithmetic: 21.3 us -> 0.78 us  [the longest x1 0.75 us: body(): jnp.concatenate([row_offset, col_offset, jnp.broadcast_to(counts, (per_ti...]
  transfers between devices with their start and end apart: 9 -> 21, of which waited for: 5 -> 6; matrix products, arithmetic and copies ran while one was open for 1% -> 11% of each run, Pallas kernels for 0% -> 0%
where the time goes in v1:
time: 144 us
  waiting for transfers between devices  58.4 us (41%)
  starting transfers between devices  33.9 us (24%)
  Pallas kernels  30 us (21%)
  other arithmetic  14.1 us (10%)
  local copies, waits for them, and re-layouts  6.62 us (5%)
    ppermute x20, waiting for transfers between devices, send(): return lax.ppermute(value, AXES, permutation(scan_size, target))  58.4 us
    ppermute x20, starting transfers between devices, send(): return lax.ppermute(value, AXES, permutation(scan_size, target))  32.4 us
    pallas_call x1, Pallas kernels, backward_gradient(): pl.pallas_call(backward_kernel, grid=(strip_rows // Y_BLOCK,), in_specs=[...  12.5 us
    pallas_call x1, Pallas kernels, forward_waves(): pl.pallas_call(forward_kernel, grid=(strip_rows // Y_BLOCK,), in_specs=[p...  10 us
    pallas_call x1, Pallas kernels, far_gradient(): pl.pallas_call(far_kernel, out_shape=[shape, shape], scratch_shapes=[pltp...  7.41 us
  transfers between devices with their start and end apart: 21, of which 6 were waited for; matrix products, arithmetic and copies ran while one was open for 11% of the time, Pallas kernels for 0%

profile of v1, /device:TPU:1, one launch (start us, length us, event | category | flops | bytes accessed | tf_op | source)
XLA Modules:
  0.0 143.9 jit_solution(2388043605940230032)
XLA Ops:
  0.7 0.8 pad_add_fusion.1
  1.4 2.0 %collective-permute-start.1 = (s32[192]{0:T(256)S(1)}, s32[192]{0:T(256)S(1)}, u32[]{:S(2)}, u32[]{:S(2)}) collective-permute-start(s32[192]{0:T(256)S(1)} %pad_add_fusion.1), channel_id=1, source_target_pairs={{0,4},{1,5},{2,6},{3,7},{4,8},{5,9},{6,10},{7,11},{8,12},{9,13},{1... | collective-permute-start | bytes 2312 | tf_op jit(solution)/shard_map/ppermute | solution.py:225
  3.5 1.6 %collective-permute-start = (s32[192]{0:T(256)S(1)}, s32[192]{0:T(256)S(1)}, u32[]{:S(2)}, u32[]{:S(2)}) collective-permute-start(s32[192]{0:T(256)S(1)} %pad_add_fusion.1), channel_id=1, source_target_pairs={{0,8},{1,9},{2,10},{3,11},{4,12},{5,13},{6,14},{7,15},{8,16},{9,17... | collective-permute-start | bytes 2312 | tf_op jit(solution)/shard_map/ppermute | solution.py:225
  5.1 0.8 fusion.15
  5.9 0.8 fusion.14
  6.7 3.6 %collective-permute-done.1 = s32[192]{0:T(256)S(1)} collective-permute-done((s32[192]{0:T(256)S(1)}, s32[192]{0:T(256)S(1)}, u32[]{:S(2)}, u32[]{:S(2)}) %collective-permute-start.1) | collective-permute-done | bytes 800 | tf_op jit(solution)/shard_map/ppermute | solution.py:225
  10.6 0.7 broadcast_select_fusion.3
  12.6 1.0 fusion.11
  13.6 1.0 add_convert_fusion.2
  14.7 10.0 %forward_waves.1 = (bf16[64,64,128]{2,1,0:T(8,128)(2,1)S(1)}, bf16[64,64,128]{2,1,0:T(8,128)(2,1)S(1)}, bf16[64,64,128]{2,1,0:T(8,128)(2,1)S(1)}, bf16[64,64,128...) custom-call(bf16[384,512]{1,0:T(8,128)(2,1)S(1)} %bitcast.32, ...), custom_call_target="tpu_custom_call" | custom-call | flops 3221225472 | bytes 14680064 | tf_op jit(solution)/shard_map/forward_waves/pallas_call | solution.py:93
  24.7 1.8 %collective-permute-start.4 = (bf16[64,64,128]{2,1,0:T(8,128)(2,1)}, bf16[64,64,128]{2,1,0:T(8,128)(2,1)}, u32[]{:S(2)}, u32[]{:S(2)}) collective-permute-start(bf16[64,64,128]{2,1,0:T(8,128)(2,1)} %get-tuple-element.16), channel_id=1, source_target_pairs={{0,1},{1,0},{2,3},{3,2},{4,5},{5,4},{6,7},{7,6},{8,9},{9,8},{10,11... | collective-permute-start | bytes 3145736 | tf_op jit(solution)/shard_map/ppermute | solution.py:225
  26.6 2.1 %dynamic-slice_convert_fusion = bf16[16,128,128]{2,1,0:T(8,128)(2,1)} fusion(f32[64,128,128]{2,1,0:T(8,128)} %param.14, s32[]{:T(128)S(6)} %select_n.207), kind=kLoop, calls=%fused_computation.4 | loop fusion | bytes 1048580 | tf_op jit(solution)/shard_map/convert_element_type | solution.py:255
  28.7 1.5 %collective-permute-start.2 = (bf16[16,128,128]{2,1,0:T(8,128)(2,1)}, bf16[16,128,128]{2,1,0:T(8,128)(2,1)}, u32[]{:S(2)}, u32[]{:S(2)}) collective-permute-start(bf16[16,128,128]{2,1,0:T(8,128)(2,1)} %dynamic-slice_convert_fusion), channel_id=1, source_target_pairs={{4,12},{5,13},{6,14},{7,15},{12,20},{13,21},{14,22},{15,23},{20,28... | collective-permute-start | bytes 1572872 | tf_op jit(solution)/shard_map/ppermute | solution.py:255
  30.9 2.6 %add_convert_fusion.1 = bf16[64,64,128]{2,1,0:T(8,128)(2,1)} fusion(bf16[64,64,128]{2,1,0:T(8,128)(2,1)} %collective-permute-done.4, bf16[64,64,128]{2,1,0:T(8,128)(2,1)S(1)} %get-tuple-element.15), kind=kLoop, calls=%fused_computation.2 | loop fusion | flops 2097152 | bytes 3145728 | tf_op jit(solution)/shard_map/convert_element_type | solution.py:315
  33.5 1.7 %collective-permute-start.5 = (bf16[64,64,128]{2,1,0:T(8,128)(2,1)}, bf16[64,64,128]{2,1,0:T(8,128)(2,1)}, u32[]{:S(2)}, u32[]{:S(2)}) collective-permute-start(bf16[64,64,128]{2,1,0:T(8,128)(2,1)} %add_convert_fusion.1), channel_id=1, source_target_pairs={{0,120},{1,121},{2,122},{3,123},{4,12},{5,13},{6,14},{7,15},{8,0},... | collective-permute-start | bytes 3145736 | tf_op jit(solution)/shard_map/ppermute | solution.py:225
  35.7 1.6 %add_convert_fusion = bf16[64,64,128]{2,1,0:T(8,128)(2,1)S(1)} fusion(bf16[64,64,128]{2,1,0:T(8,128)(2,1)} %collective-permute-done.7, bf16[64,64,128]{2,1,0:T(8,128)(2,1)S(1)} %get-tuple-element.17), kind=kLoop, calls=%fused_computation | loop fusion | flops 2097152 | bytes 3145728 | tf_op jit(solution)/shard_map/convert_element_type | solution.py:317
  37.4 1.6 %collective-permute-start.9 = (bf16[64,32,128]{2,1,0:T(8,128)(2,1)S(1)}, bf16[64,32,128]{2,1,0:T(8,128)(2,1)S(1)}, u32[]{:S(2)}, u32[]{:S(2)}) collective-permute-start(bf16[64,32,128]{2,1,0:T(8,128)(2,1)S(1)} %get-tuple-element.25), channel_id=1, source_target_pairs={{0,6},{1,7},{2,4},{3,5},{4,2},{5,3},{6,0},{7,1},{8,14},{9,15},{10,... | collective-permute-start | bytes 1572872 | tf_op jit(solution)/shard_map/ppermute | solution.py:225
  39.6 18.9 %collective-permute-done.5 = bf16[64,64,128]{2,1,0:T(8,128)(2,1)} collective-permute-done((bf16[64,64,128]{2,1,0:T(8,128)(2,1)}, bf16[64,64,128]{2,1,0:T(8,128)(2,1)}, u32[]{:S(2)}, u32[]{:S(2)}) %collective-permute-start.5) | collective-permute-done | bytes 1048608 | tf_op jit(solution)/shard_map/ppermute | solution.py:225
  58.5 2.8 %select_convert_fusion = bf16[64,64,128]{2,1,0:T(8,128)(2,1)S(1)} fusion(bf16[64,64,128]{2,1,0:T(8,128)(2,1)} %collective-permute-done.5, bf16[64,64,128]{2,1,0:T(8,128)(2,1)} %collective-permute-done.3, bf16[64,64,128]{2,1,0:T(8,128)(2,1)S(1)} %get-tuple-element.13, pred[64,64]{1,0:T(8,128)(4,1)S(1)} %fusion.10), kind=kLoop, calls=%fused_computation.1 | loop fusion | flops 3145728 | bytes 4198400 | tf_op jit(solution)/shard_map/convert_element_type | solution.py:325
  61.5 2.5 %collective-permute-start.6 = (bf16[64,32,128]{2,1,0:T(8,128)(2,1)S(1)}, bf16[64,32,128]{2,1,0:T(8,128)(2,1)S(1)}, u32[]{:S(2)}, u32[]{:S(2)}) collective-permute-start(bf16[64,32,128]{2,1,0:T(8,128)(2,1)S(1)} %get-tuple-element.27), channel_id=1, source_target_pairs={{0,2},{1,3},{2,0},{3,1},{4,6},{5,7},{6,4},{7,5},{8,10},{9,11},{10,... | collective-permute-start | bytes 1572872 | tf_op jit(solution)/shard_map/ppermute | solution.py:225
  65.2 2.5 %convert_select_fusion.amp_ref = f32[16,128,128]{2,1,0:T(8,128)} fusion(bf16[16,128,128]{2,1,0:T(8,128)(2,1)} %collective-permute-done.2, f32[64,128,128]{2,1,0:T(8,128)} %param.14, s32[]{:T(128)S(6)} %select_n.207, pred[]{:T(512)S(6)} %eq.14), kind=kLoop, calls=%fused_computation.3 | loop fusion | flops 524288 | bytes 2621445 | tf_op jit(solution)/shard_map/jit(_where)/select_n | solution.py:256
  67.7 8.0 %collective-permute-done.6.a1_ref = bf16[64,32,128]{2,1,0:T(8,128)(2,1)S(1)} collective-permute-done((bf16[64,32,128]{2,1,0:T(8,128)(2,1)S(1)}, bf16[64,32,128]{2,1,0:T(8,128)(2,1)S(1)}, u32[]{:S(2)}, u32[]{:S(2)}) %collective-permute-start.6) | collective-permute-done | bytes 524320 | tf_op jit(solution)/shard_map/ppermute | solution.py:225
  75.7 7.4 %far_gradient.1 = (bf16[64,32,128]{2,1,0:T(8,128)(2,1)S(1)}, bf16[64,32,128]{2,1,0:T(8,128)(2,1)S(1)}) custom-call(bf16[4,256,256]{2,1,0:T(8,128)(2,1)S(1)} %copy-done, f32[16,128,128]{2,1,0:T(8,128)} %convert_select_fusion.amp_ref, f32[16,1,128]{2,1,0:T(1,128)S(1)} %broadcast_in_dim.34.live_ref, bf16[64,32,128]{2,1,0:T(8,128)(2,1)S(1)} %get-tuple-element.28.a0_ref, ...), custom_call_target="tpu_custom_call" | custom-call | flops 3221225472 | bytes 4194304 | tf_op jit(solution)/shard_map/far_gradient/pallas_call | solution.py:196
  83.1 2.7 %collective-permute-start.11 = (bf16[64,32,128]{2,1,0:T(8,128)(2,1)S(1)}, bf16[64,32,128]{2,1,0:T(8,128)(2,1)S(1)}, u32[]{:S(2)}, u32[]{:S(2)}) collective-permute-start(bf16[64,32,128]{2,1,0:T(8,128)(2,1)S(1)} %get-tuple-element.19.refs_2_), channel_id=1, source_target_pairs={{0,2},{1,3},{2,0},{3,1},{4,6},{5,7},{6,4},{7,5},{8,10},{9,11},{10,... | collective-permute-start | bytes 1572872 | tf_op jit(solution)/shard_map/ppermute | solution.py:225
  85.9 12.1 %collective-permute-start.14 = (bf16[64,32,128]{2,1,0:T(8,128)(2,1)S(1)}, bf16[64,32,128]{2,1,0:T(8,128)(2,1)S(1)}, u32[]{:S(2)}, u32[]{:S(2)}) collective-permute-start(bf16[64,32,128]{2,1,0:T(8,128)(2,1)S(1)} %get-tuple-element.20), channel_id=1, source_target_pairs={{0,6},{1,7},{2,4},{3,5},{4,2},{5,3},{6,0},{7,1},{8,14},{9,15},{10,... | collective-permute-start | bytes 1572872 | tf_op jit(solution)/shard_map/ppermute | solution.py:225
  98.0 2.2 %collective-permute-start.17 = (bf16[64,32,128]{2,1,0:T(8,128)(2,1)S(1)}, bf16[64,32,128]{2,1,0:T(8,128)(2,1)S(1)}, u32[]{:S(2)}, u32[]{:S(2)}) collective-permute-start(bf16[64,32,128]{2,1,0:T(8,128)(2,1)S(1)} %get-tuple-element.19.refs_2_), channel_id=1, source_target_pairs={{0,1},{1,0},{2,3},{3,2},{4,5},{5,4},{6,7},{7,6},{8,9},{9,8},{10,11... | collective-permute-start | bytes 1572872 | tf_op jit(solution)/shard_map/ppermute | solution.py:225
  100.2 20.1 %collective-permute-done.14.refs_5_ = bf16[64,32,128]{2,1,0:T(8,128)(2,1)S(1)} collective-permute-done((bf16[64,32,128]{2,1,0:T(8,128)(2,1)S(1)}, bf16[64,32,128]{2,1,0:T(8,128)(2,1)S(1)}, u32[]{:S(2)}, u32[]{:S(2)}) %collective-permute-start.14) | collective-permute-done | bytes 524320 | tf_op jit(solution)/shard_map/ppermute | solution.py:225
  120.8 1.1 collective-permute-start.20
  122.4 6.1 %collective-permute-done.12.refs_1_ = bf16[64,32,128]{2,1,0:T(8,128)(2,1)} collective-permute-done((bf16[64,32,128]{2,1,0:T(8,128)(2,1)S(1)}, bf16[64,32,128]{2,1,0:T(8,128)(2,1)}, u32[]{:S(2)}, u32[]{:S(2)}) %collective-permute-start.12) | collective-permute-done | bytes 524320 | tf_op jit(solution)/shard_map/ppermute | solution.py:225
  128.5 0.8 collective-permute-start.16
  129.5 1.6 %collective-permute-done.16.refs_7_ = bf16[64,32,128]{2,1,0:T(8,128)(2,1)} collective-permute-done((bf16[64,32,128]{2,1,0:T(8,128)(2,1)}, bf16[64,32,128]{2,1,0:T(8,128)(2,1)}, u32[]{:S(2)}, u32[]{:S(2)}) %collective-permute-start.16) | collective-permute-done | bytes 524320 | tf_op jit(solution)/shard_map/ppermute | solution.py:225
  131.3 12.5 %backward_gradient.1 = bf16[2,256,64,128]{3,2,1,0:T(8,128)(2,1)} custom-call(bf16[512,384]{1,0:T(8,128)(2,1)S(1)} %bitcast.34, f32[384,128]{1,0:T(8,128)S(1)} %broadcast_in_dim.30.low_ref, f32[384,128]{1,0:T(8,128)S(1)} %broadcast_in_dim.33.high_ref, bf16[64,32,128]{2,1,0:T(8,128)(2,1)S(1)} %collective-permute-done.10.refs_0_, ...), custom_call_target="tpu_custom_call" | custom-call | flops 3221225472 | bytes 14680064 | tf_op jit(solution)/shard_map/backward_gradient/pallas_call | solution.py:131
  (90 shorter events, 6.2 us)
Async XLA Ops:
  1.4 8.9 %collective-permute-start.1 = (s32[192]{0:T(256)S(1)}, s32[192]{0:T(256)S(1)}, u32[]{:S(2)}, u32[]{:S(2)}) collective-permute-start(s32[192]{0:T(256)S(1)} %pad_add_fusion.1), channel_id=1, source_target_pairs={{0,4},{1,5},{2,6},{3,7},{4,8},{5,9},{6,10},{7,11},{8,12},{9,13},{1... | collective-permute-start | bytes 2312 | tf_op jit(solution)/shard_map/ppermute | solution.py:225
  3.5 7.2 %collective-permute-start = (s32[192]{0:T(256)S(1)}, s32[192]{0:T(256)S(1)}, u32[]{:S(2)}, u32[]{:S(2)}) collective-permute-start(s32[192]{0:T(256)S(1)} %pad_add_fusion.1), channel_id=1, source_target_pairs={{0,8},{1,9},{2,10},{3,11},{4,12},{5,13},{6,14},{7,15},{8,16},{9,17... | collective-permute-start | bytes 2312 | tf_op jit(solution)/shard_map/ppermute | solution.py:225
  11.4 0.5 copy-start.2
  24.7 6.1 %collective-permute-start.4 = (bf16[64,64,128]{2,1,0:T(8,128)(2,1)}, bf16[64,64,128]{2,1,0:T(8,128)(2,1)}, u32[]{:S(2)}, u32[]{:S(2)}) collective-permute-start(bf16[64,64,128]{2,1,0:T(8,128)(2,1)} %get-tuple-element.16), channel_id=1, source_target_pairs={{0,1},{1,0},{2,3},{3,2},{4,5},{5,4},{6,7},{7,6},{8,9},{9,8},{10,11... | collective-permute-start | bytes 3145736 | tf_op jit(solution)/shard_map/ppermute | solution.py:225
  28.7 36.5 %collective-permute-start.2 = (bf16[16,128,128]{2,1,0:T(8,128)(2,1)}, bf16[16,128,128]{2,1,0:T(8,128)(2,1)}, u32[]{:S(2)}, u32[]{:S(2)}) collective-permute-start(bf16[16,128,128]{2,1,0:T(8,128)(2,1)} %dynamic-slice_convert_fusion), channel_id=1, source_target_pairs={{4,12},{5,13},{6,14},{7,15},{12,20},{13,21},{14,22},{15,23},{20,28... | collective-permute-start | bytes 1572872 | tf_op jit(solution)/shard_map/ppermute | solution.py:255
  30.3 9.3 %collective-permute-start.3 = (bf16[64,64,128]{2,1,0:T(8,128)(2,1)}, bf16[64,64,128]{2,1,0:T(8,128)(2,1)}, u32[]{:S(2)}, u32[]{:S(2)}) collective-permute-start(bf16[64,64,128]{2,1,0:T(8,128)(2,1)} %get-tuple-element.14), channel_id=1, source_target_pairs={{0,1},{1,0},{2,3},{3,2},{4,5},{5,4},{6,7},{7,6},{8,9},{9,8},{10,11... | collective-permute-start | bytes 3145736 | tf_op jit(solution)/shard_map/ppermute | solution.py:225
  30.3 5.4 %collective-permute-start.7 = (bf16[64,64,128]{2,1,0:T(8,128)(2,1)}, bf16[64,64,128]{2,1,0:T(8,128)(2,1)}, u32[]{:S(2)}, u32[]{:S(2)}) collective-permute-start(bf16[64,64,128]{2,1,0:T(8,128)(2,1)} %get-tuple-element.18), channel_id=1, source_target_pairs={{0,1},{1,0},{2,3},{3,2},{4,5},{5,4},{6,7},{7,6},{8,9},{9,8},{10,11... | collective-permute-start | bytes 3145736 | tf_op jit(solution)/shard_map/ppermute | solution.py:225
  33.5 25.1 %collective-permute-start.5 = (bf16[64,64,128]{2,1,0:T(8,128)(2,1)}, bf16[64,64,128]{2,1,0:T(8,128)(2,1)}, u32[]{:S(2)}, u32[]{:S(2)}) collective-permute-start(bf16[64,64,128]{2,1,0:T(8,128)(2,1)} %add_convert_fusion.1), channel_id=1, source_target_pairs={{0,120},{1,121},{2,122},{3,123},{4,12},{5,13},{6,14},{7,15},{8,0},... | collective-permute-start | bytes 3145736 | tf_op jit(solution)/shard_map/ppermute | solution.py:225
  37.4 30.2 %collective-permute-start.9 = (bf16[64,32,128]{2,1,0:T(8,128)(2,1)S(1)}, bf16[64,32,128]{2,1,0:T(8,128)(2,1)S(1)}, u32[]{:S(2)}, u32[]{:S(2)}) collective-permute-start(bf16[64,32,128]{2,1,0:T(8,128)(2,1)S(1)} %get-tuple-element.25), channel_id=1, source_target_pairs={{0,6},{1,7},{2,4},{3,5},{4,2},{5,3},{6,0},{7,1},{8,14},{9,15},{10,... | collective-permute-start | bytes 1572872 | tf_op jit(solution)/shard_map/ppermute | solution.py:225
  39.1 28.6 %collective-permute-start.8 = (bf16[64,32,128]{2,1,0:T(8,128)(2,1)S(1)}, bf16[64,32,128]{2,1,0:T(8,128)(2,1)S(1)}, u32[]{:S(2)}, u32[]{:S(2)}) collective-permute-start(bf16[64,32,128]{2,1,0:T(8,128)(2,1)S(1)} %get-tuple-element.26), channel_id=1, source_target_pairs={{0,4},{1,5},{2,6},{3,7},{4,0},{5,1},{6,2},{7,3},{8,12},{9,13},{10,... | collective-permute-start | bytes 1572872 | tf_op jit(solution)/shard_map/ppermute | solution.py:225
  61.4 2.6 %copy-start.3 = (s32[192]{0:T(256)S(1)}, s32[192]{0:T(256)}, u32[]{:S(2)}) copy-start(s32[192]{0:T(256)} %copy-done.2) | copy-start | bytes 2308
  61.4 14.4 %copy-start = (bf16[4,256,256]{2,1,0:T(8,128)(2,1)S(1)}, bf16[4,256,256]{2,1,0:T(8,128)(2,1)}, u32[]{:S(2)}) copy-start(bf16[4,256,256]{2,1,0:T(8,128)(2,1)} %constant.104.clone.table_ref) | copy-start | bytes 1572868
  61.5 14.2 %collective-permute-start.6 = (bf16[64,32,128]{2,1,0:T(8,128)(2,1)S(1)}, bf16[64,32,128]{2,1,0:T(8,128)(2,1)S(1)}, u32[]{:S(2)}, u32[]{:S(2)}) collective-permute-start(bf16[64,32,128]{2,1,0:T(8,128)(2,1)S(1)} %get-tuple-element.27), channel_id=1, source_target_pairs={{0,2},{1,3},{2,0},{3,1},{4,6},{5,7},{6,4},{7,5},{8,10},{9,11},{10,... | collective-permute-start | bytes 1572872 | tf_op jit(solution)/shard_map/ppermute | solution.py:225
  83.1 17.1 %collective-permute-start.11 = (bf16[64,32,128]{2,1,0:T(8,128)(2,1)S(1)}, bf16[64,32,128]{2,1,0:T(8,128)(2,1)S(1)}, u32[]{:S(2)}, u32[]{:S(2)}) collective-permute-start(bf16[64,32,128]{2,1,0:T(8,128)(2,1)S(1)} %get-tuple-element.19.refs_2_), channel_id=1, source_target_pairs={{0,2},{1,3},{2,0},{3,1},{4,6},{5,7},{6,4},{7,5},{8,10},{9,11},{10,... | collective-permute-start | bytes 1572872 | tf_op jit(solution)/shard_map/ppermute | solution.py:225
  85.9 34.5 %collective-permute-start.14 = (bf16[64,32,128]{2,1,0:T(8,128)(2,1)S(1)}, bf16[64,32,128]{2,1,0:T(8,128)(2,1)S(1)}, u32[]{:S(2)}, u32[]{:S(2)}) collective-permute-start(bf16[64,32,128]{2,1,0:T(8,128)(2,1)S(1)} %get-tuple-element.20), channel_id=1, source_target_pairs={{0,6},{1,7},{2,4},{3,5},{4,2},{5,3},{6,0},{7,1},{8,14},{9,15},{10,... | collective-permute-start | bytes 1572872 | tf_op jit(solution)/shard_map/ppermute | solution.py:225
  98.0 22.8 %collective-permute-start.13 = (bf16[64,32,128]{2,1,0:T(8,128)(2,1)S(1)}, bf16[64,32,128]{2,1,0:T(8,128)(2,1)S(1)}, u32[]{:S(2)}, u32[]{:S(2)}) collective-permute-start(bf16[64,32,128]{2,1,0:T(8,128)(2,1)S(1)} %get-tuple-element.20), channel_id=1, source_target_pairs={{0,4},{1,5},{2,6},{3,7},{4,0},{5,1},{6,2},{7,3},{8,12},{9,13},{10,... | collective-permute-start | bytes 1572872 | tf_op jit(solution)/shard_map/ppermute | solution.py:225
  98.0 23.9 %collective-permute-start.17 = (bf16[64,32,128]{2,1,0:T(8,128)(2,1)S(1)}, bf16[64,32,128]{2,1,0:T(8,128)(2,1)S(1)}, u32[]{:S(2)}, u32[]{:S(2)}) collective-permute-start(bf16[64,32,128]{2,1,0:T(8,128)(2,1)S(1)} %get-tuple-element.19.refs_2_), channel_id=1, source_target_pairs={{0,1},{1,0},{2,3},{3,2},{4,5},{5,4},{6,7},{7,6},{8,9},{9,8},{10,11... | collective-permute-start | bytes 1572872 | tf_op jit(solution)/shard_map/ppermute | solution.py:225
  100.2 21.8 %collective-permute-start.10 = (bf16[64,32,128]{2,1,0:T(8,128)(2,1)S(1)}, bf16[64,32,128]{2,1,0:T(8,128)(2,1)S(1)}, u32[]{:S(2)}, u32[]{:S(2)}) collective-permute-start(bf16[64,32,128]{2,1,0:T(8,128)(2,1)S(1)} %get-tuple-element.19.refs_2_), channel_id=1, source_target_pairs={{0,8},{1,9},{2,10},{3,11},{4,124},{5,125},{6,126},{7,127},{8,16},{... | collective-permute-start | bytes 1572872 | tf_op jit(solution)/shard_map/ppermute | solution.py:225
  100.2 28.2 %collective-permute-start.12 = (bf16[64,32,128]{2,1,0:T(8,128)(2,1)S(1)}, bf16[64,32,128]{2,1,0:T(8,128)(2,1)}, u32[]{:S(2)}, u32[]{:S(2)}) collective-permute-start(bf16[64,32,128]{2,1,0:T(8,128)(2,1)S(1)} %collective-permute-done.11.refs_3_), channel_id=1, source_target_pairs={{0,8},{1,9},{2,10},{3,11},{4,124},{5,125},{6,126},{7,127},{8,16},{... | collective-permute-start | bytes 1572872 | tf_op jit(solution)/shard_map/ppermute | solution.py:225
  120.3 9.2 %collective-permute-start.18 = (bf16[64,32,128]{2,1,0:T(8,128)(2,1)S(1)}, bf16[64,32,128]{2,1,0:T(8,128)(2,1)}, u32[]{:S(2)}, u32[]{:S(2)}) collective-permute-start(bf16[64,32,128]{2,1,0:T(8,128)(2,1)S(1)} %collective-permute-done.11.refs_3_), channel_id=1, source_target_pairs={{0,1},{1,0},{2,3},{3,2},{4,5},{5,4},{6,7},{7,6},{8,9},{9,8},{10,11... | collective-permute-start | bytes 1572872 | tf_op jit(solution)/shard_map/ppermute | solution.py:225
  120.8 8.6 %collective-permute-start.20 = (bf16[64,32,128]{2,1,0:T(8,128)(2,1)S(1)}, bf16[64,32,128]{2,1,0:T(8,128)(2,1)}, u32[]{:S(2)}, u32[]{:S(2)}) collective-permute-start(bf16[64,32,128]{2,1,0:T(8,128)(2,1)S(1)} %collective-permute-done.14.refs_5_), channel_id=1, source_target_pairs={{0,1},{1,0},{2,3},{3,2},{4,5},{5,4},{6,7},{7,6},{8,9},{9,8},{10,11... | collective-permute-start | bytes 1572872 | tf_op jit(solution)/shard_map/ppermute | solution.py:225
  121.9 7.4 %copy-start.1 = (bf16[64,32,128]{2,1,0:T(8,128)(2,1)}, bf16[64,32,128]{2,1,0:T(8,128)(2,1)S(1)}, u32[]{:S(2)}) copy-start(bf16[64,32,128]{2,1,0:T(8,128)(2,1)S(1)} %collective-permute-done.17.refs_8_) | copy-start | bytes 1572868
  121.9 7.6 %collective-permute-start.19 = (bf16[64,32,128]{2,1,0:T(8,128)(2,1)S(1)}, bf16[64,32,128]{2,1,0:T(8,128)(2,1)}, u32[]{:S(2)}, u32[]{:S(2)}) collective-permute-start(bf16[64,32,128]{2,1,0:T(8,128)(2,1)S(1)} %collective-permute-done.13.refs_4_), channel_id=1, source_target_pairs={{0,1},{1,0},{2,3},{3,2},{4,5},{5,4},{6,7},{7,6},{8,9},{9,8},{10,11... | collective-permute-start | bytes 1572872 | tf_op jit(solution)/shard_map/ppermute | solution.py:225
  122.0 7.5 %collective-permute-start.15 = (bf16[64,32,128]{2,1,0:T(8,128)(2,1)S(1)}, bf16[64,32,128]{2,1,0:T(8,128)(2,1)}, u32[]{:S(2)}, u32[]{:S(2)}) collective-permute-start(bf16[64,32,128]{2,1,0:T(8,128)(2,1)S(1)} %collective-permute-done.10.refs_0_), channel_id=1, source_target_pairs={{0,1},{1,0},{2,3},{3,2},{4,5},{5,4},{6,7},{7,6},{8,9},{9,8},{10,11... | collective-permute-start | bytes 1572872 | tf_op jit(solution)/shard_map/ppermute | solution.py:225
  128.5 2.6 %collective-permute-start.16 = (bf16[64,32,128]{2,1,0:T(8,128)(2,1)}, bf16[64,32,128]{2,1,0:T(8,128)(2,1)}, u32[]{:S(2)}, u32[]{:S(2)}) collective-permute-start(bf16[64,32,128]{2,1,0:T(8,128)(2,1)} %collective-permute-done.12.refs_1_), channel_id=1, source_target_pairs={{0,1},{1,0},{2,3},{3,2},{4,5},{5,4},{6,7},{7,6},{8,9},{9,8},{10,11... | collective-permute-start | bytes 1572872 | tf_op jit(solution)/shard_map/ppermute | solution.py:225

commit v2 on v1

v2 whole, which is shorter than its diff:
```python
import functools
import math

import jax
import jax.numpy as jnp
import ml_dtypes
import numpy as np
from jax import lax
from jax.experimental import pallas as pl
from jax.experimental.pallas import tpu as pltpu
from jax.sharding import PartitionSpec as P

TWO_PI = 6.283185307179586
ETA = 0.1
BF16 = jnp.bfloat16
F32 = jnp.float32
AXES = ("scan", "beam")
Y_BLOCK = 16


def permutation(scan_size, target):
    pairs = []
    for s in range(scan_size):
        for hi in range(2):
            for core in range(2):
                ts, th, tc = target(s, hi, core)
                pairs.append(((s * 2 + hi) * 2 + core, ((ts % scan_size) * 2 + th) * 2 + tc))
    return pairs


def coefficient_kernel(
    where_ref, here_ref, before_1_ref, before_2_ref, freq_ref, amp_ref,
    rem_ref, rest_ref, low_ref, high_ref, live_ref,
):
    me, odd, core, hi, tiles = (where_ref[k] for k in range(5))
    per_tile = here_ref.shape[1]
    quarter = per_tile // 4
    beams = freq_ref.shape[1]
    window = low_ref.shape[1]
    strip_rows = window // 2
    field_rows = tiles * strip_rows
    is_odd = odd == 1
    here, before_1, before_2 = here_ref[...], before_1_ref[...], before_2_ref[...]
    remote = jnp.where(is_odd, here, before_2)
    local = jnp.where(is_odd, before_2, here)
    back = 2 * odd
    parts = ((remote, me - 2 + back), (local, me - back), (before_1, me - 1))
    lane = lax.broadcasted_iota(jnp.int32, (quarter, per_tile), 1)
    index = lax.broadcasted_iota(jnp.int32, (quarter, per_tile), 0)
    step = 2 * quarter
    for part, (tile, tile_id) in enumerate(parts):
        for block in range(4):
            first = jnp.bitwise_xor(core, block // 2) * step + jnp.bitwise_xor(hi, block % 2) * quarter
            chosen = lane == first + index
            row = jnp.sum(jnp.where(chosen, tile[0:1], 0), axis=1, keepdims=True)
            col = jnp.sum(jnp.where(chosen, tile[1:2], 0), axis=1, keepdims=True)
            global_row = tile_id * strip_rows + row
            along_rows = jnp.bitwise_and(freq_ref[0:1] * global_row, field_rows - 1)
            along_cols = jnp.bitwise_and(freq_ref[1:2] * col, window - 1)
            turns = along_rows.astype(F32) / field_rows.astype(F32) + along_cols.astype(F32) / window
            angle = -TWO_PI * turns
            cos_part, sin_part = jnp.cos(angle), jnp.sin(angle)
            re = amp_ref[0:1] * cos_part - amp_ref[1:2] * sin_part
            im = amp_ref[0:1] * sin_part + amp_ref[1:2] * cos_part
            re, im = re.astype(BF16), im.astype(BF16)
            out_ref = rest_ref if part else rem_ref
            start = ((part - 1) * 4 if part else 0) * step + block * step
            out_ref[start : start + quarter, :beams] = re
            out_ref[start : start + quarter, beams:] = -im
            out_ref[start + quarter : start + step, :beams] = im
            out_ref[start + quarter : start + step, beams:] = re
            row = jnp.broadcast_to(row.astype(F32), (quarter, window))
            none, full = jnp.zeros_like(row), jnp.full_like(row, strip_rows)
            from_row = is_odd if part == 0 else jnp.logical_not(is_odd)
            if part == 2:
                low, high = none, full
            else:
                low, high = jnp.where(from_row, row, none), jnp.where(from_row, full, row)
            start = (part * 4 + block) * step
            for copy in range(2):
                at = start + copy * quarter
                low_ref[at : at + quarter] = low
                high_ref[at : at + quarter] = high
    first = core * step + hi * quarter
    position = lax.broadcasted_iota(jnp.int32, (quarter, window), 0) + first
    live_ref[...] = (position < local[2:3, :1]).astype(F32)


def coefficients(where, here, before_1, before_2, beam_freq, beam_amp, parts, window):
    beams = beam_freq.shape[1]
    per_tile = here.shape[1]
    shapes = [
        jax.ShapeDtypeStruct((2 * per_tile, parts * beams), BF16),
        jax.ShapeDtypeStruct((4 * per_tile, parts * beams), BF16),
        jax.ShapeDtypeStruct((6 * per_tile, window), F32),
        jax.ShapeDtypeStruct((6 * per_tile, window), F32),
        jax.ShapeDtypeStruct((per_tile // 4, window), F32),
    ]
    return pl.pallas_call(
        coefficient_kernel,
        in_specs=[pl.BlockSpec(memory_space=pltpu.SMEM)]
        + [pl.BlockSpec(memory_space=pltpu.VMEM)] * 5,
        out_specs=[pl.BlockSpec(memory_space=pltpu.VMEM)] * 5,
        out_shape=shapes,
        compiler_params=pltpu.CompilerParams(vmem_limit_bytes=16 << 20),
        name="coefficients",
    )(where, here, before_1, before_2, beam_freq, beam_amp)


def dft_matrices(window):
    counter = np.arange(window)
    angle = (counter[:, None] * counter[None, :] % window) * (2.0 * math.pi / window)
    re = np.cos(angle) / math.sqrt(window)
    im = -np.sin(angle) / math.sqrt(window)
    full = np.block([[re, im], [-im, re]])
    high = full.astype(ml_dtypes.bfloat16)
    low = (full - high.astype(np.float64)).astype(ml_dtypes.bfloat16)
    return np.stack([high, low, high.T, low.T])


def split(value):
    high = value.astype(BF16)
    return high, (value - high.astype(F32)).astype(BF16)


def dot(left, right):
    return jnp.dot(left, right, preferred_element_type=F32)


def right_product(value, high, low):
    value_hi, value_lo = split(value)
    return dot(value_hi, high) + (dot(value_lo, high) + dot(value_hi, low))


def left_product(high, low, value):
    value_hi, value_lo = split(value)
    return dot(high, value_hi) + (dot(high, value_lo) + dot(low, value_hi))


def transpose_kernel(at_ref, field_ref, amp_ref, out_ref, own_ref, sent_ref):
    parts, beams, rows, window = field_ref.shape
    out_ref[...] = jnp.swapaxes(field_ref[...].reshape(parts * beams, rows, window), 0, 1)
    own_ref[...] = amp_ref[...]
    sent_ref[...] = amp_ref[...].astype(BF16)


def rows_first(at, smatrix, amplitude):
    parts, beams, strip_rows, window = smatrix.shape
    blocks = strip_rows // Y_BLOCK
    quarter = amplitude.shape[0] // 4
    each = quarter // (blocks * parts)
    amp_block = (each, *amplitude.shape[1:])
    amp_out = pl.BlockSpec(amp_block, lambda i, p, at: (i * parts + p, 0, 0))
    return pl.pallas_call(
        transpose_kernel,
        grid_spec=pltpu.PrefetchScalarGridSpec(
            num_scalar_prefetch=1,
            grid=(blocks, parts),
            in_specs=[
                pl.BlockSpec((1, beams, Y_BLOCK, window), lambda i, p, at: (p, 0, i, 0)),
                pl.BlockSpec(
                    amp_block, lambda i, p, at: (at[0] * (blocks * parts) + i * parts + p, 0, 0)
                ),
            ],
            out_specs=[
                pl.BlockSpec((Y_BLOCK, beams, window), lambda i, p, at: (i, p, 0)),
                amp_out,
                amp_out,
            ],
        ),
        out_shape=[
            jax.ShapeDtypeStruct((strip_rows, parts * beams, window), BF16),
            jax.ShapeDtypeStruct((quarter, *amplitude.shape[1:]), F32),
            jax.ShapeDtypeStruct((quarter, *amplitude.shape[1:]), BF16),
        ],
        compiler_params=pltpu.CompilerParams(vmem_limit_bytes=24 << 20),
        cost_estimate=pl.CostEstimate(
            flops=0, bytes_accessed=4 * parts * beams * strip_rows * window, transcendentals=0
        ),
        name="rows_first",
    )(at, smatrix, amplitude)


def forward_kernel(rem_ref, rest_ref, field_ref, *out_refs):
    coef = jnp.concatenate([rem_ref[...], rest_ref[...]], axis=0)
    for y in range(field_ref.shape[0]):
        waves = dot(coef, field_ref[y]).astype(BF16)
        start = 0
        for out_ref in out_refs:
            rows = out_ref.shape[1]
            out_ref[y] = waves[start : start + rows]
            start += rows


def forward_waves(coefs, field):
    strip_rows, depth, window = field.shape
    total = sum(coef.shape[0] for coef in coefs)
    rows = total // 6
    block = Y_BLOCK // 2
    return pl.pallas_call(
        forward_kernel,
        grid=(strip_rows // block,),
        in_specs=[pl.BlockSpec(coef.shape, lambda i: (0, 0)) for coef in coefs]
        + [pl.BlockSpec((block, depth, window), lambda i: (i, 0, 0))],
        out_specs=[pl.BlockSpec((block, rows, window), lambda i: (i, 0, 0))] * 6,
        out_shape=[jax.ShapeDtypeStruct((strip_rows, rows, window), BF16)] * 6,
        compiler_params=pltpu.CompilerParams(vmem_limit_bytes=16 << 20),
        cost_estimate=pl.CostEstimate(
            flops=2 * total * depth * strip_rows * window,
            bytes_accessed=2 * (depth + total) * strip_rows * window,
            transcendentals=0,
        ),
        name="forward_waves",
    )(*coefs, field)


def backward_kernel(first_row, has_before, rem_ref, rest_ref, low_ref, high_ref, *refs):
    refs = refs[2:] if has_before else refs
    wave_refs, out_ref, done_ref, turned = refs[:-3], refs[-3], refs[-2], refs[-1]
    done_ref[...] = jnp.zeros_like(done_ref)
    parts, beams = out_ref.shape[0], out_ref.shape[1]
    split_at = rem_ref.shape[0]

    @pl.when(pl.program_id(0) == 0)
    def turn():
        turned[:, :split_at] = rem_ref[...].T
        turned[:, split_at:] = rest_ref[...].T

    first = pl.program_id(0) * Y_BLOCK + first_row
    low, high = low_ref[...], high_ref[...]
    rows = []
    for y in range(Y_BLOCK):
        waves = jnp.concatenate([ref[y] for ref in wave_refs], axis=0)
        row = (first + y).astype(F32)
        keep = jnp.logical_and(low <= row, row < high)
        waves = jnp.where(keep, waves, jnp.zeros_like(waves))
        rows.append(dot(turned[...], waves).astype(BF16))
    by_row = jnp.stack(rows, axis=0)
    out_ref[...] = jnp.swapaxes(by_row, 0, 1).reshape(parts, beams, Y_BLOCK, by_row.shape[2])


def backward_gradient(coefs, low, high, pieces, parts, beams, first_row, strip_rows, before):
    rows, window = pieces[0].shape[1:]
    part_rows = strip_rows // 2
    total = low.shape[0]
    offset = first_row // Y_BLOCK
    kept = [] if before is None else [*before]

    def piece_spec(piece):
        skip = offset if piece.shape[0] == strip_rows else 0
        return pl.BlockSpec((Y_BLOCK, rows, window), lambda i: (i + skip, 0, 0))

    def whole(value):
        return pl.BlockSpec(value.shape, lambda i: (0, 0))

    return pl.pallas_call(
        functools.partial(backward_kernel, first_row, before is not None),
        grid=(part_rows // Y_BLOCK,),
        in_specs=[whole(value) for value in (*coefs, low, high)]
        + [pl.BlockSpec(memory_space=pl.ANY)] * len(kept)
        + [piece_spec(piece) for piece in pieces],
        out_specs=[
            pl.BlockSpec((parts, beams, Y_BLOCK, window), lambda i: (0, 0, i + offset, 0)),
            pl.BlockSpec((8, window), lambda i: (0, 0)),
        ],
        out_shape=[
            jax.ShapeDtypeStruct((parts, beams, strip_rows, window), BF16),
            jax.ShapeDtypeStruct((8, window), F32),
        ],
        scratch_shapes=[pltpu.VMEM((parts * beams, total), BF16)],
        input_output_aliases={4: 0} if kept else {},
        compiler_params=pltpu.CompilerParams(vmem_limit_bytes=32 << 20),
        cost_estimate=pl.CostEstimate(
            flops=2 * total * parts * beams * part_rows * window,
            bytes_accessed=2 * (parts * beams + total) * part_rows * window,
            transcendentals=0,
        ),
        name=f"backward_gradient_{first_row}",
    )(*coefs, low, high, *kept, *pieces)


def far_kernel(
    table_ref, amp_ref, moved_ref, odd_ref, live_ref, low_ref, high_ref, mine_ref, got_ref,
    top_rem_ref, top_got_ref, end_got_ref, end_rem_ref, near_ref, cross_ref,
    ga_top_ref, ga_end_ref, ga_ref, gb_ref, mid, back,
):
    half, both, window = near_ref.shape
    part = half // 2
    count = both // 2
    fwd_hi, fwd_lo = table_ref[0], table_ref[1]
    inv_hi, inv_lo = table_ref[2], table_ref[3]
    own = mine_ref[...].astype(F32) + got_ref[...].astype(F32)
    row = lax.broadcasted_iota(jnp.int32, own.shape, 0).astype(F32)
    inside = jnp.logical_and(low_ref[...][None] <= row, row < high_ref[...][None])
    top = jnp.where(inside[:part], own[:part], top_rem_ref[...].astype(F32))
    top = top + top_got_ref[...].astype(F32)
    end = own[part:] + end_got_ref[...].astype(F32)
    end = jnp.where(inside[part:], end, end_rem_ref[...].astype(F32))
    middle = near_ref[...].astype(F32) + cross_ref[...].astype(F32)
    for first, total in ((0, top), (part, end), (half, middle)):
        rows = total.shape[0]
        pair = jnp.concatenate([total[:, :count], total[:, count:]], axis=2)
        out = right_product(pair.reshape(rows * count, 2 * window), fwd_hi, fwd_lo)
        out = jnp.swapaxes(out.reshape(rows, count, 2 * window), 0, 1)
        mid[:, first : first + rows, :] = out
    odd = jnp.broadcast_to(odd_ref[...], (2 * half, window)) > 0.0

    def amplitude(p):
        return jnp.where(odd, moved_ref[p].astype(F32), amp_ref[p])

    def one_pair(step, carry):
        first = step * 2
        stacked = []
        for p in range(2):
            rows = mid[first + p]
            stacked.append(jnp.concatenate([rows[:, :window], rows[:, window:]], axis=0))
        far = left_product(inv_hi, inv_lo, jnp.concatenate(stacked, axis=1))
        far_re, far_im = far[: 2 * half], far[2 * half :]
        measured = jnp.concatenate([amplitude(first), amplitude(first + 1)], axis=1)
        keep = 1.0 - measured * lax.rsqrt(far_re * far_re + far_im * far_im + ETA)
        residual = jnp.concatenate([far_re * keep, far_im * keep], axis=0)
        grad = left_product(fwd_hi, fwd_lo, residual)
        for p in range(2):
            lanes = slice(p * window, (p + 1) * window)
            pair = jnp.concatenate([grad[: 2 * half, lanes], grad[2 * half :, lanes]], axis=1)
            back[first + p] = pair
        return carry

    lax.fori_loop(0, count // 2, one_pair, 0, unroll=2)
    live = live_ref[...][:, None, :1]
    for first in range(0, 2 * half, part):
        rows = back[:, first : first + part, :]
        out = right_product(rows.reshape(count * part, 2 * window), inv_hi, inv_lo)
        out = jnp.swapaxes(out.reshape(count, part, 2 * window) * live, 0, 1)
        out_re, out_im = out[:, :, :window].astype(BF16), out[:, :, window:].astype(BF16)
        g_ref = ga_ref if first < half else gb_ref
        targets = [g_ref.at[first % half : first % half + part]]
        if first < half:
            targets.append(ga_end_ref if first else ga_top_ref)
        for target in targets:
            target[:, :count, :] = out_re
            target[:, count:, :] = out_im


def far_gradient(tables, amplitude, moved, odd, live, low, high, pieces):
    half, both, window = pieces[-1].shape
    count = both // 2
    shape = jax.ShapeDtypeStruct((half // 2, both, window), BF16)
    whole_shape = jax.ShapeDtypeStruct((half, both, window), BF16)

    def whole(value):
        return pl.BlockSpec(value.shape, lambda i: (0,) * value.ndim)

    def rows_of(value, index):
        return pl.BlockSpec((*value.shape[:-2], both, window), lambda i: index)

    mine, got, top_rem, *rest = pieces
    own_block = 4
    return pl.pallas_call(
        far_kernel,
        grid=(1,),
        in_specs=[whole(value) for value in (tables, amplitude, moved, odd, live)]
        + [rows_of(low, (own_block, 0)), rows_of(high, (own_block, 0))]
        + [rows_of(value, (0, 0, 0)) for value in (mine, got, top_rem)]
        + [whole(value) for value in rest],
        out_specs=[whole(shape), whole(shape), whole(whole_shape), whole(whole_shape)],
        out_shape=[shape, shape, whole_shape, whole_shape],
        scratch_shapes=[
            pltpu.VMEM((count, 2 * half, 2 * window), F32),
            pltpu.VMEM((count, 2 * half, 2 * window), F32),
        ],
        compiler_params=pltpu.CompilerParams(vmem_limit_bytes=36 << 20),
        cost_estimate=pl.CostEstimate(
            flops=12 * 2 * count * 2 * half * 4 * window * window,
            bytes_accessed=16 * half * both * window,
            transcendentals=count * window * window,
        ),
        name="far_gradient",
    )(tables, amplitude, moved, odd, live, low, high, *pieces)


def body(smatrix, beam_freq, beam_amp, row_offset, col_offset, counts, amplitude):
    parts, beams, strip_rows, window = smatrix.shape
    per_tile = row_offset.shape[0]
    quarter = per_tile // 4
    scan_size = lax.axis_size("scan")
    me = lax.axis_index("scan")
    beam_at = lax.axis_index("beam")
    hi, core = beam_at // 2, beam_at % 2
    at = core * 2 + hi
    odd = me % 2
    where = jnp.stack([me, odd, core, hi, jnp.int32(scan_size), at]).astype(jnp.int32)
    odd_row = jnp.broadcast_to(odd.astype(F32), (1, window))

    def send(value, target):
        return lax.ppermute(value, AXES, permutation(scan_size, target))

    def to_core(value):
        return send(value, lambda s, h, c: (s, h, 1 - c))

    def to_hi(value):
        return send(value, lambda s, h, c: (s, 1 - h, c))

    def to_near(value):
        return send(value, lambda s, h, c: (s ^ 1, h, c))

    def to_cross(value):
        return send(value, lambda s, h, c: (s ^ 1, 1 - h, c))

    def to_owner(value):
        return send(value, lambda s, h, c: (s + 2 if s % 2 else s - 2, h, c))

    def to_strip(value):
        return send(value, lambda s, h, c: (s - 2 if s % 2 else s + 2, h, c))

    packed = jnp.stack([row_offset, col_offset, jnp.broadcast_to(counts, (per_tile,))])
    before_1 = send(packed, lambda s, h, c: (s + 1, h, c))
    before_2 = send(packed, lambda s, h, c: (s + 2, h, c))
    odd_pairs = [
        pair
        for pair in permutation(scan_size, lambda s, h, c: (s + 2, h, c))
        if (pair[0] // 4) % 2
    ]
    smatrix, where, odd_row = lax.optimization_barrier((smatrix, where, odd_row))
    field, own_amp, sent_amp = rows_first(where[5:], smatrix, amplitude)
    moved_amp = lax.ppermute(sent_amp, AXES, odd_pairs)

    coef_rem, coef_rest, low, high, live = coefficients(
        where, packed, before_1, before_2, beam_freq, beam_amp, parts, window
    )
    unit = 2 * quarter
    part = strip_rows // 2
    tile_rows = 4 * unit
    coefs = (coef_rem, coef_rest)

    def joined(mine, got):
        return mine.astype(F32) + got.astype(F32)

    mine_rem, other_rem, mine_loc, other_loc, mine_mid, other_mid = forward_waves(
        coefs, field
    )
    got_rem = to_core(other_rem)
    rem_top = to_owner(joined(mine_rem[:part], got_rem[:part]).astype(BF16))
    end_got = to_hi(joined(mine_rem[part:, unit:], got_rem[part:, unit:]).astype(BF16))
    rem_end = joined(mine_rem[part:, :unit], got_rem[part:, :unit]) + end_got.astype(F32)
    rem_end = to_owner(rem_end.astype(BF16))
    got_mid = to_core(other_mid)
    near_mid = to_near(joined(mine_mid[:, :unit], got_mid[:, :unit]).astype(BF16))
    cross_mid = to_cross(joined(mine_mid[:, unit:], got_mid[:, unit:]).astype(BF16))
    got_loc = to_core(other_loc)
    loc_end_got = to_hi(joined(mine_loc[part:, unit:], got_loc[part:, unit:]).astype(BF16))

    far_rows = slice(tile_rows + unit, tile_rows + 2 * unit)
    y_index = jnp.arange(part, dtype=F32)[:, None, None]
    inside = jnp.logical_and(low[None, far_rows] <= y_index, y_index < high[None, far_rows])
    top_sent = jnp.where(
        inside,
        joined(mine_loc[:part, unit:], got_loc[:part, unit:]),
        rem_top[:, unit:].astype(F32),
    )
    top_got = to_hi(top_sent.astype(BF16))

    tables = jnp.asarray(dft_matrices(window))
    ga_top, ga_end, grad_a, grad_b = far_gradient(
        tables, own_amp, moved_amp, odd_row, live,
        low, high, (mine_loc, got_loc, rem_top, top_got, loc_end_got, rem_end, near_mid, cross_mid),
    )

    ga_top_hi = to_hi(ga_top)
    rem_top = to_strip(ga_top)
    rem_end = to_strip(ga_end)
    other_a = to_core(grad_a)
    near, cross = to_near(grad_b), to_cross(grad_b)
    ga_end, ga_top_hi = lax.optimization_barrier((ga_end, ga_top_hi))
    rem_top_hi = to_strip(ga_top_hi)
    ga_end_hi = to_hi(ga_end)
    rem_end_hi = to_strip(ga_end_hi)
    middle = [near, cross, to_core(near), to_core(cross)]

    def ordered_pieces(rem, rem_hi, loc_hi):
        remote = [rem, rem_hi, to_core(rem), to_core(rem_hi)]
        return remote + [grad_a, loc_hi, other_a, to_core(loc_hi)] + middle

    out, done = backward_gradient(
        coefs, low, high, ordered_pieces(rem_top, rem_top_hi, ga_top_hi),
        parts, beams, 0, strip_rows, None,
    )
    rem_end_hi, done = lax.optimization_barrier((rem_end_hi, done))
    out, _ = backward_gradient(
        coefs, low, high, ordered_pieces(rem_end, rem_end_hi, ga_end_hi),
        parts, beams, part, strip_rows, (out, done),
    )
    return out


def solution(mesh):
    return jax.shard_map(
        body,
        mesh=mesh,
        in_specs=(
            P(None, "beam", "scan", None),
            P(None, "beam"),
            P(None, "beam"),
            P("scan"),
            P("scan"),
            P("scan"),
            P("scan", None, None),
        ),
        out_specs=P(None, "beam", "scan", None),
        check_vma=False,
    )
```

time: 144 us -> 132 us (0.917)
  waiting for transfers between devices: 58.4 us -> 38.5 us
  starting transfers between devices: 33.9 us -> 50.4 us
  other arithmetic: 14.1 us -> 1.68 us
  Pallas kernels: 30 us -> 34 us
    ppermute x20 -> x29, waiting for transfers between devices: 58.4 us -> 38.5 us  [send(): return lax.ppermute(value, AXES, permutation(scan_size, target))]
    ppermute x20 -> x29, starting transfers between devices: 32.4 us -> 49.8 us  [send(): return lax.ppermute(value, AXES, permutation(scan_size, target))]
    convert_element_type x7 -> x5, other arithmetic: 8.72 us -> 0.94 us  [the longest x1 0.28 us: body(): joined(mine_loc[part:, unit:], got_loc[part:, unit:]).astype(BF16)]
    unnamed x8 -> x10, local copies, waits for them, and re-layouts: 0.41 us -> 5.58 us
    pallas_call x3 -> x6, Pallas kernels: 30 us -> 34 us  [the longest x2 12.8 us: backward_gradient(): pl.pallas_call(functools.partial(backward_kernel, first_row, before is no...]
    select_n x6 -> x0, other arithmetic: 3.26 us -> none  [the longest x1 2.48 us: body(): my_amp = jnp.where(odd, moved_amp.astype(F32), own_amp)]
    slice x14 -> x3, local copies, waits for them, and re-layouts: 2.88 us -> 0.59 us  [the longest x1 0.58 us: body(): field, own_amp, sent_amp = rows_first(where[5:], smatrix, amplitude)]
    convert_element_type x1 -> x0, local copies, waits for them, and re-layouts: 2.11 us -> none  [body(): moved_amp = lax.ppermute(own_amp.astype(BF16), AXES, odd_pairs)]
  transfers between devices with their start and end apart: 21 -> 30, of which waited for: 6 -> 12; matrix products, arithmetic and copies ran while one was open for 11% -> 1% of each run, Pallas kernels for 0% -> 9%
where the time goes in v2:
time: 132 us
  starting transfers between devices  50.4 us (38%)
  waiting for transfers between devices  38.5 us (29%)
  Pallas kernels  34 us (26%)
  local copies, waits for them, and re-layouts  6.33 us (5%)
  other arithmetic  1.68 us (1%)
    ppermute x29, starting transfers between devices, send(): return lax.ppermute(value, AXES, permutation(scan_size, target))  49.8 us
    ppermute x29, waiting for transfers between devices, send(): return lax.ppermute(value, AXES, permutation(scan_size, target))  38.5 us
    pallas_call x2, Pallas kernels, backward_gradient(): pl.pallas_call(functools.partial(backward_kernel, first_row, before is no...  12.8 us
    pallas_call x1, Pallas kernels, forward_waves(): pl.pallas_call(forward_kernel, grid=(strip_rows // block,), in_specs=[pl....  7.93 us
    pallas_call x1, Pallas kernels, far_gradient(): pl.pallas_call(far_kernel, grid=(1,), in_specs=[whole(value) for value in...  6.38 us
    unnamed x10, local copies, waits for them, and re-layouts  5.58 us
    pallas_call x1, Pallas kernels, rows_first(): pl.pallas_call(transpose_kernel, grid_spec=pltpu.PrefetchScalarGridSpec(n...  5.44 us
  transfers between devices with their start and end apart: 30, of which 12 were waited for; matrix products, arithmetic and copies ran while one was open for 1% of the time, Pallas kernels for 9%

profile of v2, /device:TPU:1, one launch (start us, length us, event | category | flops | bytes accessed | tf_op | source)
XLA Modules:
  0.0 131.8 jit_solution(10766609805307138753)
XLA Ops:
  1.5 2.5 %collective-permute-start.1 = (s32[3,64]{1,0:T(4,128)S(1)}, s32[3,64]{1,0:T(4,128)S(1)}, u32[]{:S(2)}, u32[]{:S(2)}) collective-permute-start(s32[3,64]{1,0:T(4,128)S(1)} %add_add_fusion.here_ref), channel_id=1, source_target_pairs={{0,8},{1,9},{2,10},{3,11},{4,12},{5,13},{6,14},{7,15},{8,16},{9,17... | collective-permute-start | bytes 2312 | tf_op jit(solution)/shard_map/ppermute | solution.py:396
  4.0 1.2 collective-permute-start
  5.9 3.4 %copy-done = bf16[2,256,64,128]{3,2,1,0:T(8,128)(2,1)S(1)} copy-done((bf16[2,256,64,128]{3,2,1,0:T(8,128)(2,1)S(1)}, bf16[2,256,64,128]{3,2,1,0:T(8,128)(2,1)}, u32[]{:S(2)}) %copy-start) | copy-done | bytes 8388632
  9.2 2.2 %copy-done.1 = f32[64,128,128]{2,1,0:T(8,128)S(1)} copy-done((f32[64,128,128]{2,1,0:T(8,128)S(1)}, f32[64,128,128]{2,1,0:T(8,128)}, u32[]{:S(2)}) %copy-start.1) | copy-done | bytes 4194328
  11.4 5.4 %rows_first.1 = (bf16[64,512,128]{2,1,0:T(8,128)(2,1)S(1)}, f32[16,128,128]{2,1,0:T(8,128)S(1)}, bf16[16,128,128]{2,1,0:T(8,128)(2,1)S(1)}) custom-call(s32[1]{0:T(128)} %slice.54.at_ref, bf16[2,256,64,128]{3,2,1,0:T(8,128)(2,1)S(1)} %copy-done, f32[64,128,128]{2,1,0:T(8,128)S(1)} %copy-done.1), custom_call_target="tpu_custom_call" | custom-call | bytes 16777216 | tf_op jit(solution)/shard_map/rows_first/pallas_call | solution.py:154
  16.9 1.5 %coefficients.1 = (bf16[128,512]{1,0:T(8,128)(2,1)S(1)}, bf16[256,512]{1,0:T(8,128)(2,1)S(1)}, f32[384,128]{1,0:T(8,128)S(1)}, f32[384,128]{1,0:T(8,128)S(1)}, f32[16,128]{1,0:T(8,128)S(1)}) custom-call(s32[6]{0:T(128)S(1)} %stack.32.where_ref, s32[3,64]{1,0:T(4,128)S(1)} %add_add_fusion.here_ref, s32[3,64]{1,0:T(4,128)S(1)} %collective-permute-done.before_1_ref, ...), custom_call_target="tpu_custom_call" | custom-call | tf_op jit(solution)/shard_map/coefficients/pallas_call | solution.py:99
  18.4 7.9 %forward_waves.1 = (bf16[64,64,128]{2,1,0:T(8,128)(2,1)S(1)}, bf16[64,64,128]{2,1,0:T(8,128)(2,1)S(1)}, bf16[64,64,128]{2,1,0:T(8,128)(2,1)S(1)}, bf16[64,64,128...) custom-call(bf16[128,512]{1,0:T(8,128)(2,1)S(1)} %get-tuple-element.34.rem_ref, ...), custom_call_target="tpu_custom_call" | custom-call | flops 3221225472 | bytes 14680064 | tf_op jit(solution)/shard_map/forward_waves/pallas_call | solution.py:200
  26.4 1.3 collective-permute-start.4
  28.9 1.1 collective-permute-done.4
  30.1 2.5 %collective-permute-start.8 = (bf16[32,32,128]{2,1,0:T(8,128)(2,1)S(1)}, bf16[32,32,128]{2,1,0:T(8,128)(2,1)S(1)}, u32[]{:S(2)}, u32[]{:S(2)}) collective-permute-start(bf16[32,32,128]{2,1,0:T(8,128)(2,1)S(1)} %add_convert_fusion.4), channel_id=1, source_target_pairs={{0,2},{1,3},{2,0},{3,1},{4,6},{5,7},{6,4},{7,5},{8,10},{9,11},{10,... | collective-permute-start | bytes 786440 | tf_op jit(solution)/shard_map/ppermute | solution.py:396
  32.8 4.4 %collective-permute-start.5 = (bf16[32,64,128]{2,1,0:T(8,128)(2,1)S(1)}, bf16[32,64,128]{2,1,0:T(8,128)(2,1)S(1)}, u32[]{:S(2)}, u32[]{:S(2)}) collective-permute-start(bf16[32,64,128]{2,1,0:T(8,128)(2,1)S(1)} %add_convert_fusion.2), channel_id=1, source_target_pairs={{0,120},{1,121},{2,122},{3,123},{4,12},{5,13},{6,14},{7,15},{8,0},... | collective-permute-start | bytes 1572872 | tf_op jit(solution)/shard_map/ppermute | solution.py:396
  37.6 1.6 %collective-permute-done.8 = bf16[32,32,128]{2,1,0:T(8,128)(2,1)S(1)} collective-permute-done((bf16[32,32,128]{2,1,0:T(8,128)(2,1)S(1)}, bf16[32,32,128]{2,1,0:T(8,128)(2,1)S(1)}, u32[]{:S(2)}, u32[]{:S(2)}) %collective-permute-start.8) | collective-permute-done | bytes 262176 | tf_op jit(solution)/shard_map/ppermute | solution.py:396
  39.2 3.2 %collective-permute-start.11 = (bf16[64,32,128]{2,1,0:T(8,128)(2,1)S(1)}, bf16[64,32,128]{2,1,0:T(8,128)(2,1)S(1)}, u32[]{:S(2)}, u32[]{:S(2)}) collective-permute-start(bf16[64,32,128]{2,1,0:T(8,128)(2,1)S(1)} %get-tuple-element.62), channel_id=1, source_target_pairs={{0,4},{1,5},{2,6},{3,7},{4,0},{5,1},{6,2},{7,3},{8,12},{9,13},{10,... | collective-permute-start | bytes 1572872 | tf_op jit(solution)/shard_map/ppermute | solution.py:396
  42.5 3.5 %collective-permute-start.9 = (bf16[32,32,128]{2,1,0:T(8,128)(2,1)S(1)}, bf16[32,32,128]{2,1,0:T(8,128)(2,1)S(1)}, u32[]{:S(2)}, u32[]{:S(2)}) collective-permute-start(bf16[32,32,128]{2,1,0:T(8,128)(2,1)S(1)} %add_convert_fusion.3), channel_id=1, source_target_pairs={{0,120},{1,121},{2,122},{3,123},{4,12},{5,13},{6,14},{7,15},{8,0},... | collective-permute-start | bytes 786440 | tf_op jit(solution)/shard_map/ppermute | solution.py:396
  46.0 1.8 %collective-permute-done.5.top_rem_ref = bf16[32,64,128]{2,1,0:T(8,128)(2,1)S(1)} collective-permute-done((bf16[32,64,128]{2,1,0:T(8,128)(2,1)S(1)}, bf16[32,64,128]{2,1,0:T(8,128)(2,1)S(1)}, u32[]{:S(2)}, u32[]{:S(2)}) %collective-permute-start.5) | collective-permute-done | bytes 524320 | tf_op jit(solution)/shard_map/ppermute | solution.py:396
  49.1 2.1 %collective-permute-start.6 = (bf16[32,32,128]{2,1,0:T(8,128)(2,1)S(1)}, bf16[32,32,128]{2,1,0:T(8,128)(2,1)S(1)}, u32[]{:S(2)}, u32[]{:S(2)}) collective-permute-start(bf16[32,32,128]{2,1,0:T(8,128)(2,1)S(1)} %get-tuple-element.64), channel_id=1, source_target_pairs={{0,2},{1,3},{2,0},{3,1},{4,6},{5,7},{6,4},{7,5},{8,10},{9,11},{10,... | collective-permute-start | bytes 786440 | tf_op jit(solution)/shard_map/ppermute | solution.py:396
  51.2 2.3 %collective-permute-done.9.end_rem_ref = bf16[32,32,128]{2,1,0:T(8,128)(2,1)S(1)} collective-permute-done((bf16[32,32,128]{2,1,0:T(8,128)(2,1)S(1)}, bf16[32,32,128]{2,1,0:T(8,128)(2,1)S(1)}, u32[]{:S(2)}, u32[]{:S(2)}) %collective-permute-start.9) | collective-permute-done | bytes 262176 | tf_op jit(solution)/shard_map/ppermute | solution.py:396
  53.5 8.0 %collective-permute-done.7.end_got_ref = bf16[32,32,128]{2,1,0:T(8,128)(2,1)S(1)} collective-permute-done((bf16[32,32,128]{2,1,0:T(8,128)(2,1)S(1)}, bf16[32,32,128]{2,1,0:T(8,128)(2,1)S(1)}, u32[]{:S(2)}, u32[]{:S(2)}) %collective-permute-start.7) | collective-permute-done | bytes 262176 | tf_op jit(solution)/shard_map/ppermute | solution.py:396
  61.4 5.6 %collective-permute-done.6.top_got_ref = bf16[32,32,128]{2,1,0:T(8,128)(2,1)S(1)} collective-permute-done((bf16[32,32,128]{2,1,0:T(8,128)(2,1)S(1)}, bf16[32,32,128]{2,1,0:T(8,128)(2,1)S(1)}, u32[]{:S(2)}, u32[]{:S(2)}) %collective-permute-start.6) | collective-permute-done | bytes 262176 | tf_op jit(solution)/shard_map/ppermute | solution.py:396
  67.0 6.4 %far_gradient.1 = (bf16[32,32,128]{2,1,0:T(8,128)(2,1)S(1)}, bf16[32,32,128]{2,1,0:T(8,128)(2,1)S(1)}, bf16[64,32,128]{2,1,0:T(8,128)(2,1)S(1)}, bf16[64,32,128]{2,1,0:T(8,128)(2,1)S(1)}) custom-call(bf16[4,256,256]{2,1,0:T(8,128)(2,1)S(1)} %copy-done.4, f32[16,128,128]{2,1,0:T(8,128)S(1)} %get-tuple-element.39.amp_ref, ...), custom_call_target="tpu_custom_call" | custom-call | flops 3221225472 | bytes 4194304 | tf_op jit(solution)/shard_map/far_gradient/pallas_call | solution.py:359
  73.7 8.8 %collective-permute-start.21 = (bf16[64,32,128]{2,1,0:T(8,128)(2,1)S(1)}, bf16[64,32,128]{2,1,0:T(8,128)(2,1)S(1)}, u32[]{:S(2)}, u32[]{:S(2)}) collective-permute-start(bf16[64,32,128]{2,1,0:T(8,128)(2,1)S(1)} %get-tuple-element.54), channel_id=1, source_target_pairs={{0,6},{1,7},{2,4},{3,5},{4,2},{5,3},{6,0},{7,1},{8,14},{9,15},{10,... | collective-permute-start | bytes 1572872 | tf_op jit(solution)/shard_map/ppermute | solution.py:396
  82.6 1.6 %collective-permute-start.24 = (bf16[32,32,128]{2,1,0:T(8,128)(2,1)S(1)}, bf16[32,32,128]{2,1,0:T(8,128)(2,1)S(1)}, u32[]{:S(2)}, u32[]{:S(2)}) collective-permute-start(bf16[32,32,128]{2,1,0:T(8,128)(2,1)S(1)} %get-tuple-element.56), channel_id=1, source_target_pairs={{0,2},{1,3},{2,0},{3,1},{4,6},{5,7},{6,4},{7,5},{8,10},{9,11},{10,... | collective-permute-start | bytes 786440 | tf_op jit(solution)/shard_map/ppermute | solution.py:396
  84.2 6.9 %collective-permute-done.13.refs_0_ = bf16[32,32,128]{2,1,0:T(8,128)(2,1)S(1)} collective-permute-done((bf16[32,32,128]{2,1,0:T(8,128)(2,1)S(1)}, bf16[32,32,128]{2,1,0:T(8,128)(2,1)S(1)}, u32[]{:S(2)}, u32[]{:S(2)}) %collective-permute-start.13) | collective-permute-done | bytes 262176 | tf_op jit(solution)/shard_map/ppermute | solution.py:396
  91.1 6.3 %collective-permute-start.19 = (bf16[32,32,128]{2,1,0:T(8,128)(2,1)S(1)}, bf16[32,32,128]{2,1,0:T(8,128)(2,1)S(1)}, u32[]{:S(2)}, u32[]{:S(2)}) collective-permute-start(bf16[32,32,128]{2,1,0:T(8,128)(2,1)S(1)} %collective-permute-done.14.refs_5_), channel_id=1, source_target_pairs={{0,1},{1,0},{2,3},{3,2},{4,5},{5,4},{6,7},{7,6},{8,9},{9,8},{10,11... | collective-permute-start | bytes 786440 | tf_op jit(solution)/shard_map/ppermute | solution.py:396
  97.4 2.8 %collective-permute-start.18 = (bf16[64,32,128]{2,1,0:T(8,128)(2,1)S(1)}, bf16[64,32,128]{2,1,0:T(8,128)(2,1)S(1)}, u32[]{:S(2)}, u32[]{:S(2)}) collective-permute-start(bf16[64,32,128]{2,1,0:T(8,128)(2,1)S(1)} %get-tuple-element.53.refs_4_.refs_6_), channel_id=1, source_target_pairs={{0,1},{1,0},{2,3},{3,2},{4,5},{5,4},{6,7},{7,6},{8,9},{9,8},{10,11... | collective-permute-start | bytes 1572872 | tf_op jit(solution)/shard_map/ppermute | solution.py:396
  100.7 1.9 %collective-permute-start.23 = (bf16[64,32,128]{2,1,0:T(8,128)(2,1)S(1)}, bf16[64,32,128]{2,1,0:T(8,128)(2,1)S(1)}, u32[]{:S(2)}, u32[]{:S(2)}) collective-permute-start(bf16[64,32,128]{2,1,0:T(8,128)(2,1)S(1)} %collective-permute-done.21.refs_9_.refs_11_), channel_id=1, source_target_pairs={{0,1},{1,0},{2,3},{3,2},{4,5},{5,4},{6,7},{7,6},{8,9},{9,8},{10,11... | collective-permute-start | bytes 1572872 | tf_op jit(solution)/shard_map/ppermute | solution.py:396
  103.6 5.2 %collective-permute-done.15.refs_1_ = bf16[32,32,128]{2,1,0:T(8,128)(2,1)S(1)} collective-permute-done((bf16[32,32,128]{2,1,0:T(8,128)(2,1)S(1)}, bf16[32,32,128]{2,1,0:T(8,128)(2,1)S(1)}, u32[]{:S(2)}, u32[]{:S(2)}) %collective-permute-start.15) | collective-permute-done | bytes 262176 | tf_op jit(solution)/shard_map/ppermute | solution.py:396
  108.7 3.5 %collective-permute-start.17 = (bf16[32,32,128]{2,1,0:T(8,128)(2,1)S(1)}, bf16[32,32,128]{2,1,0:T(8,128)(2,1)S(1)}, u32[]{:S(2)}, u32[]{:S(2)}) collective-permute-start(bf16[32,32,128]{2,1,0:T(8,128)(2,1)S(1)} %collective-permute-done.15.refs_1_), channel_id=1, source_target_pairs={{0,1},{1,0},{2,3},{3,2},{4,5},{5,4},{6,7},{7,6},{8,9},{9,8},{10,11... | collective-permute-start | bytes 786440 | tf_op jit(solution)/shard_map/ppermute | solution.py:396
  113.8 6.4 %backward_gradient_0.1 = (bf16[2,256,64,128]{3,2,1,0:T(8,128)(2,1)}, f32[8,128]{1,0:T(8,128)S(1)}) custom-call(bf16[128,512]{1,0:T(8,128)(2,1)S(1)} %get-tuple-element.34.rem_ref, bf16[256,512]{1,0:T(8,128)(2,1)S(1)} %get-tuple-element.35.rest_ref, f32[384,128]{1,0:T(8,128)S(1)} %get-tuple-element.36.low_ref, f32[384,128]{1,0:T(8,128)S(1)} %get-tuple-element.37.high_ref, ...), custom_call_target="tpu_custom_call" | custom-call | flops 1610612736 | bytes 7340032 | tf_op jit(solution)/shard_map/backward_gradient_0/pallas_call | solution.py:256
  120.2 3.3 %collective-permute-done.25.refs_3_ = bf16[32,32,128]{2,1,0:T(8,128)(2,1)S(1)} collective-permute-done((bf16[32,32,128]{2,1,0:T(8,128)(2,1)S(1)}, bf16[32,32,128]{2,1,0:T(8,128)(2,1)S(1)}, u32[]{:S(2)}, u32[]{:S(2)}) %collective-permute-start.25) | collective-permute-done | bytes 262176 | tf_op jit(solution)/shard_map/ppermute | solution.py:396
  124.3 1.2 collective-permute-done.28.refs_5_
  125.5 6.4 %backward_gradient_32.1 = (bf16[2,256,64,128]{3,2,1,0:T(8,128)(2,1)}, f32[8,128]{1,0:T(8,128)}) custom-call(bf16[128,512]{1,0:T(8,128)(2,1)S(1)} %get-tuple-element.34.rem_ref, bf16[256,512]{1,0:T(8,128)(2,1)S(1)} %get-tuple-element.35.rest_ref, f32[384,128]{1,0:T(8,128)S(1)} %get-tuple-element.36.low_ref, ...), custom_call_target="tpu_custom_call", output_to_operand_aliasing={{0}: (4, {})} | custom-call | flops 1610612736 | bytes 7340032 | tf_op jit(solution)/shard_map/backward_gradient_32/pallas_call | solution.py:256
  (56 shorter events, 8.9 us)
Async XLA Ops:
  0.0 16.9 %copy-start.2 = (s32[2,256]{1,0:T(2,128)S(1)}, s32[2,256]{1,0:T(2,128)}, u32[]{:S(2)}) copy-start(s32[2,256]{1,0:T(2,128)} %freq_ref.1) | copy-start | bytes 6148
  1.5 15.4 %collective-permute-start.1 = (s32[3,64]{1,0:T(4,128)S(1)}, s32[3,64]{1,0:T(4,128)S(1)}, u32[]{:S(2)}, u32[]{:S(2)}) collective-permute-start(s32[3,64]{1,0:T(4,128)S(1)} %add_add_fusion.here_ref), channel_id=1, source_target_pairs={{0,8},{1,9},{2,10},{3,11},{4,12},{5,13},{6,14},{7,15},{8,16},{9,17... | collective-permute-start | bytes 2312 | tf_op jit(solution)/shard_map/ppermute | solution.py:396
  4.0 12.9 %collective-permute-start = (s32[3,64]{1,0:T(4,128)S(1)}, s32[3,64]{1,0:T(4,128)S(1)}, u32[]{:S(2)}, u32[]{:S(2)}) collective-permute-start(s32[3,64]{1,0:T(4,128)S(1)} %add_add_fusion.here_ref), channel_id=1, source_target_pairs={{0,4},{1,5},{2,6},{3,7},{4,8},{5,9},{6,10},{7,11},{8,12},{9,13},{1... | collective-permute-start | bytes 2312 | tf_op jit(solution)/shard_map/ppermute | solution.py:396
  18.4 48.6 %copy-start.4 = (bf16[4,256,256]{2,1,0:T(8,128)(2,1)S(1)}, bf16[4,256,256]{2,1,0:T(8,128)(2,1)}, u32[]{:S(2)}) copy-start(bf16[4,256,256]{2,1,0:T(8,128)(2,1)} %constant.41.clone.table_ref) | copy-start | bytes 1572868
  26.4 3.6 %collective-permute-start.4 = (bf16[64,64,128]{2,1,0:T(8,128)(2,1)S(1)}, bf16[64,64,128]{2,1,0:T(8,128)(2,1)S(1)}, u32[]{:S(2)}, u32[]{:S(2)}) collective-permute-start(bf16[64,64,128]{2,1,0:T(8,128)(2,1)S(1)} %get-tuple-element.47), channel_id=1, source_target_pairs={{0,1},{1,0},{2,3},{3,2},{4,5},{5,4},{6,7},{7,6},{8,9},{9,8},{10,11... | collective-permute-start | bytes 3145736 | tf_op jit(solution)/shard_map/ppermute | solution.py:396
  27.7 9.5 %collective-permute-start.10 = (bf16[64,64,128]{2,1,0:T(8,128)(2,1)S(1)}, bf16[64,64,128]{2,1,0:T(8,128)(2,1)S(1)}, u32[]{:S(2)}, u32[]{:S(2)}) collective-permute-start(bf16[64,64,128]{2,1,0:T(8,128)(2,1)S(1)} %get-tuple-element.49), channel_id=1, source_target_pairs={{0,1},{1,0},{2,3},{3,2},{4,5},{5,4},{6,7},{7,6},{8,9},{9,8},{10,11... | collective-permute-start | bytes 3145736 | tf_op jit(solution)/shard_map/ppermute | solution.py:396
  27.8 14.7 %collective-permute-start.3 = (bf16[64,64,128]{2,1,0:T(8,128)(2,1)S(1)}, bf16[64,64,128]{2,1,0:T(8,128)(2,1)S(1)}, u32[]{:S(2)}, u32[]{:S(2)}) collective-permute-start(bf16[64,64,128]{2,1,0:T(8,128)(2,1)S(1)} %get-tuple-element.45), channel_id=1, source_target_pairs={{0,1},{1,0},{2,3},{3,2},{4,5},{5,4},{6,7},{7,6},{8,9},{9,8},{10,11... | collective-permute-start | bytes 3145736 | tf_op jit(solution)/shard_map/ppermute | solution.py:396
  28.2 20.9 %collective-permute-start.2 = (bf16[16,128,128]{2,1,0:T(8,128)(2,1)S(1)}, bf16[16,128,128]{2,1,0:T(8,128)(2,1)S(1)}, u32[]{:S(2)}, u32[]{:S(2)}) collective-permute-start(bf16[16,128,128]{2,1,0:T(8,128)(2,1)S(1)} %get-tuple-element.40), channel_id=1, source_target_pairs={{4,12},{5,13},{6,14},{7,15},{12,20},{13,21},{14,22},{15,23},{20,28... | collective-permute-start | bytes 1572872 | tf_op jit(solution)/shard_map/ppermute | solution.py:426
  30.1 9.1 %collective-permute-start.8 = (bf16[32,32,128]{2,1,0:T(8,128)(2,1)S(1)}, bf16[32,32,128]{2,1,0:T(8,128)(2,1)S(1)}, u32[]{:S(2)}, u32[]{:S(2)}) collective-permute-start(bf16[32,32,128]{2,1,0:T(8,128)(2,1)S(1)} %add_convert_fusion.4), channel_id=1, source_target_pairs={{0,2},{1,3},{2,0},{3,1},{4,6},{5,7},{6,4},{7,5},{8,10},{9,11},{10,... | collective-permute-start | bytes 786440 | tf_op jit(solution)/shard_map/ppermute | solution.py:396
  32.8 15.1 %collective-permute-start.5 = (bf16[32,64,128]{2,1,0:T(8,128)(2,1)S(1)}, bf16[32,64,128]{2,1,0:T(8,128)(2,1)S(1)}, u32[]{:S(2)}, u32[]{:S(2)}) collective-permute-start(bf16[32,64,128]{2,1,0:T(8,128)(2,1)S(1)} %add_convert_fusion.2), channel_id=1, source_target_pairs={{0,120},{1,121},{2,122},{3,123},{4,12},{5,13},{6,14},{7,15},{8,0},... | collective-permute-start | bytes 1572872 | tf_op jit(solution)/shard_map/ppermute | solution.py:396
  37.5 16.0 %collective-permute-start.12 = (bf16[64,32,128]{2,1,0:T(8,128)(2,1)S(1)}, bf16[64,32,128]{2,1,0:T(8,128)(2,1)S(1)}, u32[]{:S(2)}, u32[]{:S(2)}) collective-permute-start(bf16[64,32,128]{2,1,0:T(8,128)(2,1)S(1)} %get-tuple-element.61), channel_id=1, source_target_pairs={{0,6},{1,7},{2,4},{3,5},{4,2},{5,3},{6,0},{7,1},{8,14},{9,15},{10,... | collective-permute-start | bytes 1572872 | tf_op jit(solution)/shard_map/ppermute | solution.py:396
  39.2 14.3 %collective-permute-start.11 = (bf16[64,32,128]{2,1,0:T(8,128)(2,1)S(1)}, bf16[64,32,128]{2,1,0:T(8,128)(2,1)S(1)}, u32[]{:S(2)}, u32[]{:S(2)}) collective-permute-start(bf16[64,32,128]{2,1,0:T(8,128)(2,1)S(1)} %get-tuple-element.62), channel_id=1, source_target_pairs={{0,4},{1,5},{2,6},{3,7},{4,0},{5,1},{6,2},{7,3},{8,12},{9,13},{10,... | collective-permute-start | bytes 1572872 | tf_op jit(solution)/shard_map/ppermute | solution.py:396
  42.5 11.0 %collective-permute-start.9 = (bf16[32,32,128]{2,1,0:T(8,128)(2,1)S(1)}, bf16[32,32,128]{2,1,0:T(8,128)(2,1)S(1)}, u32[]{:S(2)}, u32[]{:S(2)}) collective-permute-start(bf16[32,32,128]{2,1,0:T(8,128)(2,1)S(1)} %add_convert_fusion.3), channel_id=1, source_target_pairs={{0,120},{1,121},{2,122},{3,123},{4,12},{5,13},{6,14},{7,15},{8,0},... | collective-permute-start | bytes 786440 | tf_op jit(solution)/shard_map/ppermute | solution.py:396
  48.1 13.3 %collective-permute-start.7 = (bf16[32,32,128]{2,1,0:T(8,128)(2,1)S(1)}, bf16[32,32,128]{2,1,0:T(8,128)(2,1)S(1)}, u32[]{:S(2)}, u32[]{:S(2)}) collective-permute-start(bf16[32,32,128]{2,1,0:T(8,128)(2,1)S(1)} %get-tuple-element.63), channel_id=1, source_target_pairs={{0,2},{1,3},{2,0},{3,1},{4,6},{5,7},{6,4},{7,5},{8,10},{9,11},{10,... | collective-permute-start | bytes 786440 | tf_op jit(solution)/shard_map/ppermute | solution.py:396
  49.1 17.9 %collective-permute-start.6 = (bf16[32,32,128]{2,1,0:T(8,128)(2,1)S(1)}, bf16[32,32,128]{2,1,0:T(8,128)(2,1)S(1)}, u32[]{:S(2)}, u32[]{:S(2)}) collective-permute-start(bf16[32,32,128]{2,1,0:T(8,128)(2,1)S(1)} %get-tuple-element.64), channel_id=1, source_target_pairs={{0,2},{1,3},{2,0},{3,1},{4,6},{5,7},{6,4},{7,5},{8,10},{9,11},{10,... | collective-permute-start | bytes 786440 | tf_op jit(solution)/shard_map/ppermute | solution.py:396
  73.4 9.1 %collective-permute-start.14 = (bf16[32,32,128]{2,1,0:T(8,128)(2,1)S(1)}, bf16[32,32,128]{2,1,0:T(8,128)(2,1)S(1)}, u32[]{:S(2)}, u32[]{:S(2)}) collective-permute-start(bf16[32,32,128]{2,1,0:T(8,128)(2,1)S(1)} %get-tuple-element.50), channel_id=1, source_target_pairs={{0,2},{1,3},{2,0},{3,1},{4,6},{5,7},{6,4},{7,5},{8,10},{9,11},{10,... | collective-permute-start | bytes 786440 | tf_op jit(solution)/shard_map/ppermute | solution.py:396
  73.7 26.9 %collective-permute-start.21 = (bf16[64,32,128]{2,1,0:T(8,128)(2,1)S(1)}, bf16[64,32,128]{2,1,0:T(8,128)(2,1)S(1)}, u32[]{:S(2)}, u32[]{:S(2)}) collective-permute-start(bf16[64,32,128]{2,1,0:T(8,128)(2,1)S(1)} %get-tuple-element.54), channel_id=1, source_target_pairs={{0,6},{1,7},{2,4},{3,5},{4,2},{5,3},{6,0},{7,1},{8,14},{9,15},{10,... | collective-permute-start | bytes 1572872 | tf_op jit(solution)/shard_map/ppermute | solution.py:396
  82.5 20.0 %collective-permute-start.20 = (bf16[64,32,128]{2,1,0:T(8,128)(2,1)S(1)}, bf16[64,32,128]{2,1,0:T(8,128)(2,1)S(1)}, u32[]{:S(2)}, u32[]{:S(2)}) collective-permute-start(bf16[64,32,128]{2,1,0:T(8,128)(2,1)S(1)} %get-tuple-element.54), channel_id=1, source_target_pairs={{0,4},{1,5},{2,6},{3,7},{4,0},{5,1},{6,2},{7,3},{8,12},{9,13},{10,... | collective-permute-start | bytes 1572872 | tf_op jit(solution)/shard_map/ppermute | solution.py:396
  82.5 8.5 %collective-permute-start.13 = (bf16[32,32,128]{2,1,0:T(8,128)(2,1)S(1)}, bf16[32,32,128]{2,1,0:T(8,128)(2,1)S(1)}, u32[]{:S(2)}, u32[]{:S(2)}) collective-permute-start(bf16[32,32,128]{2,1,0:T(8,128)(2,1)S(1)} %get-tuple-element.50), channel_id=1, source_target_pairs={{0,8},{1,9},{2,10},{3,11},{4,124},{5,125},{6,126},{7,127},{8,16},{... | collective-permute-start | bytes 786440 | tf_op jit(solution)/shard_map/ppermute | solution.py:396
  82.5 14.9 %collective-permute-start.26 = (bf16[32,32,128]{2,1,0:T(8,128)(2,1)S(1)}, bf16[32,32,128]{2,1,0:T(8,128)(2,1)S(1)}, u32[]{:S(2)}, u32[]{:S(2)}) collective-permute-start(bf16[32,32,128]{2,1,0:T(8,128)(2,1)S(1)} %get-tuple-element.56), channel_id=1, source_target_pairs={{0,8},{1,9},{2,10},{3,11},{4,124},{5,125},{6,126},{7,127},{8,16},{... | collective-permute-start | bytes 786440 | tf_op jit(solution)/shard_map/ppermute | solution.py:396
  82.6 17.6 %collective-permute-start.24 = (bf16[32,32,128]{2,1,0:T(8,128)(2,1)S(1)}, bf16[32,32,128]{2,1,0:T(8,128)(2,1)S(1)}, u32[]{:S(2)}, u32[]{:S(2)}) collective-permute-start(bf16[32,32,128]{2,1,0:T(8,128)(2,1)S(1)} %get-tuple-element.56), channel_id=1, source_target_pairs={{0,2},{1,3},{2,0},{3,1},{4,6},{5,7},{6,4},{7,5},{8,10},{9,11},{10,... | collective-permute-start | bytes 786440 | tf_op jit(solution)/shard_map/ppermute | solution.py:396
  91.1 12.5 %collective-permute-start.19 = (bf16[32,32,128]{2,1,0:T(8,128)(2,1)S(1)}, bf16[32,32,128]{2,1,0:T(8,128)(2,1)S(1)}, u32[]{:S(2)}, u32[]{:S(2)}) collective-permute-start(bf16[32,32,128]{2,1,0:T(8,128)(2,1)S(1)} %collective-permute-done.14.refs_5_), channel_id=1, source_target_pairs={{0,1},{1,0},{2,3},{3,2},{4,5},{5,4},{6,7},{7,6},{8,9},{9,8},{10,11... | collective-permute-start | bytes 786440 | tf_op jit(solution)/shard_map/ppermute | solution.py:396
  97.4 14.9 %collective-permute-start.18 = (bf16[64,32,128]{2,1,0:T(8,128)(2,1)S(1)}, bf16[64,32,128]{2,1,0:T(8,128)(2,1)S(1)}, u32[]{:S(2)}, u32[]{:S(2)}) collective-permute-start(bf16[64,32,128]{2,1,0:T(8,128)(2,1)S(1)} %get-tuple-element.53.refs_4_.refs_6_), channel_id=1, source_target_pairs={{0,1},{1,0},{2,3},{3,2},{4,5},{5,4},{6,7},{7,6},{8,9},{9,8},{10,11... | collective-permute-start | bytes 1572872 | tf_op jit(solution)/shard_map/ppermute | solution.py:396
  100.2 8.5 %collective-permute-start.15 = (bf16[32,32,128]{2,1,0:T(8,128)(2,1)S(1)}, bf16[32,32,128]{2,1,0:T(8,128)(2,1)S(1)}, u32[]{:S(2)}, u32[]{:S(2)}) collective-permute-start(bf16[32,32,128]{2,1,0:T(8,128)(2,1)S(1)} %collective-permute-done.14.refs_5_), channel_id=1, source_target_pairs={{0,8},{1,9},{2,10},{3,11},{4,124},{5,125},{6,126},{7,127},{8,16},{... | collective-permute-start | bytes 786440 | tf_op jit(solution)/shard_map/ppermute | solution.py:396
  100.7 13.1 %collective-permute-start.23 = (bf16[64,32,128]{2,1,0:T(8,128)(2,1)S(1)}, bf16[64,32,128]{2,1,0:T(8,128)(2,1)S(1)}, u32[]{:S(2)}, u32[]{:S(2)}) collective-permute-start(bf16[64,32,128]{2,1,0:T(8,128)(2,1)S(1)} %collective-permute-done.21.refs_9_.refs_11_), channel_id=1, source_target_pairs={{0,1},{1,0},{2,3},{3,2},{4,5},{5,4},{6,7},{7,6},{8,9},{9,8},{10,11... | collective-permute-start | bytes 1572872 | tf_op jit(solution)/shard_map/ppermute | solution.py:396
  102.6 11.2 %collective-permute-start.22 = (bf16[64,32,128]{2,1,0:T(8,128)(2,1)S(1)}, bf16[64,32,128]{2,1,0:T(8,128)(2,1)S(1)}, u32[]{:S(2)}, u32[]{:S(2)}) collective-permute-start(bf16[64,32,128]{2,1,0:T(8,128)(2,1)S(1)} %collective-permute-done.20.refs_8_.refs_10_), channel_id=1, source_target_pairs={{0,1},{1,0},{2,3},{3,2},{4,5},{5,4},{6,7},{7,6},{8,9},{9,8},{10,11... | collective-permute-start | bytes 1572872 | tf_op jit(solution)/shard_map/ppermute | solution.py:396
  103.6 8.7 %collective-permute-start.16 = (bf16[32,32,128]{2,1,0:T(8,128)(2,1)S(1)}, bf16[32,32,128]{2,1,0:T(8,128)(2,1)S(1)}, u32[]{:S(2)}, u32[]{:S(2)}) collective-permute-start(bf16[32,32,128]{2,1,0:T(8,128)(2,1)S(1)} %collective-permute-done.13.refs_0_), channel_id=1, source_target_pairs={{0,1},{1,0},{2,3},{3,2},{4,5},{5,4},{6,7},{7,6},{8,9},{9,8},{10,11... | collective-permute-start | bytes 786440 | tf_op jit(solution)/shard_map/ppermute | solution.py:396
  108.7 4.7 %collective-permute-start.17 = (bf16[32,32,128]{2,1,0:T(8,128)(2,1)S(1)}, bf16[32,32,128]{2,1,0:T(8,128)(2,1)S(1)}, u32[]{:S(2)}, u32[]{:S(2)}) collective-permute-start(bf16[32,32,128]{2,1,0:T(8,128)(2,1)S(1)} %collective-permute-done.15.refs_1_), channel_id=1, source_target_pairs={{0,1},{1,0},{2,3},{3,2},{4,5},{5,4},{6,7},{7,6},{8,9},{9,8},{10,11... | collective-permute-start | bytes 786440 | tf_op jit(solution)/shard_map/ppermute | solution.py:396
  112.2 11.3 %collective-permute-start.25 = (bf16[32,32,128]{2,1,0:T(8,128)(2,1)S(1)}, bf16[32,32,128]{2,1,0:T(8,128)(2,1)S(1)}, u32[]{:S(2)}, u32[]{:S(2)}) collective-permute-start(bf16[32,32,128]{2,1,0:T(8,128)(2,1)S(1)} %collective-permute-done.24.refs_7_), channel_id=1, source_target_pairs={{0,8},{1,9},{2,10},{3,11},{4,124},{5,125},{6,126},{7,127},{8,16},{... | collective-permute-start | bytes 786440 | tf_op jit(solution)/shard_map/ppermute | solution.py:396
  112.3 12.0 %collective-permute-start.27 = (bf16[32,32,128]{2,1,0:T(8,128)(2,1)S(1)}, bf16[32,32,128]{2,1,0:T(8,128)(2,1)S(1)}, u32[]{:S(2)}, u32[]{:S(2)}) collective-permute-start(bf16[32,32,128]{2,1,0:T(8,128)(2,1)S(1)} %collective-permute-done.26.refs_2_), channel_id=1, source_target_pairs={{0,1},{1,0},{2,3},{3,2},{4,5},{5,4},{6,7},{7,6},{8,9},{9,8},{10,11... | collective-permute-start | bytes 786440 | tf_op jit(solution)/shard_map/ppermute | solution.py:396
  113.4 10.9 %collective-permute-start.29 = (bf16[32,32,128]{2,1,0:T(8,128)(2,1)S(1)}, bf16[32,32,128]{2,1,0:T(8,128)(2,1)S(1)}, u32[]{:S(2)}, u32[]{:S(2)}) collective-permute-start(bf16[32,32,128]{2,1,0:T(8,128)(2,1)S(1)} %collective-permute-done.24.refs_7_), channel_id=1, source_target_pairs={{0,1},{1,0},{2,3},{3,2},{4,5},{5,4},{6,7},{7,6},{8,9},{9,8},{10,11... | collective-permute-start | bytes 786440 | tf_op jit(solution)/shard_map/ppermute | solution.py:396
  123.5 1.9 %collective-permute-start.28 = (bf16[32,32,128]{2,1,0:T(8,128)(2,1)S(1)}, bf16[32,32,128]{2,1,0:T(8,128)(2,1)S(1)}, u32[]{:S(2)}, u32[]{:S(2)}) collective-permute-start(bf16[32,32,128]{2,1,0:T(8,128)(2,1)S(1)} %collective-permute-done.25.refs_3_), channel_id=1, source_target_pairs={{0,1},{1,0},{2,3},{3,2},{4,5},{5,4},{6,7},{7,6},{8,9},{9,8},{10,11... | collective-permute-start | bytes 786440 | tf_op jit(solution)/shard_map/ppermute | solution.py:396
  (3 other events, 22.5 us)

commit v3 on v2

--- a/solution.py
+++ b/solution.py
@@ -1,4 +1,3 @@
-import functools
 import math
 
 import jax
@@ -137,58 +136,48 @@
     return dot(high, value_hi) + (dot(high, value_lo) + dot(low, value_hi))
 
 
-def transpose_kernel(at_ref, field_ref, amp_ref, out_ref, own_ref, sent_ref):
-    parts, beams, rows, window = field_ref.shape
-    out_ref[...] = jnp.swapaxes(field_ref[...].reshape(parts * beams, rows, window), 0, 1)
-    own_ref[...] = amp_ref[...]
-    sent_ref[...] = amp_ref[...].astype(BF16)
-
-
-def rows_first(at, smatrix, amplitude):
+FIELD_CUTS = 4
+
+
+def transpose_kernel(*refs):
+    field_refs, out_ref = refs[:-1], refs[-1]
+    _, beams, rows, window = field_refs[0].shape
+    for k, field_ref in enumerate(field_refs):
+        turned = jnp.swapaxes(field_ref[...].reshape(beams, rows, window), 0, 1)
+        out_ref[:, k * beams : (k + 1) * beams, :] = turned
+
+
+def rows_first(smatrix):
     parts, beams, strip_rows, window = smatrix.shape
-    blocks = strip_rows // Y_BLOCK
-    quarter = amplitude.shape[0] // 4
-    each = quarter // (blocks * parts)
-    amp_block = (each, *amplitude.shape[1:])
-    amp_out = pl.BlockSpec(amp_block, lambda i, p, at: (i * parts + p, 0, 0))
+    cut = beams // FIELD_CUTS
     return pl.pallas_call(
         transpose_kernel,
-        grid_spec=pltpu.PrefetchScalarGridSpec(
-            num_scalar_prefetch=1,
-            grid=(blocks, parts),
-            in_specs=[
-                pl.BlockSpec((1, beams, Y_BLOCK, window), lambda i, p, at: (p, 0, i, 0)),
-                pl.BlockSpec(
-                    amp_block, lambda i, p, at: (at[0] * (blocks * parts) + i * parts + p, 0, 0)
-                ),
-            ],
-            out_specs=[
-                pl.BlockSpec((Y_BLOCK, beams, window), lambda i, p, at: (i, p, 0)),
-                amp_out,
-                amp_out,
-            ],
-        ),
-        out_shape=[
-            jax.ShapeDtypeStruct((strip_rows, parts * beams, window), BF16),
-            jax.ShapeDtypeStruct((quarter, *amplitude.shape[1:]), F32),
-            jax.ShapeDtypeStruct((quarter, *amplitude.shape[1:]), BF16),
+        grid=(strip_rows // Y_BLOCK, parts),
+        in_specs=[
+            pl.BlockSpec((1, cut, Y_BLOCK, window), lambda i, p, k=k: (p, k, i, 0))
+            for k in range(FIELD_CUTS)
         ],
-        compiler_params=pltpu.CompilerParams(vmem_limit_bytes=24 << 20),
+        out_specs=pl.BlockSpec((Y_BLOCK, beams, window), lambda i, p: (i, p, 0)),
+        out_shape=jax.ShapeDtypeStruct((strip_rows, parts * beams, window), BF16),
+        compiler_params=pltpu.CompilerParams(vmem_limit_bytes=38 << 20),
         cost_estimate=pl.CostEstimate(
             flops=0, bytes_accessed=4 * parts * beams * strip_rows * window, transcendentals=0
         ),
         name="rows_first",
-    )(at, smatrix, amplitude)
+    )(*[smatrix] * FIELD_CUTS)
 
 
 def forward_kernel(rem_ref, rest_ref, field_ref, *out_refs):
     coef = jnp.concatenate([rem_ref[...], rest_ref[...]], axis=0)
-    for y in range(field_ref.shape[0]):
-        waves = dot(coef, field_ref[y]).astype(BF16)
+    window = field_ref.shape[2]
+    for y in range(0, field_ref.shape[0], 2):
+        pair = jnp.concatenate([field_ref[y], field_ref[y + 1]], axis=1)
+        waves = dot(coef, pair).astype(BF16)
         start = 0
         for out_ref in out_refs:
             rows = out_ref.shape[1]
-            out_ref[y] = waves[start : start + rows]
+            for k in range(2):
+                out_ref[y + k] = waves[start : start + rows, k * window : (k + 1) * window]
             start += rows
 
 
@@ -214,11 +203,9 @@
     )(*coefs, field)
 
 
-def backward_kernel(first_row, has_before, rem_ref, rest_ref, low_ref, high_ref, *refs):
-    refs = refs[2:] if has_before else refs
-    wave_refs, out_ref, done_ref, turned = refs[:-3], refs[-3], refs[-2], refs[-1]
-    done_ref[...] = jnp.zeros_like(done_ref)
-    parts, beams = out_ref.shape[0], out_ref.shape[1]
+def backward_kernel(rem_ref, rest_ref, low_ref, high_ref, *refs):
+    wave_refs, out_ref, turned = refs[:-2], refs[-2], refs[-1]
+    parts, beams, _, window = out_ref.shape
     split_at = rem_ref.shape[0]
 
     @pl.when(pl.program_id(0) == 0)
@@ -226,78 +213,63 @@
         turned[:, :split_at] = rem_ref[...].T
         turned[:, split_at:] = rest_ref[...].T
 
-    first = pl.program_id(0) * Y_BLOCK + first_row
+    first = pl.program_id(0) * Y_BLOCK
     low, high = low_ref[...], high_ref[...]
-    rows = []
-    for y in range(Y_BLOCK):
+
+    def masked(y):
         waves = jnp.concatenate([ref[y] for ref in wave_refs], axis=0)
         row = (first + y).astype(F32)
         keep = jnp.logical_and(low <= row, row < high)
-        waves = jnp.where(keep, waves, jnp.zeros_like(waves))
-        rows.append(dot(turned[...], waves).astype(BF16))
+        return jnp.where(keep, waves, jnp.zeros_like(waves))
+
+    rows = []
+    for y in range(0, Y_BLOCK, 2):
+        waves = jnp.concatenate([masked(y), masked(y + 1)], axis=1)
+        gradient = dot(turned[...], waves).astype(BF16)
+        rows += [gradient[:, :window], gradient[:, window:]]
     by_row = jnp.stack(rows, axis=0)
-    out_ref[...] = jnp.swapaxes(by_row, 0, 1).reshape(parts, beams, Y_BLOCK, by_row.shape[2])
-
-
-def backward_gradient(coefs, low, high, pieces, parts, beams, first_row, strip_rows, before):
-    rows, window = pieces[0].shape[1:]
-    part_rows = strip_rows // 2
+    out_ref[...] = jnp.swapaxes(by_row, 0, 1).reshape(parts, beams, Y_BLOCK, window)
+
+
+def backward_gradient(coefs, low, high, pieces, parts, beams):
+    strip_rows, _, window = pieces[0].shape
     total = low.shape[0]
-    offset = first_row // Y_BLOCK
-    kept = [] if before is None else [*before]
-
-    def piece_spec(piece):
-        skip = offset if piece.shape[0] == strip_rows else 0
-        return pl.BlockSpec((Y_BLOCK, rows, window), lambda i: (i + skip, 0, 0))
 
     def whole(value):
         return pl.BlockSpec(value.shape, lambda i: (0, 0))
 
     return pl.pallas_call(
-        functools.partial(backward_kernel, first_row, before is not None),
-        grid=(part_rows // Y_BLOCK,),
+        backward_kernel,
+        grid=(strip_rows // Y_BLOCK,),
         in_specs=[whole(value) for value in (*coefs, low, high)]
-        + [pl.BlockSpec(memory_space=pl.ANY)] * len(kept)
-        + [piece_spec(piece) for piece in pieces],
-        out_specs=[
-            pl.BlockSpec((parts, beams, Y_BLOCK, window), lambda i: (0, 0, i + offset, 0)),
-            pl.BlockSpec((8, window), lambda i: (0, 0)),
-        ],
-        out_shape=[
-            jax.ShapeDtypeStruct((parts, beams, strip_rows, window), BF16),
-            jax.ShapeDtypeStruct((8, window), F32),
-        ],
+        + [pl.BlockSpec((Y_BLOCK, *piece.shape[1:]), lambda i: (i, 0, 0)) for piece in pieces],
+        out_specs=pl.BlockSpec((parts, beams, Y_BLOCK, window), lambda i: (0, 0, i, 0)),
+        out_shape=jax.ShapeDtypeStruct((parts, beams, strip_rows, window), BF16),
         scratch_shapes=[pltpu.VMEM((parts * beams, total), BF16)],
-        input_output_aliases={4: 0} if kept else {},
         compiler_params=pltpu.CompilerParams(vmem_limit_bytes=32 << 20),
         cost_estimate=pl.CostEstimate(
-            flops=2 * total * parts * beams * part_rows * window,
-            bytes_accessed=2 * (parts * beams + total) * part_rows * window,
+            flops=2 * total * parts * beams * strip_rows * window,
+            bytes_accessed=2 * (parts * beams + total) * strip_rows * window,
             transcendentals=0,
         ),
-        name=f"backward_gradient_{first_row}",
-    )(*coefs, low, high, *kept, *pieces)
+        name="backward_gradient",
+    )(*coefs, low, high, *pieces)
 
 
 def far_kernel(
     table_ref, amp_ref, moved_ref, odd_ref, live_ref, low_ref, high_ref, mine_ref, got_ref,
-    top_rem_ref, top_got_ref, end_got_ref, end_rem_ref, near_ref, cross_ref,
-    ga_top_ref, ga_end_ref, ga_ref, gb_ref, mid, back,
+    rem_own_ref, a_got_ref, near_ref, cross_ref, ga_ref, gb_ref, mid, back,
 ):
     half, both, window = near_ref.shape
-    part = half // 2
     count = both // 2
     fwd_hi, fwd_lo = table_ref[0], table_ref[1]
     inv_hi, inv_lo = table_ref[2], table_ref[3]
     own = mine_ref[...].astype(F32) + got_ref[...].astype(F32)
     row = lax.broadcasted_iota(jnp.int32, own.shape, 0).astype(F32)
     inside = jnp.logical_and(low_ref[...][None] <= row, row < high_ref[...][None])
-    top = jnp.where(inside[:part], own[:part], top_rem_ref[...].astype(F32))
-    top = top + top_got_ref[...].astype(F32)
-    end = own[part:] + end_got_ref[...].astype(F32)
-    end = jnp.where(inside[part:], end, end_rem_ref[...].astype(F32))
+    own = jnp.where(inside, own, rem_own_ref[...].astype(F32)) + a_got_ref[...].astype(F32)
     middle = near_ref[...].astype(F32) + cross_ref[...].astype(F32)
-    for first, total in ((0, top), (part, end), (half, middle)):
+    for first, total in ((0, own), (half, middle)):
         rows = total.shape[0]
         pair = jnp.concatenate([total[:, :count], total[:, count:]], axis=2)
         out = right_product(pair.reshape(rows * count, 2 * window), fwd_hi, fwd_lo)
@@ -306,7 +278,7 @@
     odd = jnp.broadcast_to(odd_ref[...], (2 * half, window)) > 0.0
 
     def amplitude(p):
-        return jnp.where(odd, moved_ref[p].astype(F32), amp_ref[p])
+        return jnp.where(odd, moved_ref[p].astype(F32), amp_ref[p].astype(F32))
 
     def one_pair(step, carry):
         first = step * 2
@@ -328,25 +300,18 @@
 
     lax.fori_loop(0, count // 2, one_pair, 0, unroll=2)
     live = live_ref[...][:, None, :1]
-    for first in range(0, 2 * half, part):
-        rows = back[:, first : first + part, :]
-        out = right_product(rows.reshape(count * part, 2 * window), inv_hi, inv_lo)
-        out = jnp.swapaxes(out.reshape(count, part, 2 * window) * live, 0, 1)
-        out_re, out_im = out[:, :, :window].astype(BF16), out[:, :, window:].astype(BF16)
-        g_ref = ga_ref if first < half else gb_ref
-        targets = [g_ref.at[first % half : first % half + part]]
-        if first < half:
-            targets.append(ga_end_ref if first else ga_top_ref)
-        for target in targets:
-            target[:, :count, :] = out_re
-            target[:, count:, :] = out_im
+    for first, g_ref in ((0, ga_ref), (half, gb_ref)):
+        rows = back[:, first : first + half, :]
+        out = right_product(rows.reshape(count * half, 2 * window), inv_hi, inv_lo)
+        out = jnp.swapaxes(out.reshape(count, half, 2 * window) * live, 0, 1)
+        g_ref[:, :count, :] = out[:, :, :window].astype(BF16)
+        g_ref[:, count:, :] = out[:, :, window:].astype(BF16)
 
 
 def far_gradient(tables, amplitude, moved, odd, live, low, high, pieces):
     half, both, window = pieces[-1].shape
     count = both // 2
-    shape = jax.ShapeDtypeStruct((half // 2, both, window), BF16)
-    whole_shape = jax.ShapeDtypeStruct((half, both, window), BF16)
+    shape = jax.ShapeDtypeStruct((half, both, window), BF16)
 
     def whole(value):
         return pl.BlockSpec(value.shape, lambda i: (0,) * value.ndim)
@@ -354,17 +319,17 @@
     def rows_of(value, index):
         return pl.BlockSpec((*value.shape[:-2], both, window), lambda i: index)
 
-    mine, got, top_rem, *rest = pieces
+    mine, got, *rest = pieces
     own_block = 4
     return pl.pallas_call(
         far_kernel,
         grid=(1,),
         in_specs=[whole(value) for value in (tables, amplitude, moved, odd, live)]
         + [rows_of(low, (own_block, 0)), rows_of(high, (own_block, 0))]
-        + [rows_of(value, (0, 0, 0)) for value in (mine, got, top_rem)]
+        + [rows_of(value, (0, 0, 0)) for value in (mine, got)]
         + [whole(value) for value in rest],
-        out_specs=[whole(shape), whole(shape), whole(whole_shape), whole(whole_shape)],
-        out_shape=[shape, shape, whole_shape, whole_shape],
+        out_specs=[whole(shape)] * 2,
+        out_shape=[shape] * 2,
         scratch_shapes=[
             pltpu.VMEM((count, 2 * half, 2 * window), F32),
             pltpu.VMEM((count, 2 * half, 2 * window), F32),
@@ -389,7 +354,7 @@
     hi, core = beam_at // 2, beam_at % 2
     at = core * 2 + hi
     odd = me % 2
-    where = jnp.stack([me, odd, core, hi, jnp.int32(scan_size), at]).astype(jnp.int32)
+    where = jnp.stack([me, odd, core, hi, jnp.int32(scan_size)]).astype(jnp.int32)
     odd_row = jnp.broadcast_to(odd.astype(F32), (1, window))
 
     def send(value, target):
@@ -421,15 +386,15 @@
         for pair in permutation(scan_size, lambda s, h, c: (s + 2, h, c))
         if (pair[0] // 4) % 2
     ]
-    smatrix, where, odd_row = lax.optimization_barrier((smatrix, where, odd_row))
-    field, own_amp, sent_amp = rows_first(where[5:], smatrix, amplitude)
-    moved_amp = lax.ppermute(sent_amp, AXES, odd_pairs)
+    own_amp = lax.dynamic_slice_in_dim(amplitude, at * quarter, quarter, 0).astype(BF16)
+    smatrix, where, odd_row, own_amp = lax.optimization_barrier((smatrix, where, odd_row, own_amp))
+    moved_amp = lax.ppermute(own_amp, AXES, odd_pairs)
+    field = rows_first(smatrix)
 
     coef_rem, coef_rest, low, high, live = coefficients(
         where, packed, before_1, before_2, beam_freq, beam_amp, parts, window
     )
     unit = 2 * quarter
-    part = strip_rows // 2
     tile_rows = 4 * unit
     coefs = (coef_rem, coef_rest)
 
@@ -439,58 +404,37 @@
     mine_rem, other_rem, mine_loc, other_loc, mine_mid, other_mid = forward_waves(
         coefs, field
     )
+    other_rem, moved_amp = lax.optimization_barrier((other_rem, moved_amp))
     got_rem = to_core(other_rem)
-    rem_top = to_owner(joined(mine_rem[:part], got_rem[:part]).astype(BF16))
-    end_got = to_hi(joined(mine_rem[part:, unit:], got_rem[part:, unit:]).astype(BF16))
-    rem_end = joined(mine_rem[part:, :unit], got_rem[part:, :unit]) + end_got.astype(F32)
-    rem_end = to_owner(rem_end.astype(BF16))
+    rem_other = to_owner(joined(mine_rem[:, unit:], got_rem[:, unit:]).astype(BF16))
     got_mid = to_core(other_mid)
     near_mid = to_near(joined(mine_mid[:, :unit], got_mid[:, :unit]).astype(BF16))
     cross_mid = to_cross(joined(mine_mid[:, unit:], got_mid[:, unit:]).astype(BF16))
     got_loc = to_core(other_loc)
-    loc_end_got = to_hi(joined(mine_loc[part:, unit:], got_loc[part:, unit:]).astype(BF16))
-
+    rem_own = joined(mine_rem[:, :unit], got_rem[:, :unit]).astype(BF16)
+    rem_own, rem_other = lax.optimization_barrier((rem_own, rem_other))
+    rem_own = to_owner(rem_own)
     far_rows = slice(tile_rows + unit, tile_rows + 2 * unit)
-    y_index = jnp.arange(part, dtype=F32)[:, None, None]
+    y_index = jnp.arange(strip_rows).astype(F32)[:, None, None]
     inside = jnp.logical_and(low[None, far_rows] <= y_index, y_index < high[None, far_rows])
-    top_sent = jnp.where(
-        inside,
-        joined(mine_loc[:part, unit:], got_loc[:part, unit:]),
-        rem_top[:, unit:].astype(F32),
+    sent = jnp.where(inside, joined(mine_loc[:, unit:], got_loc[:, unit:]), rem_other.astype(F32))
+    got_a = to_hi(sent.astype(BF16))
+
+    tables = jnp.asarray(dft_matrices(window))
+    grad_a, grad_b = far_gradient(
+        tables, own_amp, moved_amp, odd_row, live,
+        low, high, (mine_loc, got_loc, rem_own, got_a, near_mid, cross_mid),
     )
-    top_got = to_hi(top_sent.astype(BF16))
-
-    tables = jnp.asarray(dft_matrices(window))
-    ga_top, ga_end, grad_a, grad_b = far_gradient(
-        tables, own_amp, moved_amp, odd_row, live,
-        low, high, (mine_loc, got_loc, rem_top, top_got, loc_end_got, rem_end, near_mid, cross_mid),
-    )
-
-    ga_top_hi = to_hi(ga_top)
-    rem_top = to_strip(ga_top)
-    rem_end = to_strip(ga_end)
-    other_a = to_core(grad_a)
+
+    a_hi = to_hi(grad_a)
+    rem = to_strip(grad_a)
+    grad_b, a_hi = lax.optimization_barrier((grad_b, a_hi))
+    rem_hi = to_strip(a_hi)
     near, cross = to_near(grad_b), to_cross(grad_b)
-    ga_end, ga_top_hi = lax.optimization_barrier((ga_end, ga_top_hi))
-    rem_top_hi = to_strip(ga_top_hi)
-    ga_end_hi = to_hi(ga_end)
-    rem_end_hi = to_strip(ga_end_hi)
-    middle = [near, cross, to_core(near), to_core(cross)]
-
-    def ordered_pieces(rem, rem_hi, loc_hi):
-        remote = [rem, rem_hi, to_core(rem), to_core(rem_hi)]
-        return remote + [grad_a, loc_hi, other_a, to_core(loc_hi)] + middle
-
-    out, done = backward_gradient(
-        coefs, low, high, ordered_pieces(rem_top, rem_top_hi, ga_top_hi),
-        parts, beams, 0, strip_rows, None,
-    )
-    rem_end_hi, done = lax.optimization_barrier((rem_end_hi, done))
-    out, _ = backward_gradient(
-        coefs, low, high, ordered_pieces(rem_end, rem_end_hi, ga_end_hi),
-        parts, beams, part, strip_rows, (out, done),
-    )
-    return out
+    pieces = []
+    for own, other in ((rem, rem_hi), (grad_a, a_hi), (near, cross)):
+        pieces += [own, other, to_core(own), to_core(other)]
+    return backward_gradient(coefs, low, high, pieces, parts, beams)
 
 
 def solution(mesh):

time: 132 us -> 113 us (0.86)
  waiting for transfers between devices: 38.5 us -> 31.7 us
  Pallas kernels: 34 us -> 28.8 us
  local copies, waits for them, and re-layouts: 6.33 us -> 1.49 us
  starting transfers between devices: 50.4 us -> 48.2 us
    ppermute x29 -> x21, waiting for transfers between devices: 38.5 us -> 31.7 us  [send(): return lax.ppermute(value, AXES, permutation(scan_size, target))]
    unnamed x10 -> x6, local copies, waits for them, and re-layouts: 5.58 us -> 0.01 us
    pallas_call x1, Pallas kernels: 7.93 us -> 4.72 us  [forward_waves(): pl.pallas_call(forward_kernel, grid=(strip_rows // block,), in_specs=[pl....]
    ppermute x29 -> x21, starting transfers between devices: 49.8 us -> 47.5 us  [send(): return lax.ppermute(value, AXES, permutation(scan_size, target))]
    pallas_call x3 -> x2, Pallas kernels: 18.2 us -> 16.2 us  [the longest x1 9.13 us: backward_gradient(): pl.pallas_call(backward_kernel, grid=(strip_rows // Y_BLOCK,), in_specs=[...]
  transfers between devices with their start and end apart: 30 -> 22, of which waited for: 12 -> 6; matrix products, arithmetic and copies ran while one was open for 1% -> 2% of each run, Pallas kernels for 9% -> 12%
where the time goes in v3:
time: 113 us
  starting transfers between devices  48.2 us (43%)
  waiting for transfers between devices  31.7 us (28%)
  Pallas kernels  28.8 us (25%)
  other arithmetic  1.66 us (1%)
  local copies, waits for them, and re-layouts  1.49 us (1%)
    ppermute x21, starting transfers between devices, send(): return lax.ppermute(value, AXES, permutation(scan_size, target))  47.5 us
    ppermute x21, waiting for transfers between devices, send(): return lax.ppermute(value, AXES, permutation(scan_size, target))  31.7 us
    pallas_call x1, Pallas kernels, backward_gradient(): pl.pallas_call(backward_kernel, grid=(strip_rows // Y_BLOCK,), in_specs=[...  9.13 us
    pallas_call x1, Pallas kernels, rows_first(): pl.pallas_call(transpose_kernel, grid=(strip_rows // Y_BLOCK, parts), in_...  7.08 us
    pallas_call x1, Pallas kernels, far_gradient(): pl.pallas_call(far_kernel, grid=(1,), in_specs=[whole(value) for value in...  6.38 us
    pallas_call x1, Pallas kernels, forward_waves(): pl.pallas_call(forward_kernel, grid=(strip_rows // block,), in_specs=[pl....  4.72 us
  transfers between devices with their start and end apart: 22, of which 6 were waited for; matrix products, arithmetic and copies ran while one was open for 2% of the time, Pallas kernels for 12%

profile of v3, /device:TPU:1, one launch (start us, length us, event | category | flops | bytes accessed | tf_op | source)
XLA Modules:
  0.0 112.7 jit_solution(9180232099807340046)
XLA Ops:
  0.0 1.3 %dynamic-slice_convert_fusion.amp_ref = bf16[16,128,128]{2,1,0:T(8,128)(2,1)S(1)} fusion(f32[64,128,128]{2,1,0:T(8,128)} %param.14, s32[]{:T(128)S(6)} %select_n.25), kind=kLoop, calls=%fused_computation.5 | loop fusion | bytes 1048580 | tf_op jit(solution)/shard_map/convert_element_type | solution.py:389
  1.4 0.7 collective-permute-start.2
  2.8 0.7 add_add_fusion.here_ref
  3.6 4.9 %collective-permute-start = (s32[3,64]{1,0:T(4,128)S(1)}, s32[3,64]{1,0:T(4,128)S(1)}, u32[]{:S(2)}, u32[]{:S(2)}) collective-permute-start(s32[3,64]{1,0:T(4,128)S(1)} %add_add_fusion.here_ref), channel_id=1, source_target_pairs={{0,4},{1,5},{2,6},{3,7},{4,8},{5,9},{6,10},{7,11},{8,12},{9,13},{1... | collective-permute-start | bytes 2312 | tf_op jit(solution)/shard_map/ppermute | solution.py:361
  8.5 1.6 %collective-permute-start.1 = (s32[3,64]{1,0:T(4,128)S(1)}, s32[3,64]{1,0:T(4,128)S(1)}, u32[]{:S(2)}, u32[]{:S(2)}) collective-permute-start(s32[3,64]{1,0:T(4,128)S(1)} %add_add_fusion.here_ref), channel_id=1, source_target_pairs={{0,8},{1,9},{2,10},{3,11},{4,12},{5,13},{6,14},{7,15},{8,16},{9,17... | collective-permute-start | bytes 2312 | tf_op jit(solution)/shard_map/ppermute | solution.py:361
  10.1 7.1 %rows_first.1.field_ref = bf16[64,512,128]{2,1,0:T(8,128)(2,1)S(1)} custom-call(bf16[2,256,64,128]{3,2,1,0:T(8,128)(2,1)} %refs_3_, bf16[2,256,64,128]{3,2,1,0:T(8,128)(2,1)} %refs_3_, bf16[2,256,64,128]{3,2,1,0:T(8,128)(2,1)} %refs_3_, bf16[2,256,64,128]{3,2,1,0:T(8,128)(2,1)} %refs_3_), custom_call_target="tpu_custom_call" | custom-call | bytes 16777216 | tf_op jit(solution)/shard_map/rows_first/pallas_call | solution.py:153
  17.3 1.5 %coefficients.1 = (bf16[128,512]{1,0:T(8,128)(2,1)S(1)}, bf16[256,512]{1,0:T(8,128)(2,1)S(1)}, f32[384,128]{1,0:T(8,128)S(1)}, f32[384,128]{1,0:T(8,128)S(1)}, f32[16,128]{1,0:T(8,128)S(1)}) custom-call(s32[5]{0:T(128)S(1)} %stack.28.where_ref, s32[3,64]{1,0:T(4,128)S(1)} %add_add_fusion.here_ref, s32[3,64]{1,0:T(4,128)S(1)} %collective-permute-done.before_1_ref, ...), custom_call_target="tpu_custom_call" | custom-call | tf_op jit(solution)/shard_map/coefficients/pallas_call | solution.py:98
  18.8 4.7 %forward_waves.1 = (bf16[64,64,128]{2,1,0:T(8,128)(2,1)S(1)}, bf16[64,64,128]{2,1,0:T(8,128)(2,1)S(1)}, bf16[64,64,128]{2,1,0:T(8,128)(2,1)S(1)}, bf16[64,64,128...) custom-call(bf16[128,512]{1,0:T(8,128)(2,1)S(1)} %get-tuple-element.29.rem_ref, ...), custom_call_target="tpu_custom_call" | custom-call | flops 3221225472 | bytes 14680064 | tf_op jit(solution)/shard_map/forward_waves/pallas_call | solution.py:189
  23.5 1.6 %collective-permute-start.4 = (bf16[64,64,128]{2,1,0:T(8,128)(2,1)S(1)}, bf16[64,64,128]{2,1,0:T(8,128)(2,1)S(1)}, u32[]{:S(2)}, u32[]{:S(2)}) collective-permute-start(bf16[64,64,128]{2,1,0:T(8,128)(2,1)S(1)} %get-tuple-element.42), channel_id=1, source_target_pairs={{0,1},{1,0},{2,3},{3,2},{4,5},{5,4},{6,7},{7,6},{8,9},{9,8},{10,11... | collective-permute-start | bytes 3145736 | tf_op jit(solution)/shard_map/ppermute | solution.py:361
  25.2 0.4 collective-permute-start.3
  25.6 1.8 %collective-permute-done.4 = bf16[64,64,128]{2,1,0:T(8,128)(2,1)S(1)} collective-permute-done((bf16[64,64,128]{2,1,0:T(8,128)(2,1)S(1)}, bf16[64,64,128]{2,1,0:T(8,128)(2,1)S(1)}, u32[]{:S(2)}, u32[]{:S(2)}) %collective-permute-start.4) | collective-permute-done | bytes 1048608 | tf_op jit(solution)/shard_map/ppermute | solution.py:361
  27.7 3.2 %collective-permute-start.5 = (bf16[64,32,128]{2,1,0:T(8,128)(2,1)S(1)}, bf16[64,32,128]{2,1,0:T(8,128)(2,1)S(1)}, u32[]{:S(2)}, u32[]{:S(2)}) collective-permute-start(bf16[64,32,128]{2,1,0:T(8,128)(2,1)S(1)} %get-tuple-element.53), channel_id=1, source_target_pairs={{0,120},{1,121},{2,122},{3,123},{4,12},{5,13},{6,14},{7,15},{8,0},... | collective-permute-start | bytes 1572872 | tf_op jit(solution)/shard_map/ppermute | solution.py:361
  30.9 0.3 add_convert_fusion
  31.2 5.0 %collective-permute-start.10 = (bf16[64,32,128]{2,1,0:T(8,128)(2,1)S(1)}, bf16[64,32,128]{2,1,0:T(8,128)(2,1)S(1)}, u32[]{:S(2)}, u32[]{:S(2)}) collective-permute-start(bf16[64,32,128]{2,1,0:T(8,128)(2,1)S(1)} %get-tuple-element.51), channel_id=1, source_target_pairs={{0,6},{1,7},{2,4},{3,5},{4,2},{5,3},{6,0},{7,1},{8,14},{9,15},{10,... | collective-permute-start | bytes 1572872 | tf_op jit(solution)/shard_map/ppermute | solution.py:361
  36.2 5.6 %collective-permute-done.5 = bf16[64,32,128]{2,1,0:T(8,128)(2,1)S(1)} collective-permute-done((bf16[64,32,128]{2,1,0:T(8,128)(2,1)S(1)}, bf16[64,32,128]{2,1,0:T(8,128)(2,1)S(1)}, u32[]{:S(2)}, u32[]{:S(2)}) %collective-permute-start.5) | collective-permute-done | bytes 524320 | tf_op jit(solution)/shard_map/ppermute | solution.py:361
  41.8 0.4 select_convert_fusion
  42.2 2.5 %collective-permute-start.7 = (bf16[64,32,128]{2,1,0:T(8,128)(2,1)S(1)}, bf16[64,32,128]{2,1,0:T(8,128)(2,1)S(1)}, u32[]{:S(2)}, u32[]{:S(2)}) collective-permute-start(bf16[64,32,128]{2,1,0:T(8,128)(2,1)S(1)} %select_convert_fusion), channel_id=1, source_target_pairs={{0,2},{1,3},{2,0},{3,1},{4,6},{5,7},{6,4},{7,5},{8,10},{9,11},{10,... | collective-permute-start | bytes 1572872 | tf_op jit(solution)/shard_map/ppermute | solution.py:361
  44.7 5.5 %collective-permute-start.6 = (bf16[64,32,128]{2,1,0:T(8,128)(2,1)S(1)}, bf16[64,32,128]{2,1,0:T(8,128)(2,1)S(1)}, u32[]{:S(2)}, u32[]{:S(2)}) collective-permute-start(bf16[64,32,128]{2,1,0:T(8,128)(2,1)S(1)} %get-tuple-element.43), channel_id=1, source_target_pairs={{0,120},{1,121},{2,122},{3,123},{4,12},{5,13},{6,14},{7,15},{8,0},... | collective-permute-start | bytes 1572872 | tf_op jit(solution)/shard_map/ppermute | solution.py:361
  50.3 10.1 %collective-permute-done.7.a_got_ref = bf16[64,32,128]{2,1,0:T(8,128)(2,1)S(1)} collective-permute-done((bf16[64,32,128]{2,1,0:T(8,128)(2,1)S(1)}, bf16[64,32,128]{2,1,0:T(8,128)(2,1)S(1)}, u32[]{:S(2)}, u32[]{:S(2)}) %collective-permute-start.7) | collective-permute-done | bytes 524320 | tf_op jit(solution)/shard_map/ppermute | solution.py:361
  60.4 6.4 %far_gradient.1 = (bf16[64,32,128]{2,1,0:T(8,128)(2,1)S(1)}, bf16[64,32,128]{2,1,0:T(8,128)(2,1)S(1)}) custom-call(bf16[4,256,256]{2,1,0:T(8,128)(2,1)S(1)} %copy-done.2, bf16[16,128,128]{2,1,0:T(8,128)(2,1)S(1)} %dynamic-slice_convert_fusion.amp_ref, bf16[16,128,128]{2,1,0:T(8,128)(2,1)S(1)} %collective-permute-done.2.moved_ref, ...), custom_call_target="tpu_custom_call" | custom-call | flops 3221225472 | bytes 4194304 | tf_op jit(solution)/shard_map/far_gradient/pallas_call | solution.py:324
  66.8 1.8 %collective-permute-start.12 = (bf16[64,32,128]{2,1,0:T(8,128)(2,1)S(1)}, bf16[64,32,128]{2,1,0:T(8,128)(2,1)S(1)}, u32[]{:S(2)}, u32[]{:S(2)}) collective-permute-start(bf16[64,32,128]{2,1,0:T(8,128)(2,1)S(1)} %get-tuple-element.47.refs_4_), channel_id=1, source_target_pairs={{0,2},{1,3},{2,0},{3,1},{4,6},{5,7},{6,4},{7,5},{8,10},{9,11},{10,... | collective-permute-start | bytes 1572872 | tf_op jit(solution)/shard_map/ppermute | solution.py:361
  68.6 1.5 %collective-permute-start.16 = (bf16[64,32,128]{2,1,0:T(8,128)(2,1)S(1)}, bf16[64,32,128]{2,1,0:T(8,128)(2,1)S(1)}, u32[]{:S(2)}, u32[]{:S(2)}) collective-permute-start(bf16[64,32,128]{2,1,0:T(8,128)(2,1)S(1)} %get-tuple-element.47.refs_4_), channel_id=1, source_target_pairs={{0,1},{1,0},{2,3},{3,2},{4,5},{5,4},{6,7},{7,6},{8,9},{9,8},{10,11... | collective-permute-start | bytes 1572872 | tf_op jit(solution)/shard_map/ppermute | solution.py:361
  70.1 9.7 %collective-permute-done.12.refs_5_ = bf16[64,32,128]{2,1,0:T(8,128)(2,1)S(1)} collective-permute-done((bf16[64,32,128]{2,1,0:T(8,128)(2,1)S(1)}, bf16[64,32,128]{2,1,0:T(8,128)(2,1)S(1)}, u32[]{:S(2)}, u32[]{:S(2)}) %collective-permute-start.12) | collective-permute-done | bytes 524320 | tf_op jit(solution)/shard_map/ppermute | solution.py:361
  79.8 6.6 %collective-permute-start.18 = (bf16[64,32,128]{2,1,0:T(8,128)(2,1)S(1)}, bf16[64,32,128]{2,1,0:T(8,128)(2,1)S(1)}, u32[]{:S(2)}, u32[]{:S(2)}) collective-permute-start(bf16[64,32,128]{2,1,0:T(8,128)(2,1)S(1)} %get-tuple-element.50), channel_id=1, source_target_pairs={{0,4},{1,5},{2,6},{3,7},{4,0},{5,1},{6,2},{7,3},{8,12},{9,13},{10,... | collective-permute-start | bytes 1572872 | tf_op jit(solution)/shard_map/ppermute | solution.py:361
  86.5 0.6 collective-permute-start.19
  87.0 3.6 %collective-permute-start.17 = (bf16[64,32,128]{2,1,0:T(8,128)(2,1)S(1)}, bf16[64,32,128]{2,1,0:T(8,128)(2,1)S(1)}, u32[]{:S(2)}, u32[]{:S(2)}) collective-permute-start(bf16[64,32,128]{2,1,0:T(8,128)(2,1)S(1)} %collective-permute-done.12.refs_5_), channel_id=1, source_target_pairs={{0,1},{1,0},{2,3},{3,2},{4,5},{5,4},{6,7},{7,6},{8,9},{9,8},{10,11... | collective-permute-start | bytes 1572872 | tf_op jit(solution)/shard_map/ppermute | solution.py:361
  90.7 2.9 %collective-permute-done.13.refs_1_ = bf16[64,32,128]{2,1,0:T(8,128)(2,1)S(1)} collective-permute-done((bf16[64,32,128]{2,1,0:T(8,128)(2,1)S(1)}, bf16[64,32,128]{2,1,0:T(8,128)(2,1)S(1)}, u32[]{:S(2)}, u32[]{:S(2)}) %collective-permute-start.13) | collective-permute-done | bytes 524320 | tf_op jit(solution)/shard_map/ppermute | solution.py:361
  93.6 3.9 %collective-permute-start.15 = (bf16[64,32,128]{2,1,0:T(8,128)(2,1)S(1)}, bf16[64,32,128]{2,1,0:T(8,128)(2,1)S(1)}, u32[]{:S(2)}, u32[]{:S(2)}) collective-permute-start(bf16[64,32,128]{2,1,0:T(8,128)(2,1)S(1)} %collective-permute-done.13.refs_1_), channel_id=1, source_target_pairs={{0,1},{1,0},{2,3},{3,2},{4,5},{5,4},{6,7},{7,6},{8,9},{9,8},{10,11... | collective-permute-start | bytes 1572872 | tf_op jit(solution)/shard_map/ppermute | solution.py:361
  97.5 1.9 %collective-permute-start.20 = (bf16[64,32,128]{2,1,0:T(8,128)(2,1)S(1)}, bf16[64,32,128]{2,1,0:T(8,128)(2,1)S(1)}, u32[]{:S(2)}, u32[]{:S(2)}) collective-permute-start(bf16[64,32,128]{2,1,0:T(8,128)(2,1)S(1)} %collective-permute-done.18.refs_8_), channel_id=1, source_target_pairs={{0,1},{1,0},{2,3},{3,2},{4,5},{5,4},{6,7},{7,6},{8,9},{9,8},{10,11... | collective-permute-start | bytes 1572872 | tf_op jit(solution)/shard_map/ppermute | solution.py:361
  99.3 2.7 %collective-permute-start.21 = (bf16[64,32,128]{2,1,0:T(8,128)(2,1)S(1)}, bf16[64,32,128]{2,1,0:T(8,128)(2,1)S(1)}, u32[]{:S(2)}, u32[]{:S(2)}) collective-permute-start(bf16[64,32,128]{2,1,0:T(8,128)(2,1)S(1)} %collective-permute-done.19.refs_9_), channel_id=1, source_target_pairs={{0,1},{1,0},{2,3},{3,2},{4,5},{5,4},{6,7},{7,6},{8,9},{9,8},{10,11... | collective-permute-start | bytes 1572872 | tf_op jit(solution)/shard_map/ppermute | solution.py:361
  102.0 1.5 %collective-permute-done.21.refs_11_ = bf16[64,32,128]{2,1,0:T(8,128)(2,1)S(1)} collective-permute-done((bf16[64,32,128]{2,1,0:T(8,128)(2,1)S(1)}, bf16[64,32,128]{2,1,0:T(8,128)(2,1)S(1)}, u32[]{:S(2)}, u32[]{:S(2)}) %collective-permute-start.21) | collective-permute-done | bytes 524320 | tf_op jit(solution)/shard_map/ppermute | solution.py:361
  103.5 9.1 %backward_gradient.1 = bf16[2,256,64,128]{3,2,1,0:T(8,128)(2,1)} custom-call(bf16[128,512]{1,0:T(8,128)(2,1)S(1)} %get-tuple-element.29.rem_ref, bf16[256,512]{1,0:T(8,128)(2,1)S(1)} %get-tuple-element.30.rest_ref, f32[384,128]{1,0:T(8,128)S(1)} %get-tuple-element.31.low_ref, f32[384,128]{1,0:T(8,128)S(1)} %get-tuple-element.32.high_ref, ...), custom_call_target="tpu_custom_call" | custom-call | flops 3221225472 | bytes 14680064 | tf_op jit(solution)/shard_map/backward_gradient/pallas_call | solution.py:241
  (34 shorter events, 0.7 us)
Async XLA Ops:
  1.4 22.1 %collective-permute-start.2 = (bf16[16,128,128]{2,1,0:T(8,128)(2,1)S(1)}, bf16[16,128,128]{2,1,0:T(8,128)(2,1)S(1)}, u32[]{:S(2)}, u32[]{:S(2)}) collective-permute-start(bf16[16,128,128]{2,1,0:T(8,128)(2,1)S(1)} %dynamic-slice_convert_fusion.amp_ref), channel_id=1, source_target_pairs={{4,12},{5,13},{6,14},{7,15},{12,20},{13,21},{14,22},{15,23},{20,28... | collective-permute-start | bytes 1572872 | tf_op jit(solution)/shard_map/ppermute | solution.py:391
  3.6 13.7 %copy-start = (s32[2,256]{1,0:T(2,128)S(1)}, s32[2,256]{1,0:T(2,128)}, u32[]{:S(2)}) copy-start(s32[2,256]{1,0:T(2,128)} %freq_ref.1) | copy-start | bytes 6148
  3.6 13.7 %copy-start.1 = (f32[2,256]{1,0:T(2,128)S(1)}, f32[2,256]{1,0:T(2,128)}, u32[]{:S(2)}) copy-start(f32[2,256]{1,0:T(2,128)} %amp_ref.1) | copy-start | bytes 6148
  3.6 13.6 %collective-permute-start = (s32[3,64]{1,0:T(4,128)S(1)}, s32[3,64]{1,0:T(4,128)S(1)}, u32[]{:S(2)}, u32[]{:S(2)}) collective-permute-start(s32[3,64]{1,0:T(4,128)S(1)} %add_add_fusion.here_ref), channel_id=1, source_target_pairs={{0,4},{1,5},{2,6},{3,7},{4,8},{5,9},{6,10},{7,11},{8,12},{9,13},{1... | collective-permute-start | bytes 2312 | tf_op jit(solution)/shard_map/ppermute | solution.py:361
  8.5 8.7 %collective-permute-start.1 = (s32[3,64]{1,0:T(4,128)S(1)}, s32[3,64]{1,0:T(4,128)S(1)}, u32[]{:S(2)}, u32[]{:S(2)}) collective-permute-start(s32[3,64]{1,0:T(4,128)S(1)} %add_add_fusion.here_ref), channel_id=1, source_target_pairs={{0,8},{1,9},{2,10},{3,11},{4,12},{5,13},{6,14},{7,15},{8,16},{9,17... | collective-permute-start | bytes 2312 | tf_op jit(solution)/shard_map/ppermute | solution.py:361
  18.8 41.7 %copy-start.2 = (bf16[4,256,256]{2,1,0:T(8,128)(2,1)S(1)}, bf16[4,256,256]{2,1,0:T(8,128)(2,1)}, u32[]{:S(2)}) copy-start(bf16[4,256,256]{2,1,0:T(8,128)(2,1)} %constant.46.clone.table_ref) | copy-start | bytes 1572868
  23.5 3.9 %collective-permute-start.4 = (bf16[64,64,128]{2,1,0:T(8,128)(2,1)S(1)}, bf16[64,64,128]{2,1,0:T(8,128)(2,1)S(1)}, u32[]{:S(2)}, u32[]{:S(2)}) collective-permute-start(bf16[64,64,128]{2,1,0:T(8,128)(2,1)S(1)} %get-tuple-element.42), channel_id=1, source_target_pairs={{0,1},{1,0},{2,3},{3,2},{4,5},{5,4},{6,7},{7,6},{8,9},{9,8},{10,11... | collective-permute-start | bytes 3145736 | tf_op jit(solution)/shard_map/ppermute | solution.py:361
  25.1 5.8 %collective-permute-start.8 = (bf16[64,64,128]{2,1,0:T(8,128)(2,1)S(1)}, bf16[64,64,128]{2,1,0:T(8,128)(2,1)S(1)}, u32[]{:S(2)}, u32[]{:S(2)}) collective-permute-start(bf16[64,64,128]{2,1,0:T(8,128)(2,1)S(1)} %get-tuple-element.46), channel_id=1, source_target_pairs={{0,1},{1,0},{2,3},{3,2},{4,5},{5,4},{6,7},{7,6},{8,9},{9,8},{10,11... | collective-permute-start | bytes 3145736 | tf_op jit(solution)/shard_map/ppermute | solution.py:361
  25.2 16.6 %collective-permute-start.3 = (bf16[64,64,128]{2,1,0:T(8,128)(2,1)S(1)}, bf16[64,64,128]{2,1,0:T(8,128)(2,1)S(1)}, u32[]{:S(2)}, u32[]{:S(2)}) collective-permute-start(bf16[64,64,128]{2,1,0:T(8,128)(2,1)S(1)} %get-tuple-element.40), channel_id=1, source_target_pairs={{0,1},{1,0},{2,3},{3,2},{4,5},{5,4},{6,7},{7,6},{8,9},{9,8},{10,11... | collective-permute-start | bytes 3145736 | tf_op jit(solution)/shard_map/ppermute | solution.py:361
  27.7 14.2 %collective-permute-start.5 = (bf16[64,32,128]{2,1,0:T(8,128)(2,1)S(1)}, bf16[64,32,128]{2,1,0:T(8,128)(2,1)S(1)}, u32[]{:S(2)}, u32[]{:S(2)}) collective-permute-start(bf16[64,32,128]{2,1,0:T(8,128)(2,1)S(1)} %get-tuple-element.53), channel_id=1, source_target_pairs={{0,120},{1,121},{2,122},{3,123},{4,12},{5,13},{6,14},{7,15},{8,0},... | collective-permute-start | bytes 1572872 | tf_op jit(solution)/shard_map/ppermute | solution.py:361
  31.2 19.1 %collective-permute-start.10 = (bf16[64,32,128]{2,1,0:T(8,128)(2,1)S(1)}, bf16[64,32,128]{2,1,0:T(8,128)(2,1)S(1)}, u32[]{:S(2)}, u32[]{:S(2)}) collective-permute-start(bf16[64,32,128]{2,1,0:T(8,128)(2,1)S(1)} %get-tuple-element.51), channel_id=1, source_target_pairs={{0,6},{1,7},{2,4},{3,5},{4,2},{5,3},{6,0},{7,1},{8,14},{9,15},{10,... | collective-permute-start | bytes 1572872 | tf_op jit(solution)/shard_map/ppermute | solution.py:361
  36.2 14.0 %collective-permute-start.9 = (bf16[64,32,128]{2,1,0:T(8,128)(2,1)S(1)}, bf16[64,32,128]{2,1,0:T(8,128)(2,1)S(1)}, u32[]{:S(2)}, u32[]{:S(2)}) collective-permute-start(bf16[64,32,128]{2,1,0:T(8,128)(2,1)S(1)} %get-tuple-element.52), channel_id=1, source_target_pairs={{0,4},{1,5},{2,6},{3,7},{4,0},{5,1},{6,2},{7,3},{8,12},{9,13},{10,... | collective-permute-start | bytes 1572872 | tf_op jit(solution)/shard_map/ppermute | solution.py:361
  42.2 18.2 %collective-permute-start.7 = (bf16[64,32,128]{2,1,0:T(8,128)(2,1)S(1)}, bf16[64,32,128]{2,1,0:T(8,128)(2,1)S(1)}, u32[]{:S(2)}, u32[]{:S(2)}) collective-permute-start(bf16[64,32,128]{2,1,0:T(8,128)(2,1)S(1)} %select_convert_fusion), channel_id=1, source_target_pairs={{0,2},{1,3},{2,0},{3,1},{4,6},{5,7},{6,4},{7,5},{8,10},{9,11},{10,... | collective-permute-start | bytes 1572872 | tf_op jit(solution)/shard_map/ppermute | solution.py:361
  44.7 15.7 %collective-permute-start.6 = (bf16[64,32,128]{2,1,0:T(8,128)(2,1)S(1)}, bf16[64,32,128]{2,1,0:T(8,128)(2,1)S(1)}, u32[]{:S(2)}, u32[]{:S(2)}) collective-permute-start(bf16[64,32,128]{2,1,0:T(8,128)(2,1)S(1)} %get-tuple-element.43), channel_id=1, source_target_pairs={{0,120},{1,121},{2,122},{3,123},{4,12},{5,13},{6,14},{7,15},{8,0},... | collective-permute-start | bytes 1572872 | tf_op jit(solution)/shard_map/ppermute | solution.py:361
  66.8 13.0 %collective-permute-start.12 = (bf16[64,32,128]{2,1,0:T(8,128)(2,1)S(1)}, bf16[64,32,128]{2,1,0:T(8,128)(2,1)S(1)}, u32[]{:S(2)}, u32[]{:S(2)}) collective-permute-start(bf16[64,32,128]{2,1,0:T(8,128)(2,1)S(1)} %get-tuple-element.47.refs_4_), channel_id=1, source_target_pairs={{0,2},{1,3},{2,0},{3,1},{4,6},{5,7},{6,4},{7,5},{8,10},{9,11},{10,... | collective-permute-start | bytes 1572872 | tf_op jit(solution)/shard_map/ppermute | solution.py:361
  68.6 18.4 %collective-permute-start.11 = (bf16[64,32,128]{2,1,0:T(8,128)(2,1)S(1)}, bf16[64,32,128]{2,1,0:T(8,128)(2,1)S(1)}, u32[]{:S(2)}, u32[]{:S(2)}) collective-permute-start(bf16[64,32,128]{2,1,0:T(8,128)(2,1)S(1)} %get-tuple-element.47.refs_4_), channel_id=1, source_target_pairs={{0,8},{1,9},{2,10},{3,11},{4,124},{5,125},{6,126},{7,127},{8,16},{... | collective-permute-start | bytes 1572872 | tf_op jit(solution)/shard_map/ppermute | solution.py:361
  68.6 22.0 %collective-permute-start.16 = (bf16[64,32,128]{2,1,0:T(8,128)(2,1)S(1)}, bf16[64,32,128]{2,1,0:T(8,128)(2,1)S(1)}, u32[]{:S(2)}, u32[]{:S(2)}) collective-permute-start(bf16[64,32,128]{2,1,0:T(8,128)(2,1)S(1)} %get-tuple-element.47.refs_4_), channel_id=1, source_target_pairs={{0,1},{1,0},{2,3},{3,2},{4,5},{5,4},{6,7},{7,6},{8,9},{9,8},{10,11... | collective-permute-start | bytes 1572872 | tf_op jit(solution)/shard_map/ppermute | solution.py:361
  79.8 13.8 %collective-permute-start.13 = (bf16[64,32,128]{2,1,0:T(8,128)(2,1)S(1)}, bf16[64,32,128]{2,1,0:T(8,128)(2,1)S(1)}, u32[]{:S(2)}, u32[]{:S(2)}) collective-permute-start(bf16[64,32,128]{2,1,0:T(8,128)(2,1)S(1)} %collective-permute-done.12.refs_5_), channel_id=1, source_target_pairs={{0,8},{1,9},{2,10},{3,11},{4,124},{5,125},{6,126},{7,127},{8,16},{... | collective-permute-start | bytes 1572872 | tf_op jit(solution)/shard_map/ppermute | solution.py:361
  79.8 17.7 %collective-permute-start.18 = (bf16[64,32,128]{2,1,0:T(8,128)(2,1)S(1)}, bf16[64,32,128]{2,1,0:T(8,128)(2,1)S(1)}, u32[]{:S(2)}, u32[]{:S(2)}) collective-permute-start(bf16[64,32,128]{2,1,0:T(8,128)(2,1)S(1)} %get-tuple-element.50), channel_id=1, source_target_pairs={{0,4},{1,5},{2,6},{3,7},{4,0},{5,1},{6,2},{7,3},{8,12},{9,13},{10,... | collective-permute-start | bytes 1572872 | tf_op jit(solution)/shard_map/ppermute | solution.py:361
  86.5 12.9 %collective-permute-start.19 = (bf16[64,32,128]{2,1,0:T(8,128)(2,1)S(1)}, bf16[64,32,128]{2,1,0:T(8,128)(2,1)S(1)}, u32[]{:S(2)}, u32[]{:S(2)}) collective-permute-start(bf16[64,32,128]{2,1,0:T(8,128)(2,1)S(1)} %get-tuple-element.50), channel_id=1, source_target_pairs={{0,6},{1,7},{2,4},{3,5},{4,2},{5,3},{6,0},{7,1},{8,14},{9,15},{10,... | collective-permute-start | bytes 1572872 | tf_op jit(solution)/shard_map/ppermute | solution.py:361
  87.0 15.0 %collective-permute-start.17 = (bf16[64,32,128]{2,1,0:T(8,128)(2,1)S(1)}, bf16[64,32,128]{2,1,0:T(8,128)(2,1)S(1)}, u32[]{:S(2)}, u32[]{:S(2)}) collective-permute-start(bf16[64,32,128]{2,1,0:T(8,128)(2,1)S(1)} %collective-permute-done.12.refs_5_), channel_id=1, source_target_pairs={{0,1},{1,0},{2,3},{3,2},{4,5},{5,4},{6,7},{7,6},{8,9},{9,8},{10,11... | collective-permute-start | bytes 1572872 | tf_op jit(solution)/shard_map/ppermute | solution.py:361
  90.6 11.4 %collective-permute-start.14 = (bf16[64,32,128]{2,1,0:T(8,128)(2,1)S(1)}, bf16[64,32,128]{2,1,0:T(8,128)(2,1)S(1)}, u32[]{:S(2)}, u32[]{:S(2)}) collective-permute-start(bf16[64,32,128]{2,1,0:T(8,128)(2,1)S(1)} %collective-permute-done.11.refs_0_), channel_id=1, source_target_pairs={{0,1},{1,0},{2,3},{3,2},{4,5},{5,4},{6,7},{7,6},{8,9},{9,8},{10,11... | collective-permute-start | bytes 1572872 | tf_op jit(solution)/shard_map/ppermute | solution.py:361
  93.6 8.4 %collective-permute-start.15 = (bf16[64,32,128]{2,1,0:T(8,128)(2,1)S(1)}, bf16[64,32,128]{2,1,0:T(8,128)(2,1)S(1)}, u32[]{:S(2)}, u32[]{:S(2)}) collective-permute-start(bf16[64,32,128]{2,1,0:T(8,128)(2,1)S(1)} %collective-permute-done.13.refs_1_), channel_id=1, source_target_pairs={{0,1},{1,0},{2,3},{3,2},{4,5},{5,4},{6,7},{7,6},{8,9},{9,8},{10,11... | collective-permute-start | bytes 1572872 | tf_op jit(solution)/shard_map/ppermute | solution.py:361
  97.5 4.5 %collective-permute-start.20 = (bf16[64,32,128]{2,1,0:T(8,128)(2,1)S(1)}, bf16[64,32,128]{2,1,0:T(8,128)(2,1)S(1)}, u32[]{:S(2)}, u32[]{:S(2)}) collective-permute-start(bf16[64,32,128]{2,1,0:T(8,128)(2,1)S(1)} %collective-permute-done.18.refs_8_), channel_id=1, source_target_pairs={{0,1},{1,0},{2,3},{3,2},{4,5},{5,4},{6,7},{7,6},{8,9},{9,8},{10,11... | collective-permute-start | bytes 1572872 | tf_op jit(solution)/shard_map/ppermute | solution.py:361
  99.3 4.2 %collective-permute-start.21 = (bf16[64,32,128]{2,1,0:T(8,128)(2,1)S(1)}, bf16[64,32,128]{2,1,0:T(8,128)(2,1)S(1)}, u32[]{:S(2)}, u32[]{:S(2)}) collective-permute-start(bf16[64,32,128]{2,1,0:T(8,128)(2,1)S(1)} %collective-permute-done.19.refs_9_), channel_id=1, source_target_pairs={{0,1},{1,0},{2,3},{3,2},{4,5},{5,4},{6,7},{7,6},{8,9},{9,8},{10,11... | collective-permute-start | bytes 1572872 | tf_op jit(solution)/shard_map/ppermute | solution.py:361

commit v4 on v3

--- a/solution.py
+++ b/solution.py
@@ -131,6 +131,11 @@
     return dot(value_hi, high) + (dot(value_lo, high) + dot(value_hi, low))
 
 
+def right_rounded(value, high, low):
+    value = value.astype(BF16)
+    return dot(value, high) + dot(value, low)
+
+
 def left_product(high, low, value):
     value_hi, value_lo = split(value)
     return dot(high, value_hi) + (dot(high, value_lo) + dot(low, value_hi))
@@ -203,35 +208,46 @@
     )(*coefs, field)
 
 
-def backward_kernel(rem_ref, rest_ref, low_ref, high_ref, *refs):
-    wave_refs, out_ref, turned = refs[:-2], refs[-2], refs[-1]
+def turn_kernel(rem_ref, rest_ref, out_ref):
+    split_at = rem_ref.shape[0]
+    out_ref[:, :split_at] = rem_ref[...].T
+    out_ref[:, split_at:] = rest_ref[...].T
+
+
+def turned(coefs):
+    total, depth = sum(coef.shape[0] for coef in coefs), coefs[0].shape[1]
+    return pl.pallas_call(
+        turn_kernel,
+        out_shape=jax.ShapeDtypeStruct((depth, total), BF16),
+        compiler_params=pltpu.CompilerParams(vmem_limit_bytes=16 << 20),
+        name="turned",
+    )(*coefs)
+
+
+def backward_kernel(coef_ref, low_ref, high_ref, *refs):
+    wave_refs, out_ref = refs[:-1], refs[-1]
     parts, beams, _, window = out_ref.shape
-    split_at = rem_ref.shape[0]
-
-    @pl.when(pl.program_id(0) == 0)
-    def turn():
-        turned[:, :split_at] = rem_ref[...].T
-        turned[:, split_at:] = rest_ref[...].T
-
     first = pl.program_id(0) * Y_BLOCK
-    low, high = low_ref[...], high_ref[...]
+    cut = low_ref.shape[0] // 3 * 2
+    low, high = low_ref[:cut].astype(BF16), high_ref[:cut].astype(BF16)
 
     def masked(y):
         waves = jnp.concatenate([ref[y] for ref in wave_refs], axis=0)
-        row = (first + y).astype(F32)
+        row = jnp.full((1, window), first + y, jnp.int32).astype(F32).astype(BF16)
         keep = jnp.logical_and(low <= row, row < high)
-        return jnp.where(keep, waves, jnp.zeros_like(waves))
+        edge = jnp.where(keep, waves[:cut], jnp.zeros_like(waves[:cut]))
+        return jnp.concatenate([edge, waves[cut:]], axis=0)
 
     rows = []
     for y in range(0, Y_BLOCK, 2):
         waves = jnp.concatenate([masked(y), masked(y + 1)], axis=1)
-        gradient = dot(turned[...], waves).astype(BF16)
+        gradient = dot(coef_ref[...], waves).astype(BF16)
         rows += [gradient[:, :window], gradient[:, window:]]
     by_row = jnp.stack(rows, axis=0)
     out_ref[...] = jnp.swapaxes(by_row, 0, 1).reshape(parts, beams, Y_BLOCK, window)
 
 
-def backward_gradient(coefs, low, high, pieces, parts, beams):
+def backward_gradient(coef_t, low, high, pieces, parts, beams):
     strip_rows, _, window = pieces[0].shape
     total = low.shape[0]
 
@@ -241,11 +257,10 @@
     return pl.pallas_call(
         backward_kernel,
         grid=(strip_rows // Y_BLOCK,),
-        in_specs=[whole(value) for value in (*coefs, low, high)]
+        in_specs=[whole(value) for value in (coef_t, low, high)]
         + [pl.BlockSpec((Y_BLOCK, *piece.shape[1:]), lambda i: (i, 0, 0)) for piece in pieces],
         out_specs=pl.BlockSpec((parts, beams, Y_BLOCK, window), lambda i: (0, 0, i, 0)),
         out_shape=jax.ShapeDtypeStruct((parts, beams, strip_rows, window), BF16),
-        scratch_shapes=[pltpu.VMEM((parts * beams, total), BF16)],
         compiler_params=pltpu.CompilerParams(vmem_limit_bytes=32 << 20),
         cost_estimate=pl.CostEstimate(
             flops=2 * total * parts * beams * strip_rows * window,
@@ -253,7 +268,7 @@
             transcendentals=0,
         ),
         name="backward_gradient",
-    )(*coefs, low, high, *pieces)
+    )(coef_t, low, high, *pieces)
 
 
 def far_kernel(
@@ -302,7 +317,7 @@
     live = live_ref[...][:, None, :1]
     for first, g_ref in ((0, ga_ref), (half, gb_ref)):
         rows = back[:, first : first + half, :]
-        out = right_product(rows.reshape(count * half, 2 * window), inv_hi, inv_lo)
+        out = right_rounded(rows.reshape(count * half, 2 * window), inv_hi, inv_lo)
         out = jnp.swapaxes(out.reshape(count, half, 2 * window) * live, 0, 1)
         g_ref[:, :count, :] = out[:, :, :window].astype(BF16)
         g_ref[:, count:, :] = out[:, :, window:].astype(BF16)
@@ -419,6 +434,7 @@
     inside = jnp.logical_and(low[None, far_rows] <= y_index, y_index < high[None, far_rows])
     sent = jnp.where(inside, joined(mine_loc[:, unit:], got_loc[:, unit:]), rem_other.astype(F32))
     got_a = to_hi(sent.astype(BF16))
+    coef_t = turned(coefs)
 
     tables = jnp.asarray(dft_matrices(window))
     grad_a, grad_b = far_gradient(
@@ -428,13 +444,12 @@
 
     a_hi = to_hi(grad_a)
     rem = to_strip(grad_a)
-    grad_b, a_hi = lax.optimization_barrier((grad_b, a_hi))
     rem_hi = to_strip(a_hi)
     near, cross = to_near(grad_b), to_cross(grad_b)
     pieces = []
     for own, other in ((rem, rem_hi), (grad_a, a_hi), (near, cross)):
         pieces += [own, other, to_core(own), to_core(other)]
-    return backward_gradient(coefs, low, high, pieces, parts, beams)
+    return backward_gradient(coef_t, low, high, pieces, parts, beams)
 
 
 def solution(mesh):

time: 113 us -> 111 us (0.982)
  starting transfers between devices: 48.2 us -> 45.7 us
  waiting for transfers between devices: 31.7 us -> 33.5 us
    ppermute x21, starting transfers between devices: 47.5 us -> 45 us  [send(): return lax.ppermute(value, AXES, permutation(scan_size, target))]
    ppermute x21, waiting for transfers between devices: 31.7 us -> 33.5 us  [send(): return lax.ppermute(value, AXES, permutation(scan_size, target))]
  transfers between devices with their start and end apart: 22 -> 22, of which waited for: 6 -> 10; matrix products, arithmetic and copies ran while one was open for 2% -> 2% of each run, Pallas kernels for 12% -> 12%
where the time goes in v4:
time: 111 us
  starting transfers between devices  45.7 us (41%)
  waiting for transfers between devices  33.5 us (30%)
  Pallas kernels  28 us (25%)
  other arithmetic  1.66 us (1%)
  local copies, waits for them, and re-layouts  1.49 us (1%)
    ppermute x21, starting transfers between devices, send(): return lax.ppermute(value, AXES, permutation(scan_size, target))  45 us
    ppermute x21, waiting for transfers between devices, send(): return lax.ppermute(value, AXES, permutation(scan_size, target))  33.5 us
    pallas_call x1, Pallas kernels, backward_gradient(): pl.pallas_call(backward_kernel, grid=(strip_rows // Y_BLOCK,), in_specs=[...  8.45 us
    pallas_call x1, Pallas kernels, rows_first(): pl.pallas_call(transpose_kernel, grid=(strip_rows // Y_BLOCK, parts), in_...  7.08 us
    pallas_call x1, Pallas kernels, far_gradient(): pl.pallas_call(far_kernel, grid=(1,), in_specs=[whole(value) for value in...  6.11 us
    pallas_call x1, Pallas kernels, forward_waves(): pl.pallas_call(forward_kernel, grid=(strip_rows // block,), in_specs=[pl....  4.71 us
  transfers between devices with their start and end apart: 22, of which 10 were waited for; matrix products, arithmetic and copies ran while one was open for 2% of the time, Pallas kernels for 12%

profile of v4, /device:TPU:1, one launch (start us, length us, event | category | flops | bytes accessed | tf_op | source)
XLA Modules:
  0.0 111.2 jit_solution(3778574925578312878)
XLA Ops:
  0.0 1.3 %dynamic-slice_convert_fusion.amp_ref = bf16[16,128,128]{2,1,0:T(8,128)(2,1)S(1)} fusion(f32[64,128,128]{2,1,0:T(8,128)} %param.14, s32[]{:T(128)S(6)} %select_n.25), kind=kLoop, calls=%fused_computation.5 | loop fusion | bytes 1048580 | tf_op jit(solution)/shard_map/convert_element_type | solution.py:404
  1.4 0.7 collective-permute-start.2
  2.8 0.7 add_add_fusion.here_ref
  3.6 4.9 %collective-permute-start = (s32[3,64]{1,0:T(4,128)S(1)}, s32[3,64]{1,0:T(4,128)S(1)}, u32[]{:S(2)}, u32[]{:S(2)}) collective-permute-start(s32[3,64]{1,0:T(4,128)S(1)} %add_add_fusion.here_ref), channel_id=1, source_target_pairs={{0,4},{1,5},{2,6},{3,7},{4,8},{5,9},{6,10},{7,11},{8,12},{9,13},{1... | collective-permute-start | bytes 2312 | tf_op jit(solution)/shard_map/ppermute | solution.py:376
  8.5 1.6 %collective-permute-start.1 = (s32[3,64]{1,0:T(4,128)S(1)}, s32[3,64]{1,0:T(4,128)S(1)}, u32[]{:S(2)}, u32[]{:S(2)}) collective-permute-start(s32[3,64]{1,0:T(4,128)S(1)} %add_add_fusion.here_ref), channel_id=1, source_target_pairs={{0,8},{1,9},{2,10},{3,11},{4,12},{5,13},{6,14},{7,15},{8,16},{9,17... | collective-permute-start | bytes 2312 | tf_op jit(solution)/shard_map/ppermute | solution.py:376
  10.1 7.1 %rows_first.1.field_ref = bf16[64,512,128]{2,1,0:T(8,128)(2,1)S(1)} custom-call(bf16[2,256,64,128]{3,2,1,0:T(8,128)(2,1)} %refs_3_, bf16[2,256,64,128]{3,2,1,0:T(8,128)(2,1)} %refs_3_, bf16[2,256,64,128]{3,2,1,0:T(8,128)(2,1)} %refs_3_, bf16[2,256,64,128]{3,2,1,0:T(8,128)(2,1)} %refs_3_), custom_call_target="tpu_custom_call" | custom-call | bytes 16777216 | tf_op jit(solution)/shard_map/rows_first/pallas_call | solution.py:158
  17.3 1.5 %coefficients.1 = (bf16[128,512]{1,0:T(8,128)(2,1)S(1)}, bf16[256,512]{1,0:T(8,128)(2,1)S(1)}, f32[384,128]{1,0:T(8,128)S(1)}, f32[384,128]{1,0:T(8,128)S(1)}, f32[16,128]{1,0:T(8,128)S(1)}) custom-call(s32[5]{0:T(128)S(1)} %stack.28.where_ref, s32[3,64]{1,0:T(4,128)S(1)} %add_add_fusion.here_ref, s32[3,64]{1,0:T(4,128)S(1)} %collective-permute-done.before_1_ref, ...), custom_call_target="tpu_custom_call" | custom-call | tf_op jit(solution)/shard_map/coefficients/pallas_call | solution.py:98
  18.8 4.7 %forward_waves.1 = (bf16[64,64,128]{2,1,0:T(8,128)(2,1)S(1)}, bf16[64,64,128]{2,1,0:T(8,128)(2,1)S(1)}, bf16[64,64,128]{2,1,0:T(8,128)(2,1)S(1)}, bf16[64,64,128...) custom-call(bf16[128,512]{1,0:T(8,128)(2,1)S(1)} %get-tuple-element.27.rem_ref, ...), custom_call_target="tpu_custom_call" | custom-call | flops 3221225472 | bytes 14680064 | tf_op jit(solution)/shard_map/forward_waves/pallas_call | solution.py:194
  23.5 1.6 %collective-permute-start.4 = (bf16[64,64,128]{2,1,0:T(8,128)(2,1)S(1)}, bf16[64,64,128]{2,1,0:T(8,128)(2,1)S(1)}, u32[]{:S(2)}, u32[]{:S(2)}) collective-permute-start(bf16[64,64,128]{2,1,0:T(8,128)(2,1)S(1)} %get-tuple-element.40), channel_id=1, source_target_pairs={{0,1},{1,0},{2,3},{3,2},{4,5},{5,4},{6,7},{7,6},{8,9},{9,8},{10,11... | collective-permute-start | bytes 3145736 | tf_op jit(solution)/shard_map/ppermute | solution.py:376
  25.6 1.8 %collective-permute-done.4 = bf16[64,64,128]{2,1,0:T(8,128)(2,1)S(1)} collective-permute-done((bf16[64,64,128]{2,1,0:T(8,128)(2,1)S(1)}, bf16[64,64,128]{2,1,0:T(8,128)(2,1)S(1)}, u32[]{:S(2)}, u32[]{:S(2)}) %collective-permute-start.4) | collective-permute-done | bytes 1048608 | tf_op jit(solution)/shard_map/ppermute | solution.py:376
  27.7 3.2 %collective-permute-start.5 = (bf16[64,32,128]{2,1,0:T(8,128)(2,1)S(1)}, bf16[64,32,128]{2,1,0:T(8,128)(2,1)S(1)}, u32[]{:S(2)}, u32[]{:S(2)}) collective-permute-start(bf16[64,32,128]{2,1,0:T(8,128)(2,1)S(1)} %get-tuple-element.49), channel_id=1, source_target_pairs={{0,120},{1,121},{2,122},{3,123},{4,12},{5,13},{6,14},{7,15},{8,0},... | collective-permute-start | bytes 1572872 | tf_op jit(solution)/shard_map/ppermute | solution.py:376
  31.2 5.0 %collective-permute-start.10 = (bf16[64,32,128]{2,1,0:T(8,128)(2,1)S(1)}, bf16[64,32,128]{2,1,0:T(8,128)(2,1)S(1)}, u32[]{:S(2)}, u32[]{:S(2)}) collective-permute-start(bf16[64,32,128]{2,1,0:T(8,128)(2,1)S(1)} %get-tuple-element.47), channel_id=1, source_target_pairs={{0,6},{1,7},{2,4},{3,5},{4,2},{5,3},{6,0},{7,1},{8,14},{9,15},{10,... | collective-permute-start | bytes 1572872 | tf_op jit(solution)/shard_map/ppermute | solution.py:376
  36.2 5.6 %collective-permute-done.5 = bf16[64,32,128]{2,1,0:T(8,128)(2,1)S(1)} collective-permute-done((bf16[64,32,128]{2,1,0:T(8,128)(2,1)S(1)}, bf16[64,32,128]{2,1,0:T(8,128)(2,1)S(1)}, u32[]{:S(2)}, u32[]{:S(2)}) %collective-permute-start.5) | collective-permute-done | bytes 524320 | tf_op jit(solution)/shard_map/ppermute | solution.py:376
  42.2 2.5 %collective-permute-start.7 = (bf16[64,32,128]{2,1,0:T(8,128)(2,1)S(1)}, bf16[64,32,128]{2,1,0:T(8,128)(2,1)S(1)}, u32[]{:S(2)}, u32[]{:S(2)}) collective-permute-start(bf16[64,32,128]{2,1,0:T(8,128)(2,1)S(1)} %select_convert_fusion), channel_id=1, source_target_pairs={{0,2},{1,3},{2,0},{3,1},{4,6},{5,7},{6,4},{7,5},{8,10},{9,11},{10,... | collective-permute-start | bytes 1572872 | tf_op jit(solution)/shard_map/ppermute | solution.py:376
  44.7 5.5 %collective-permute-start.6 = (bf16[64,32,128]{2,1,0:T(8,128)(2,1)S(1)}, bf16[64,32,128]{2,1,0:T(8,128)(2,1)S(1)}, u32[]{:S(2)}, u32[]{:S(2)}) collective-permute-start(bf16[64,32,128]{2,1,0:T(8,128)(2,1)S(1)} %get-tuple-element.41), channel_id=1, source_target_pairs={{0,120},{1,121},{2,122},{3,123},{4,12},{5,13},{6,14},{7,15},{8,0},... | collective-permute-start | bytes 1572872 | tf_op jit(solution)/shard_map/ppermute | solution.py:376
  50.3 10.2 %collective-permute-done.7.a_got_ref = bf16[64,32,128]{2,1,0:T(8,128)(2,1)S(1)} collective-permute-done((bf16[64,32,128]{2,1,0:T(8,128)(2,1)S(1)}, bf16[64,32,128]{2,1,0:T(8,128)(2,1)S(1)}, u32[]{:S(2)}, u32[]{:S(2)}) %collective-permute-start.7) | collective-permute-done | bytes 524320 | tf_op jit(solution)/shard_map/ppermute | solution.py:376
  60.4 6.1 %far_gradient.1 = (bf16[64,32,128]{2,1,0:T(8,128)(2,1)S(1)}, bf16[64,32,128]{2,1,0:T(8,128)(2,1)S(1)}) custom-call(bf16[4,256,256]{2,1,0:T(8,128)(2,1)S(1)} %copy-done.2, bf16[16,128,128]{2,1,0:T(8,128)(2,1)S(1)} %dynamic-slice_convert_fusion.amp_ref, bf16[16,128,128]{2,1,0:T(8,128)(2,1)S(1)} %collective-permute-done.2.moved_ref, ...), custom_call_target="tpu_custom_call" | custom-call | flops 3221225472 | bytes 4194304 | tf_op jit(solution)/shard_map/far_gradient/pallas_call | solution.py:339
  66.5 1.8 %collective-permute-start.12 = (bf16[64,32,128]{2,1,0:T(8,128)(2,1)S(1)}, bf16[64,32,128]{2,1,0:T(8,128)(2,1)S(1)}, u32[]{:S(2)}, u32[]{:S(2)}) collective-permute-start(bf16[64,32,128]{2,1,0:T(8,128)(2,1)S(1)} %get-tuple-element.45.refs_4_), channel_id=1, source_target_pairs={{0,2},{1,3},{2,0},{3,1},{4,6},{5,7},{6,4},{7,5},{8,10},{9,11},{10,... | collective-permute-start | bytes 1572872 | tf_op jit(solution)/shard_map/ppermute | solution.py:376
  68.3 6.5 %collective-permute-start.18 = (bf16[64,32,128]{2,1,0:T(8,128)(2,1)S(1)}, bf16[64,32,128]{2,1,0:T(8,128)(2,1)S(1)}, u32[]{:S(2)}, u32[]{:S(2)}) collective-permute-start(bf16[64,32,128]{2,1,0:T(8,128)(2,1)S(1)} %get-tuple-element.46), channel_id=1, source_target_pairs={{0,4},{1,5},{2,6},{3,7},{4,0},{5,1},{6,2},{7,3},{8,12},{9,13},{10,... | collective-permute-start | bytes 1572872 | tf_op jit(solution)/shard_map/ppermute | solution.py:376
  74.8 1.3 %collective-permute-start.19 = (bf16[64,32,128]{2,1,0:T(8,128)(2,1)S(1)}, bf16[64,32,128]{2,1,0:T(8,128)(2,1)S(1)}, u32[]{:S(2)}, u32[]{:S(2)}) collective-permute-start(bf16[64,32,128]{2,1,0:T(8,128)(2,1)S(1)} %get-tuple-element.46), channel_id=1, source_target_pairs={{0,6},{1,7},{2,4},{3,5},{4,2},{5,3},{6,0},{7,1},{8,14},{9,15},{10,... | collective-permute-start | bytes 1572872 | tf_op jit(solution)/shard_map/ppermute | solution.py:376
  76.1 3.0 %collective-permute-start.16 = (bf16[64,32,128]{2,1,0:T(8,128)(2,1)S(1)}, bf16[64,32,128]{2,1,0:T(8,128)(2,1)S(1)}, u32[]{:S(2)}, u32[]{:S(2)}) collective-permute-start(bf16[64,32,128]{2,1,0:T(8,128)(2,1)S(1)} %get-tuple-element.45.refs_4_), channel_id=1, source_target_pairs={{0,1},{1,0},{2,3},{3,2},{4,5},{5,4},{6,7},{7,6},{8,9},{9,8},{10,11... | collective-permute-start | bytes 1572872 | tf_op jit(solution)/shard_map/ppermute | solution.py:376
  79.0 0.5 collective-permute-done.12.refs_5_
  79.6 1.2 %collective-permute-start.13 = (bf16[64,32,128]{2,1,0:T(8,128)(2,1)S(1)}, bf16[64,32,128]{2,1,0:T(8,128)(2,1)S(1)}, u32[]{:S(2)}, u32[]{:S(2)}) collective-permute-start(bf16[64,32,128]{2,1,0:T(8,128)(2,1)S(1)} %collective-permute-done.12.refs_5_), channel_id=1, source_target_pairs={{0,8},{1,9},{2,10},{3,11},{4,124},{5,125},{6,126},{7,127},{8,16},{... | collective-permute-start | bytes 1572872 | tf_op jit(solution)/shard_map/ppermute | solution.py:376
  80.8 2.7 %collective-permute-done.11.refs_0_ = bf16[64,32,128]{2,1,0:T(8,128)(2,1)S(1)} collective-permute-done((bf16[64,32,128]{2,1,0:T(8,128)(2,1)S(1)}, bf16[64,32,128]{2,1,0:T(8,128)(2,1)S(1)}, u32[]{:S(2)}, u32[]{:S(2)}) %collective-permute-start.11) | collective-permute-done | bytes 524320 | tf_op jit(solution)/shard_map/ppermute | solution.py:376
  83.5 2.5 %collective-permute-start.17 = (bf16[64,32,128]{2,1,0:T(8,128)(2,1)S(1)}, bf16[64,32,128]{2,1,0:T(8,128)(2,1)S(1)}, u32[]{:S(2)}, u32[]{:S(2)}) collective-permute-start(bf16[64,32,128]{2,1,0:T(8,128)(2,1)S(1)} %collective-permute-done.12.refs_5_), channel_id=1, source_target_pairs={{0,1},{1,0},{2,3},{3,2},{4,5},{5,4},{6,7},{7,6},{8,9},{9,8},{10,11... | collective-permute-start | bytes 1572872 | tf_op jit(solution)/shard_map/ppermute | solution.py:376
  86.0 9.6 %collective-permute-done.18.refs_8_ = bf16[64,32,128]{2,1,0:T(8,128)(2,1)S(1)} collective-permute-done((bf16[64,32,128]{2,1,0:T(8,128)(2,1)S(1)}, bf16[64,32,128]{2,1,0:T(8,128)(2,1)S(1)}, u32[]{:S(2)}, u32[]{:S(2)}) %collective-permute-start.18) | collective-permute-done | bytes 524320 | tf_op jit(solution)/shard_map/ppermute | solution.py:376
  95.6 3.3 %collective-permute-start.14 = (bf16[64,32,128]{2,1,0:T(8,128)(2,1)S(1)}, bf16[64,32,128]{2,1,0:T(8,128)(2,1)S(1)}, u32[]{:S(2)}, u32[]{:S(2)}) collective-permute-start(bf16[64,32,128]{2,1,0:T(8,128)(2,1)S(1)} %collective-permute-done.11.refs_0_), channel_id=1, source_target_pairs={{0,1},{1,0},{2,3},{3,2},{4,5},{5,4},{6,7},{7,6},{8,9},{9,8},{10,11... | collective-permute-start | bytes 1572872 | tf_op jit(solution)/shard_map/ppermute | solution.py:376
  99.7 0.8 collective-permute-done.14.refs_2_
  100.5 0.7 collective-permute-done.20.refs_10_
  101.2 0.7 collective-permute-done.21.refs_11_
  102.0 0.7 collective-permute-done.15.refs_3_
  102.7 8.4 %backward_gradient.1 = bf16[2,256,64,128]{3,2,1,0:T(8,128)(2,1)} custom-call(bf16[512,384]{1,0:T(8,128)(2,1)S(1)} %turned.1.coef_ref, f32[384,128]{1,0:T(8,128)S(1)} %get-tuple-element.29.low_ref, f32[384,128]{1,0:T(8,128)S(1)} %get-tuple-element.30.high_ref, bf16[64,32,128]{2,1,0:T(8,128)(2,1)S(1)} %collective-permute-done.11.refs_0_, ...), custom_call_target="tpu_custom_call" | custom-call | flops 3221225472 | bytes 14680064 | tf_op jit(solution)/shard_map/backward_gradient/pallas_call | solution.py:257
  (35 shorter events, 2.4 us)
Async XLA Ops:
  1.4 22.1 %collective-permute-start.2 = (bf16[16,128,128]{2,1,0:T(8,128)(2,1)S(1)}, bf16[16,128,128]{2,1,0:T(8,128)(2,1)S(1)}, u32[]{:S(2)}, u32[]{:S(2)}) collective-permute-start(bf16[16,128,128]{2,1,0:T(8,128)(2,1)S(1)} %dynamic-slice_convert_fusion.amp_ref), channel_id=1, source_target_pairs={{4,12},{5,13},{6,14},{7,15},{12,20},{13,21},{14,22},{15,23},{20,28... | collective-permute-start | bytes 1572872 | tf_op jit(solution)/shard_map/ppermute | solution.py:406
  3.6 13.7 %copy-start = (s32[2,256]{1,0:T(2,128)S(1)}, s32[2,256]{1,0:T(2,128)}, u32[]{:S(2)}) copy-start(s32[2,256]{1,0:T(2,128)} %freq_ref.1) | copy-start | bytes 6148
  3.6 13.7 %copy-start.1 = (f32[2,256]{1,0:T(2,128)S(1)}, f32[2,256]{1,0:T(2,128)}, u32[]{:S(2)}) copy-start(f32[2,256]{1,0:T(2,128)} %amp_ref.1) | copy-start | bytes 6148
  3.6 13.6 %collective-permute-start = (s32[3,64]{1,0:T(4,128)S(1)}, s32[3,64]{1,0:T(4,128)S(1)}, u32[]{:S(2)}, u32[]{:S(2)}) collective-permute-start(s32[3,64]{1,0:T(4,128)S(1)} %add_add_fusion.here_ref), channel_id=1, source_target_pairs={{0,4},{1,5},{2,6},{3,7},{4,8},{5,9},{6,10},{7,11},{8,12},{9,13},{1... | collective-permute-start | bytes 2312 | tf_op jit(solution)/shard_map/ppermute | solution.py:376
  8.5 8.7 %collective-permute-start.1 = (s32[3,64]{1,0:T(4,128)S(1)}, s32[3,64]{1,0:T(4,128)S(1)}, u32[]{:S(2)}, u32[]{:S(2)}) collective-permute-start(s32[3,64]{1,0:T(4,128)S(1)} %add_add_fusion.here_ref), channel_id=1, source_target_pairs={{0,8},{1,9},{2,10},{3,11},{4,12},{5,13},{6,14},{7,15},{8,16},{9,17... | collective-permute-start | bytes 2312 | tf_op jit(solution)/shard_map/ppermute | solution.py:376
  18.8 41.7 %copy-start.2 = (bf16[4,256,256]{2,1,0:T(8,128)(2,1)S(1)}, bf16[4,256,256]{2,1,0:T(8,128)(2,1)}, u32[]{:S(2)}) copy-start(bf16[4,256,256]{2,1,0:T(8,128)(2,1)} %constant.46.clone.table_ref) | copy-start | bytes 1572868
  23.5 3.9 %collective-permute-start.4 = (bf16[64,64,128]{2,1,0:T(8,128)(2,1)S(1)}, bf16[64,64,128]{2,1,0:T(8,128)(2,1)S(1)}, u32[]{:S(2)}, u32[]{:S(2)}) collective-permute-start(bf16[64,64,128]{2,1,0:T(8,128)(2,1)S(1)} %get-tuple-element.40), channel_id=1, source_target_pairs={{0,1},{1,0},{2,3},{3,2},{4,5},{5,4},{6,7},{7,6},{8,9},{9,8},{10,11... | collective-permute-start | bytes 3145736 | tf_op jit(solution)/shard_map/ppermute | solution.py:376
  25.1 5.8 %collective-permute-start.8 = (bf16[64,64,128]{2,1,0:T(8,128)(2,1)S(1)}, bf16[64,64,128]{2,1,0:T(8,128)(2,1)S(1)}, u32[]{:S(2)}, u32[]{:S(2)}) collective-permute-start(bf16[64,64,128]{2,1,0:T(8,128)(2,1)S(1)} %get-tuple-element.44), channel_id=1, source_target_pairs={{0,1},{1,0},{2,3},{3,2},{4,5},{5,4},{6,7},{7,6},{8,9},{9,8},{10,11... | collective-permute-start | bytes 3145736 | tf_op jit(solution)/shard_map/ppermute | solution.py:376
  25.2 16.6 %collective-permute-start.3 = (bf16[64,64,128]{2,1,0:T(8,128)(2,1)S(1)}, bf16[64,64,128]{2,1,0:T(8,128)(2,1)S(1)}, u32[]{:S(2)}, u32[]{:S(2)}) collective-permute-start(bf16[64,64,128]{2,1,0:T(8,128)(2,1)S(1)} %get-tuple-element.38), channel_id=1, source_target_pairs={{0,1},{1,0},{2,3},{3,2},{4,5},{5,4},{6,7},{7,6},{8,9},{9,8},{10,11... | collective-permute-start | bytes 3145736 | tf_op jit(solution)/shard_map/ppermute | solution.py:376
  27.7 14.2 %collective-permute-start.5 = (bf16[64,32,128]{2,1,0:T(8,128)(2,1)S(1)}, bf16[64,32,128]{2,1,0:T(8,128)(2,1)S(1)}, u32[]{:S(2)}, u32[]{:S(2)}) collective-permute-start(bf16[64,32,128]{2,1,0:T(8,128)(2,1)S(1)} %get-tuple-element.49), channel_id=1, source_target_pairs={{0,120},{1,121},{2,122},{3,123},{4,12},{5,13},{6,14},{7,15},{8,0},... | collective-permute-start | bytes 1572872 | tf_op jit(solution)/shard_map/ppermute | solution.py:376
  31.2 19.1 %collective-permute-start.10 = (bf16[64,32,128]{2,1,0:T(8,128)(2,1)S(1)}, bf16[64,32,128]{2,1,0:T(8,128)(2,1)S(1)}, u32[]{:S(2)}, u32[]{:S(2)}) collective-permute-start(bf16[64,32,128]{2,1,0:T(8,128)(2,1)S(1)} %get-tuple-element.47), channel_id=1, source_target_pairs={{0,6},{1,7},{2,4},{3,5},{4,2},{5,3},{6,0},{7,1},{8,14},{9,15},{10,... | collective-permute-start | bytes 1572872 | tf_op jit(solution)/shard_map/ppermute | solution.py:376
  36.2 14.0 %collective-permute-start.9 = (bf16[64,32,128]{2,1,0:T(8,128)(2,1)S(1)}, bf16[64,32,128]{2,1,0:T(8,128)(2,1)S(1)}, u32[]{:S(2)}, u32[]{:S(2)}) collective-permute-start(bf16[64,32,128]{2,1,0:T(8,128)(2,1)S(1)} %get-tuple-element.48), channel_id=1, source_target_pairs={{0,4},{1,5},{2,6},{3,7},{4,0},{5,1},{6,2},{7,3},{8,12},{9,13},{10,... | collective-permute-start | bytes 1572872 | tf_op jit(solution)/shard_map/ppermute | solution.py:376
  42.2 18.2 %collective-permute-start.7 = (bf16[64,32,128]{2,1,0:T(8,128)(2,1)S(1)}, bf16[64,32,128]{2,1,0:T(8,128)(2,1)S(1)}, u32[]{:S(2)}, u32[]{:S(2)}) collective-permute-start(bf16[64,32,128]{2,1,0:T(8,128)(2,1)S(1)} %select_convert_fusion), channel_id=1, source_target_pairs={{0,2},{1,3},{2,0},{3,1},{4,6},{5,7},{6,4},{7,5},{8,10},{9,11},{10,... | collective-permute-start | bytes 1572872 | tf_op jit(solution)/shard_map/ppermute | solution.py:376
  44.7 15.7 %collective-permute-start.6 = (bf16[64,32,128]{2,1,0:T(8,128)(2,1)S(1)}, bf16[64,32,128]{2,1,0:T(8,128)(2,1)S(1)}, u32[]{:S(2)}, u32[]{:S(2)}) collective-permute-start(bf16[64,32,128]{2,1,0:T(8,128)(2,1)S(1)} %get-tuple-element.41), channel_id=1, source_target_pairs={{0,120},{1,121},{2,122},{3,123},{4,12},{5,13},{6,14},{7,15},{8,0},... | collective-permute-start | bytes 1572872 | tf_op jit(solution)/shard_map/ppermute | solution.py:376
  66.5 13.0 %collective-permute-start.12 = (bf16[64,32,128]{2,1,0:T(8,128)(2,1)S(1)}, bf16[64,32,128]{2,1,0:T(8,128)(2,1)S(1)}, u32[]{:S(2)}, u32[]{:S(2)}) collective-permute-start(bf16[64,32,128]{2,1,0:T(8,128)(2,1)S(1)} %get-tuple-element.45.refs_4_), channel_id=1, source_target_pairs={{0,2},{1,3},{2,0},{3,1},{4,6},{5,7},{6,4},{7,5},{8,10},{9,11},{10,... | collective-permute-start | bytes 1572872 | tf_op jit(solution)/shard_map/ppermute | solution.py:376
  68.3 15.2 %collective-permute-start.11 = (bf16[64,32,128]{2,1,0:T(8,128)(2,1)S(1)}, bf16[64,32,128]{2,1,0:T(8,128)(2,1)S(1)}, u32[]{:S(2)}, u32[]{:S(2)}) collective-permute-start(bf16[64,32,128]{2,1,0:T(8,128)(2,1)S(1)} %get-tuple-element.45.refs_4_), channel_id=1, source_target_pairs={{0,8},{1,9},{2,10},{3,11},{4,124},{5,125},{6,126},{7,127},{8,16},{... | collective-permute-start | bytes 1572872 | tf_op jit(solution)/shard_map/ppermute | solution.py:376
  68.3 27.3 %collective-permute-start.18 = (bf16[64,32,128]{2,1,0:T(8,128)(2,1)S(1)}, bf16[64,32,128]{2,1,0:T(8,128)(2,1)S(1)}, u32[]{:S(2)}, u32[]{:S(2)}) collective-permute-start(bf16[64,32,128]{2,1,0:T(8,128)(2,1)S(1)} %get-tuple-element.46), channel_id=1, source_target_pairs={{0,4},{1,5},{2,6},{3,7},{4,0},{5,1},{6,2},{7,3},{8,12},{9,13},{10,... | collective-permute-start | bytes 1572872 | tf_op jit(solution)/shard_map/ppermute | solution.py:376
  74.8 24.2 %collective-permute-start.19 = (bf16[64,32,128]{2,1,0:T(8,128)(2,1)S(1)}, bf16[64,32,128]{2,1,0:T(8,128)(2,1)S(1)}, u32[]{:S(2)}, u32[]{:S(2)}) collective-permute-start(bf16[64,32,128]{2,1,0:T(8,128)(2,1)S(1)} %get-tuple-element.46), channel_id=1, source_target_pairs={{0,6},{1,7},{2,4},{3,5},{4,2},{5,3},{6,0},{7,1},{8,14},{9,15},{10,... | collective-permute-start | bytes 1572872 | tf_op jit(solution)/shard_map/ppermute | solution.py:376
  76.1 22.9 %collective-permute-start.16 = (bf16[64,32,128]{2,1,0:T(8,128)(2,1)S(1)}, bf16[64,32,128]{2,1,0:T(8,128)(2,1)S(1)}, u32[]{:S(2)}, u32[]{:S(2)}) collective-permute-start(bf16[64,32,128]{2,1,0:T(8,128)(2,1)S(1)} %get-tuple-element.45.refs_4_), channel_id=1, source_target_pairs={{0,1},{1,0},{2,3},{3,2},{4,5},{5,4},{6,7},{7,6},{8,9},{9,8},{10,11... | collective-permute-start | bytes 1572872 | tf_op jit(solution)/shard_map/ppermute | solution.py:376
  79.6 19.9 %collective-permute-start.13 = (bf16[64,32,128]{2,1,0:T(8,128)(2,1)S(1)}, bf16[64,32,128]{2,1,0:T(8,128)(2,1)S(1)}, u32[]{:S(2)}, u32[]{:S(2)}) collective-permute-start(bf16[64,32,128]{2,1,0:T(8,128)(2,1)S(1)} %collective-permute-done.12.refs_5_), channel_id=1, source_target_pairs={{0,8},{1,9},{2,10},{3,11},{4,124},{5,125},{6,126},{7,127},{8,16},{... | collective-permute-start | bytes 1572872 | tf_op jit(solution)/shard_map/ppermute | solution.py:376
  83.5 17.0 %collective-permute-start.17 = (bf16[64,32,128]{2,1,0:T(8,128)(2,1)S(1)}, bf16[64,32,128]{2,1,0:T(8,128)(2,1)S(1)}, u32[]{:S(2)}, u32[]{:S(2)}) collective-permute-start(bf16[64,32,128]{2,1,0:T(8,128)(2,1)S(1)} %collective-permute-done.12.refs_5_), channel_id=1, source_target_pairs={{0,1},{1,0},{2,3},{3,2},{4,5},{5,4},{6,7},{7,6},{8,9},{9,8},{10,11... | collective-permute-start | bytes 1572872 | tf_op jit(solution)/shard_map/ppermute | solution.py:376
  95.6 4.9 %collective-permute-start.14 = (bf16[64,32,128]{2,1,0:T(8,128)(2,1)S(1)}, bf16[64,32,128]{2,1,0:T(8,128)(2,1)S(1)}, u32[]{:S(2)}, u32[]{:S(2)}) collective-permute-start(bf16[64,32,128]{2,1,0:T(8,128)(2,1)S(1)} %collective-permute-done.11.refs_0_), channel_id=1, source_target_pairs={{0,1},{1,0},{2,3},{3,2},{4,5},{5,4},{6,7},{7,6},{8,9},{9,8},{10,11... | collective-permute-start | bytes 1572872 | tf_op jit(solution)/shard_map/ppermute | solution.py:376
  98.9 2.3 %collective-permute-start.20 = (bf16[64,32,128]{2,1,0:T(8,128)(2,1)S(1)}, bf16[64,32,128]{2,1,0:T(8,128)(2,1)S(1)}, u32[]{:S(2)}, u32[]{:S(2)}) collective-permute-start(bf16[64,32,128]{2,1,0:T(8,128)(2,1)S(1)} %collective-permute-done.18.refs_8_), channel_id=1, source_target_pairs={{0,1},{1,0},{2,3},{3,2},{4,5},{5,4},{6,7},{7,6},{8,9},{9,8},{10,11... | collective-permute-start | bytes 1572872 | tf_op jit(solution)/shard_map/ppermute | solution.py:376
  99.0 3.0 %collective-permute-start.21 = (bf16[64,32,128]{2,1,0:T(8,128)(2,1)S(1)}, bf16[64,32,128]{2,1,0:T(8,128)(2,1)S(1)}, u32[]{:S(2)}, u32[]{:S(2)}) collective-permute-start(bf16[64,32,128]{2,1,0:T(8,128)(2,1)S(1)} %collective-permute-done.19.refs_9_), channel_id=1, source_target_pairs={{0,1},{1,0},{2,3},{3,2},{4,5},{5,4},{6,7},{7,6},{8,9},{9,8},{10,11... | collective-permute-start | bytes 1572872 | tf_op jit(solution)/shard_map/ppermute | solution.py:376
  99.5 3.3 %collective-permute-start.15 = (bf16[64,32,128]{2,1,0:T(8,128)(2,1)S(1)}, bf16[64,32,128]{2,1,0:T(8,128)(2,1)S(1)}, u32[]{:S(2)}, u32[]{:S(2)}) collective-permute-start(bf16[64,32,128]{2,1,0:T(8,128)(2,1)S(1)} %collective-permute-done.13.refs_1_), channel_id=1, source_target_pairs={{0,1},{1,0},{2,3},{3,2},{4,5},{5,4},{6,7},{7,6},{8,9},{9,8},{10,11... | collective-permute-start | bytes 1572872 | tf_op jit(solution)/shard_map/ppermute | solution.py:376

commit v5 on v4

--- a/solution.py
+++ b/solution.py
@@ -273,7 +273,7 @@
 
 def far_kernel(
     table_ref, amp_ref, moved_ref, odd_ref, live_ref, low_ref, high_ref, mine_ref, got_ref,
-    rem_own_ref, a_got_ref, near_ref, cross_ref, ga_ref, gb_ref, mid, back,
+    rem_own_ref, top_got_ref, end_got_ref, near_ref, cross_ref, ga_ref, gb_ref, mid, back,
 ):
     half, both, window = near_ref.shape
     count = both // 2
@@ -282,7 +282,8 @@
     own = mine_ref[...].astype(F32) + got_ref[...].astype(F32)
     row = lax.broadcasted_iota(jnp.int32, own.shape, 0).astype(F32)
     inside = jnp.logical_and(low_ref[...][None] <= row, row < high_ref[...][None])
-    own = jnp.where(inside, own, rem_own_ref[...].astype(F32)) + a_got_ref[...].astype(F32)
+    got_a = jnp.concatenate([top_got_ref[...], end_got_ref[...]], axis=0)
+    own = jnp.where(inside, own, rem_own_ref[...].astype(F32)) + got_a.astype(F32)
     middle = near_ref[...].astype(F32) + cross_ref[...].astype(F32)
     for first, total in ((0, own), (half, middle)):
         rows = total.shape[0]
@@ -313,7 +314,7 @@
             back[first + p] = pair
         return carry
 
-    lax.fori_loop(0, count // 2, one_pair, 0, unroll=2)
+    lax.fori_loop(0, count // 2, one_pair, 0, unroll=8)
     live = live_ref[...][:, None, :1]
     for first, g_ref in ((0, ga_ref), (half, gb_ref)):
         rows = back[:, first : first + half, :]
@@ -421,25 +422,36 @@
     )
     other_rem, moved_amp = lax.optimization_barrier((other_rem, moved_amp))
     got_rem = to_core(other_rem)
-    rem_other = to_owner(joined(mine_rem[:, unit:], got_rem[:, unit:]).astype(BF16))
+    part = strip_rows // 2
+    halves = (slice(0, part), slice(part, strip_rows))
+    rem_other = [
+        to_owner(joined(mine_rem[half, unit:], got_rem[half, unit:]).astype(BF16)) for half in halves
+    ]
     got_mid = to_core(other_mid)
     near_mid = to_near(joined(mine_mid[:, :unit], got_mid[:, :unit]).astype(BF16))
     cross_mid = to_cross(joined(mine_mid[:, unit:], got_mid[:, unit:]).astype(BF16))
     got_loc = to_core(other_loc)
     rem_own = joined(mine_rem[:, :unit], got_rem[:, :unit]).astype(BF16)
-    rem_own, rem_other = lax.optimization_barrier((rem_own, rem_other))
+    rem_own, rem_other[1] = lax.optimization_barrier((rem_own, rem_other[1]))
     rem_own = to_owner(rem_own)
     far_rows = slice(tile_rows + unit, tile_rows + 2 * unit)
-    y_index = jnp.arange(strip_rows).astype(F32)[:, None, None]
-    inside = jnp.logical_and(low[None, far_rows] <= y_index, y_index < high[None, far_rows])
-    sent = jnp.where(inside, joined(mine_loc[:, unit:], got_loc[:, unit:]), rem_other.astype(F32))
-    got_a = to_hi(sent.astype(BF16))
+    local = got_loc
+    got_a = []
+    for half, rem_half in zip(halves, rem_other):
+        if got_a:
+            local, got_a[0] = lax.optimization_barrier((local, got_a[0]))
+        y_index = jnp.arange(half.start, half.stop).astype(F32)[:, None, None]
+        inside = jnp.logical_and(low[None, far_rows] <= y_index, y_index < high[None, far_rows])
+        sent = jnp.where(
+            inside, joined(mine_loc[half, unit:], local[half, unit:]), rem_half.astype(F32)
+        )
+        got_a.append(to_hi(sent.astype(BF16)))
     coef_t = turned(coefs)
 
     tables = jnp.asarray(dft_matrices(window))
     grad_a, grad_b = far_gradient(
         tables, own_amp, moved_amp, odd_row, live,
-        low, high, (mine_loc, got_loc, rem_own, got_a, near_mid, cross_mid),
+        low, high, (mine_loc, got_loc, rem_own, *got_a, near_mid, cross_mid),
     )
 
     a_hi = to_hi(grad_a)

time: 111 us -> 109 us (0.982)
  waiting for transfers between devices: 33.5 us -> 31.5 us
  Pallas kernels: 28 us -> 26.2 us
    ppermute x21 -> x23, waiting for transfers between devices: 33.5 us -> 31.5 us  [send(): return lax.ppermute(value, AXES, permutation(scan_size, target))]
    pallas_call x1, Pallas kernels: 6.11 us -> 4.31 us  [far_gradient(): pl.pallas_call(far_kernel, grid=(1,), in_specs=[whole(value) for value in...]
    ppermute x21 -> x23, starting transfers between devices: 45 us -> 46.1 us  [send(): return lax.ppermute(value, AXES, permutation(scan_size, target))]
  transfers between devices with their start and end apart: 22 -> 24, of which waited for: 10 -> 8; matrix products, arithmetic and copies ran while one was open for 2% -> 2% of each run, Pallas kernels for 12% -> 12%
where the time goes in v5:
time: 109 us
  starting transfers between devices  46.7 us (43%)
  waiting for transfers between devices  31.5 us (29%)
  Pallas kernels  26.2 us (24%)
  other arithmetic  1.8 us (2%)
  local copies, waits for them, and re-layouts  1.49 us (1%)
    ppermute x23, starting transfers between devices, send(): return lax.ppermute(value, AXES, permutation(scan_size, target))  46.1 us
    ppermute x23, waiting for transfers between devices, send(): return lax.ppermute(value, AXES, permutation(scan_size, target))  31.5 us
    pallas_call x1, Pallas kernels, backward_gradient(): pl.pallas_call(backward_kernel, grid=(strip_rows // Y_BLOCK,), in_specs=[...  8.45 us
    pallas_call x1, Pallas kernels, rows_first(): pl.pallas_call(transpose_kernel, grid=(strip_rows // Y_BLOCK, parts), in_...  7.08 us
    pallas_call x1, Pallas kernels, forward_waves(): pl.pallas_call(forward_kernel, grid=(strip_rows // block,), in_specs=[pl....  4.72 us
    pallas_call x1, Pallas kernels, far_gradient(): pl.pallas_call(far_kernel, grid=(1,), in_specs=[whole(value) for value in...  4.31 us
  transfers between devices with their start and end apart: 24, of which 8 were waited for; matrix products, arithmetic and copies ran while one was open for 2% of the time, Pallas kernels for 12%

profile of v5, /device:TPU:1, one launch (start us, length us, event | category | flops | bytes accessed | tf_op | source)
XLA Modules:
  0.0 108.6 jit_solution(6605417939262477969)
XLA Ops:
  0.0 1.3 %dynamic-slice_convert_fusion.amp_ref = bf16[16,128,128]{2,1,0:T(8,128)(2,1)S(1)} fusion(f32[64,128,128]{2,1,0:T(8,128)} %param.14, s32[]{:T(128)S(6)} %select_n.28), kind=kLoop, calls=%fused_computation.3 | loop fusion | bytes 1048580 | tf_op jit(solution)/shard_map/convert_element_type | solution.py:405
  1.4 0.7 collective-permute-start.2
  2.8 0.7 add_add_fusion.here_ref
  3.6 4.9 %collective-permute-start = (s32[3,64]{1,0:T(4,128)S(1)}, s32[3,64]{1,0:T(4,128)S(1)}, u32[]{:S(2)}, u32[]{:S(2)}) collective-permute-start(s32[3,64]{1,0:T(4,128)S(1)} %add_add_fusion.here_ref), channel_id=1, source_target_pairs={{0,4},{1,5},{2,6},{3,7},{4,8},{5,9},{6,10},{7,11},{8,12},{9,13},{1... | collective-permute-start | bytes 2312 | tf_op jit(solution)/shard_map/ppermute | solution.py:377
  8.5 1.6 %collective-permute-start.1 = (s32[3,64]{1,0:T(4,128)S(1)}, s32[3,64]{1,0:T(4,128)S(1)}, u32[]{:S(2)}, u32[]{:S(2)}) collective-permute-start(s32[3,64]{1,0:T(4,128)S(1)} %add_add_fusion.here_ref), channel_id=1, source_target_pairs={{0,8},{1,9},{2,10},{3,11},{4,12},{5,13},{6,14},{7,15},{8,16},{9,17... | collective-permute-start | bytes 2312 | tf_op jit(solution)/shard_map/ppermute | solution.py:377
  10.1 7.1 %rows_first.1.field_ref = bf16[64,512,128]{2,1,0:T(8,128)(2,1)S(1)} custom-call(bf16[2,256,64,128]{3,2,1,0:T(8,128)(2,1)} %refs_3_, bf16[2,256,64,128]{3,2,1,0:T(8,128)(2,1)} %refs_3_, bf16[2,256,64,128]{3,2,1,0:T(8,128)(2,1)} %refs_3_, bf16[2,256,64,128]{3,2,1,0:T(8,128)(2,1)} %refs_3_), custom_call_target="tpu_custom_call" | custom-call | bytes 16777216 | tf_op jit(solution)/shard_map/rows_first/pallas_call | solution.py:158
  17.3 1.5 %coefficients.1 = (bf16[128,512]{1,0:T(8,128)(2,1)S(1)}, bf16[256,512]{1,0:T(8,128)(2,1)S(1)}, f32[384,128]{1,0:T(8,128)S(1)}, f32[384,128]{1,0:T(8,128)S(1)}, f32[16,128]{1,0:T(8,128)S(1)}) custom-call(s32[5]{0:T(128)S(1)} %stack.28.where_ref, s32[3,64]{1,0:T(4,128)S(1)} %add_add_fusion.here_ref, s32[3,64]{1,0:T(4,128)S(1)} %collective-permute-done.before_1_ref, ...), custom_call_target="tpu_custom_call" | custom-call | tf_op jit(solution)/shard_map/coefficients/pallas_call | solution.py:98
  18.8 4.7 %forward_waves.1 = (bf16[64,64,128]{2,1,0:T(8,128)(2,1)S(1)}, bf16[64,64,128]{2,1,0:T(8,128)(2,1)S(1)}, bf16[64,64,128]{2,1,0:T(8,128)(2,1)S(1)}, bf16[64,64,128...) custom-call(bf16[128,512]{1,0:T(8,128)(2,1)S(1)} %get-tuple-element.29.rem_ref, ...), custom_call_target="tpu_custom_call" | custom-call | flops 3221225472 | bytes 14680064 | tf_op jit(solution)/shard_map/forward_waves/pallas_call | solution.py:194
  23.5 1.6 %collective-permute-start.4 = (bf16[64,64,128]{2,1,0:T(8,128)(2,1)S(1)}, bf16[64,64,128]{2,1,0:T(8,128)(2,1)S(1)}, u32[]{:S(2)}, u32[]{:S(2)}) collective-permute-start(bf16[64,64,128]{2,1,0:T(8,128)(2,1)S(1)} %get-tuple-element.42), channel_id=1, source_target_pairs={{0,1},{1,0},{2,3},{3,2},{4,5},{5,4},{6,7},{7,6},{8,9},{9,8},{10,11... | collective-permute-start | bytes 3145736 | tf_op jit(solution)/shard_map/ppermute | solution.py:377
  25.6 1.8 %collective-permute-done.4 = bf16[64,64,128]{2,1,0:T(8,128)(2,1)S(1)} collective-permute-done((bf16[64,64,128]{2,1,0:T(8,128)(2,1)S(1)}, bf16[64,64,128]{2,1,0:T(8,128)(2,1)S(1)}, u32[]{:S(2)}, u32[]{:S(2)}) %collective-permute-start.4) | collective-permute-done | bytes 1048608 | tf_op jit(solution)/shard_map/ppermute | solution.py:377
  27.6 3.2 %collective-permute-start.7 = (bf16[32,32,128]{2,1,0:T(8,128)(2,1)S(1)}, bf16[32,32,128]{2,1,0:T(8,128)(2,1)S(1)}, u32[]{:S(2)}, u32[]{:S(2)}) collective-permute-start(bf16[32,32,128]{2,1,0:T(8,128)(2,1)S(1)} %get-tuple-element.53), channel_id=1, source_target_pairs={{0,120},{1,121},{2,122},{3,123},{4,12},{5,13},{6,14},{7,15},{8,0},... | collective-permute-start | bytes 786440 | tf_op jit(solution)/shard_map/ppermute | solution.py:377
  31.1 3.9 %collective-permute-start.11 = (bf16[64,32,128]{2,1,0:T(8,128)(2,1)S(1)}, bf16[64,32,128]{2,1,0:T(8,128)(2,1)S(1)}, u32[]{:S(2)}, u32[]{:S(2)}) collective-permute-start(bf16[64,32,128]{2,1,0:T(8,128)(2,1)S(1)} %get-tuple-element.52), channel_id=1, source_target_pairs={{0,4},{1,5},{2,6},{3,7},{4,0},{5,1},{6,2},{7,3},{8,12},{9,13},{10,... | collective-permute-start | bytes 1572872 | tf_op jit(solution)/shard_map/ppermute | solution.py:377
  35.0 1.4 %collective-permute-start.12 = (bf16[64,32,128]{2,1,0:T(8,128)(2,1)S(1)}, bf16[64,32,128]{2,1,0:T(8,128)(2,1)S(1)}, u32[]{:S(2)}, u32[]{:S(2)}) collective-permute-start(bf16[64,32,128]{2,1,0:T(8,128)(2,1)S(1)} %get-tuple-element.51), channel_id=1, source_target_pairs={{0,6},{1,7},{2,4},{3,5},{4,2},{5,3},{6,0},{7,1},{8,14},{9,15},{10,... | collective-permute-start | bytes 1572872 | tf_op jit(solution)/shard_map/ppermute | solution.py:377
  36.3 3.5 %collective-permute-start.5 = (bf16[32,32,128]{2,1,0:T(8,128)(2,1)S(1)}, bf16[32,32,128]{2,1,0:T(8,128)(2,1)S(1)}, u32[]{:S(2)}, u32[]{:S(2)}) collective-permute-start(bf16[32,32,128]{2,1,0:T(8,128)(2,1)S(1)} %get-tuple-element.54), channel_id=1, source_target_pairs={{0,120},{1,121},{2,122},{3,123},{4,12},{5,13},{6,14},{7,15},{8,0},... | collective-permute-start | bytes 786440 | tf_op jit(solution)/shard_map/ppermute | solution.py:377
  40.1 1.2 %collective-permute-start.8 = (bf16[32,32,128]{2,1,0:T(8,128)(2,1)S(1)}, bf16[32,32,128]{2,1,0:T(8,128)(2,1)S(1)}, u32[]{:S(2)}, u32[]{:S(2)}) collective-permute-start(bf16[32,32,128]{2,1,0:T(8,128)(2,1)S(1)} %select_convert_fusion.1), channel_id=1, source_target_pairs={{0,2},{1,3},{2,0},{3,1},{4,6},{5,7},{6,4},{7,5},{8,10},{9,11},{10,... | collective-permute-start | bytes 786440 | tf_op jit(solution)/shard_map/ppermute | solution.py:377
  41.4 3.1 %collective-permute-done.5 = bf16[32,32,128]{2,1,0:T(8,128)(2,1)S(1)} collective-permute-done((bf16[32,32,128]{2,1,0:T(8,128)(2,1)S(1)}, bf16[32,32,128]{2,1,0:T(8,128)(2,1)S(1)}, u32[]{:S(2)}, u32[]{:S(2)}) %collective-permute-start.5) | collective-permute-done | bytes 262176 | tf_op jit(solution)/shard_map/ppermute | solution.py:377
  44.5 5.5 %collective-permute-start.6 = (bf16[64,32,128]{2,1,0:T(8,128)(2,1)S(1)}, bf16[64,32,128]{2,1,0:T(8,128)(2,1)S(1)}, u32[]{:S(2)}, u32[]{:S(2)}) collective-permute-start(bf16[64,32,128]{2,1,0:T(8,128)(2,1)S(1)} %add_convert_fusion.2), channel_id=1, source_target_pairs={{0,120},{1,121},{2,122},{3,123},{4,12},{5,13},{6,14},{7,15},{8,0},... | collective-permute-start | bytes 1572872 | tf_op jit(solution)/shard_map/ppermute | solution.py:377
  50.1 4.7 %collective-permute-done.8.top_got_ref = bf16[32,32,128]{2,1,0:T(8,128)(2,1)S(1)} collective-permute-done((bf16[32,32,128]{2,1,0:T(8,128)(2,1)S(1)}, bf16[32,32,128]{2,1,0:T(8,128)(2,1)S(1)}, u32[]{:S(2)}, u32[]{:S(2)}) %collective-permute-start.8) | collective-permute-done | bytes 262176 | tf_op jit(solution)/shard_map/ppermute | solution.py:377
  55.6 7.5 %collective-permute-done.9.end_got_ref = bf16[32,32,128]{2,1,0:T(8,128)(2,1)S(1)} collective-permute-done((bf16[32,32,128]{2,1,0:T(8,128)(2,1)S(1)}, bf16[32,32,128]{2,1,0:T(8,128)(2,1)S(1)}, u32[]{:S(2)}, u32[]{:S(2)}) %collective-permute-start.9) | collective-permute-done | bytes 262176 | tf_op jit(solution)/shard_map/ppermute | solution.py:377
  63.1 4.3 %far_gradient.1 = (bf16[64,32,128]{2,1,0:T(8,128)(2,1)S(1)}, bf16[64,32,128]{2,1,0:T(8,128)(2,1)S(1)}) custom-call(bf16[4,256,256]{2,1,0:T(8,128)(2,1)S(1)} %copy-done.2, bf16[16,128,128]{2,1,0:T(8,128)(2,1)S(1)} %dynamic-slice_convert_fusion.amp_ref, bf16[16,128,128]{2,1,0:T(8,128)(2,1)S(1)} %collective-permute-done.2.moved_ref, ...), custom_call_target="tpu_custom_call" | custom-call | flops 3221225472 | bytes 4194304 | tf_op jit(solution)/shard_map/far_gradient/pallas_call | solution.py:340
  67.4 0.6 collective-permute-start.14
  68.0 3.6 %collective-permute-start.20 = (bf16[64,32,128]{2,1,0:T(8,128)(2,1)S(1)}, bf16[64,32,128]{2,1,0:T(8,128)(2,1)S(1)}, u32[]{:S(2)}, u32[]{:S(2)}) collective-permute-start(bf16[64,32,128]{2,1,0:T(8,128)(2,1)S(1)} %get-tuple-element.50), channel_id=1, source_target_pairs={{0,4},{1,5},{2,6},{3,7},{4,0},{5,1},{6,2},{7,3},{8,12},{9,13},{10,... | collective-permute-start | bytes 1572872 | tf_op jit(solution)/shard_map/ppermute | solution.py:377
  71.6 1.2 %collective-permute-start.21 = (bf16[64,32,128]{2,1,0:T(8,128)(2,1)S(1)}, bf16[64,32,128]{2,1,0:T(8,128)(2,1)S(1)}, u32[]{:S(2)}, u32[]{:S(2)}) collective-permute-start(bf16[64,32,128]{2,1,0:T(8,128)(2,1)S(1)} %get-tuple-element.50), channel_id=1, source_target_pairs={{0,6},{1,7},{2,4},{3,5},{4,2},{5,3},{6,0},{7,1},{8,14},{9,15},{10,... | collective-permute-start | bytes 1572872 | tf_op jit(solution)/shard_map/ppermute | solution.py:377
  72.8 3.0 %collective-permute-start.18 = (bf16[64,32,128]{2,1,0:T(8,128)(2,1)S(1)}, bf16[64,32,128]{2,1,0:T(8,128)(2,1)S(1)}, u32[]{:S(2)}, u32[]{:S(2)}) collective-permute-start(bf16[64,32,128]{2,1,0:T(8,128)(2,1)S(1)} %get-tuple-element.49.refs_4_), channel_id=1, source_target_pairs={{0,1},{1,0},{2,3},{3,2},{4,5},{5,4},{6,7},{7,6},{8,9},{9,8},{10,11... | collective-permute-start | bytes 1572872 | tf_op jit(solution)/shard_map/ppermute | solution.py:377
  75.8 4.4 %collective-permute-done.14.refs_5_ = bf16[64,32,128]{2,1,0:T(8,128)(2,1)S(1)} collective-permute-done((bf16[64,32,128]{2,1,0:T(8,128)(2,1)S(1)}, bf16[64,32,128]{2,1,0:T(8,128)(2,1)S(1)}, u32[]{:S(2)}, u32[]{:S(2)}) %collective-permute-start.14) | collective-permute-done | bytes 524320 | tf_op jit(solution)/shard_map/ppermute | solution.py:377
  80.3 2.0 %collective-permute-done.13.refs_0_ = bf16[64,32,128]{2,1,0:T(8,128)(2,1)S(1)} collective-permute-done((bf16[64,32,128]{2,1,0:T(8,128)(2,1)S(1)}, bf16[64,32,128]{2,1,0:T(8,128)(2,1)S(1)}, u32[]{:S(2)}, u32[]{:S(2)}) %collective-permute-start.13) | collective-permute-done | bytes 524320 | tf_op jit(solution)/shard_map/ppermute | solution.py:377
  82.3 3.8 %collective-permute-start.19 = (bf16[64,32,128]{2,1,0:T(8,128)(2,1)S(1)}, bf16[64,32,128]{2,1,0:T(8,128)(2,1)S(1)}, u32[]{:S(2)}, u32[]{:S(2)}) collective-permute-start(bf16[64,32,128]{2,1,0:T(8,128)(2,1)S(1)} %collective-permute-done.14.refs_5_), channel_id=1, source_target_pairs={{0,1},{1,0},{2,3},{3,2},{4,5},{5,4},{6,7},{7,6},{8,9},{9,8},{10,11... | collective-permute-start | bytes 1572872 | tf_op jit(solution)/shard_map/ppermute | solution.py:377
  86.1 6.6 %collective-permute-done.20.refs_8_ = bf16[64,32,128]{2,1,0:T(8,128)(2,1)S(1)} collective-permute-done((bf16[64,32,128]{2,1,0:T(8,128)(2,1)S(1)}, bf16[64,32,128]{2,1,0:T(8,128)(2,1)S(1)}, u32[]{:S(2)}, u32[]{:S(2)}) %collective-permute-start.20) | collective-permute-done | bytes 524320 | tf_op jit(solution)/shard_map/ppermute | solution.py:377
  92.7 3.0 %collective-permute-start.16 = (bf16[64,32,128]{2,1,0:T(8,128)(2,1)S(1)}, bf16[64,32,128]{2,1,0:T(8,128)(2,1)S(1)}, u32[]{:S(2)}, u32[]{:S(2)}) collective-permute-start(bf16[64,32,128]{2,1,0:T(8,128)(2,1)S(1)} %collective-permute-done.13.refs_0_), channel_id=1, source_target_pairs={{0,1},{1,0},{2,3},{3,2},{4,5},{5,4},{6,7},{7,6},{8,9},{9,8},{10,11... | collective-permute-start | bytes 1572872 | tf_op jit(solution)/shard_map/ppermute | solution.py:377
  96.3 2.3 %collective-permute-start.17 = (bf16[64,32,128]{2,1,0:T(8,128)(2,1)S(1)}, bf16[64,32,128]{2,1,0:T(8,128)(2,1)S(1)}, u32[]{:S(2)}, u32[]{:S(2)}) collective-permute-start(bf16[64,32,128]{2,1,0:T(8,128)(2,1)S(1)} %collective-permute-done.15.refs_1_), channel_id=1, source_target_pairs={{0,1},{1,0},{2,3},{3,2},{4,5},{5,4},{6,7},{7,6},{8,9},{9,8},{10,11... | collective-permute-start | bytes 1572872 | tf_op jit(solution)/shard_map/ppermute | solution.py:377
  98.8 1.3 %collective-permute-done.17.refs_3_ = bf16[64,32,128]{2,1,0:T(8,128)(2,1)S(1)} collective-permute-done((bf16[64,32,128]{2,1,0:T(8,128)(2,1)S(1)}, bf16[64,32,128]{2,1,0:T(8,128)(2,1)S(1)}, u32[]{:S(2)}, u32[]{:S(2)}) %collective-permute-start.17) | collective-permute-done | bytes 524320 | tf_op jit(solution)/shard_map/ppermute | solution.py:377
  100.1 8.4 %backward_gradient.1 = bf16[2,256,64,128]{3,2,1,0:T(8,128)(2,1)} custom-call(bf16[512,384]{1,0:T(8,128)(2,1)S(1)} %turned.1.coef_ref, f32[384,128]{1,0:T(8,128)S(1)} %get-tuple-element.31.low_ref, f32[384,128]{1,0:T(8,128)S(1)} %get-tuple-element.32.high_ref, bf16[64,32,128]{2,1,0:T(8,128)(2,1)S(1)} %collective-permute-done.13.refs_0_, ...), custom_call_target="tpu_custom_call" | custom-call | flops 3221225472 | bytes 14680064 | tf_op jit(solution)/shard_map/backward_gradient/pallas_call | solution.py:257
  (42 shorter events, 3.1 us)
Async XLA Ops:
  1.4 22.1 %collective-permute-start.2 = (bf16[16,128,128]{2,1,0:T(8,128)(2,1)S(1)}, bf16[16,128,128]{2,1,0:T(8,128)(2,1)S(1)}, u32[]{:S(2)}, u32[]{:S(2)}) collective-permute-start(bf16[16,128,128]{2,1,0:T(8,128)(2,1)S(1)} %dynamic-slice_convert_fusion.amp_ref), channel_id=1, source_target_pairs={{4,12},{5,13},{6,14},{7,15},{12,20},{13,21},{14,22},{15,23},{20,28... | collective-permute-start | bytes 1572872 | tf_op jit(solution)/shard_map/ppermute | solution.py:407
  3.6 13.7 %copy-start = (s32[2,256]{1,0:T(2,128)S(1)}, s32[2,256]{1,0:T(2,128)}, u32[]{:S(2)}) copy-start(s32[2,256]{1,0:T(2,128)} %freq_ref.1) | copy-start | bytes 6148
  3.6 13.7 %copy-start.1 = (f32[2,256]{1,0:T(2,128)S(1)}, f32[2,256]{1,0:T(2,128)}, u32[]{:S(2)}) copy-start(f32[2,256]{1,0:T(2,128)} %amp_ref.1) | copy-start | bytes 6148
  3.6 13.6 %collective-permute-start = (s32[3,64]{1,0:T(4,128)S(1)}, s32[3,64]{1,0:T(4,128)S(1)}, u32[]{:S(2)}, u32[]{:S(2)}) collective-permute-start(s32[3,64]{1,0:T(4,128)S(1)} %add_add_fusion.here_ref), channel_id=1, source_target_pairs={{0,4},{1,5},{2,6},{3,7},{4,8},{5,9},{6,10},{7,11},{8,12},{9,13},{1... | collective-permute-start | bytes 2312 | tf_op jit(solution)/shard_map/ppermute | solution.py:377
  8.5 8.7 %collective-permute-start.1 = (s32[3,64]{1,0:T(4,128)S(1)}, s32[3,64]{1,0:T(4,128)S(1)}, u32[]{:S(2)}, u32[]{:S(2)}) collective-permute-start(s32[3,64]{1,0:T(4,128)S(1)} %add_add_fusion.here_ref), channel_id=1, source_target_pairs={{0,8},{1,9},{2,10},{3,11},{4,12},{5,13},{6,14},{7,15},{8,16},{9,17... | collective-permute-start | bytes 2312 | tf_op jit(solution)/shard_map/ppermute | solution.py:377
  18.8 44.3 %copy-start.2 = (bf16[4,256,256]{2,1,0:T(8,128)(2,1)S(1)}, bf16[4,256,256]{2,1,0:T(8,128)(2,1)}, u32[]{:S(2)}) copy-start(bf16[4,256,256]{2,1,0:T(8,128)(2,1)} %constant.48.clone.table_ref) | copy-start | bytes 1572868
  23.5 3.9 %collective-permute-start.4 = (bf16[64,64,128]{2,1,0:T(8,128)(2,1)S(1)}, bf16[64,64,128]{2,1,0:T(8,128)(2,1)S(1)}, u32[]{:S(2)}, u32[]{:S(2)}) collective-permute-start(bf16[64,64,128]{2,1,0:T(8,128)(2,1)S(1)} %get-tuple-element.42), channel_id=1, source_target_pairs={{0,1},{1,0},{2,3},{3,2},{4,5},{5,4},{6,7},{7,6},{8,9},{9,8},{10,11... | collective-permute-start | bytes 3145736 | tf_op jit(solution)/shard_map/ppermute | solution.py:377
  25.1 5.7 %collective-permute-start.10 = (bf16[64,64,128]{2,1,0:T(8,128)(2,1)S(1)}, bf16[64,64,128]{2,1,0:T(8,128)(2,1)S(1)}, u32[]{:S(2)}, u32[]{:S(2)}) collective-permute-start(bf16[64,64,128]{2,1,0:T(8,128)(2,1)S(1)} %get-tuple-element.48), channel_id=1, source_target_pairs={{0,1},{1,0},{2,3},{3,2},{4,5},{5,4},{6,7},{7,6},{8,9},{9,8},{10,11... | collective-permute-start | bytes 3145736 | tf_op jit(solution)/shard_map/ppermute | solution.py:377
  25.2 14.7 %collective-permute-start.3 = (bf16[64,64,128]{2,1,0:T(8,128)(2,1)S(1)}, bf16[64,64,128]{2,1,0:T(8,128)(2,1)S(1)}, u32[]{:S(2)}, u32[]{:S(2)}) collective-permute-start(bf16[64,64,128]{2,1,0:T(8,128)(2,1)S(1)} %get-tuple-element.40), channel_id=1, source_target_pairs={{0,1},{1,0},{2,3},{3,2},{4,5},{5,4},{6,7},{7,6},{8,9},{9,8},{10,11... | collective-permute-start | bytes 3145736 | tf_op jit(solution)/shard_map/ppermute | solution.py:377
  27.6 12.3 %collective-permute-start.7 = (bf16[32,32,128]{2,1,0:T(8,128)(2,1)S(1)}, bf16[32,32,128]{2,1,0:T(8,128)(2,1)S(1)}, u32[]{:S(2)}, u32[]{:S(2)}) collective-permute-start(bf16[32,32,128]{2,1,0:T(8,128)(2,1)S(1)} %get-tuple-element.53), channel_id=1, source_target_pairs={{0,120},{1,121},{2,122},{3,123},{4,12},{5,13},{6,14},{7,15},{8,0},... | collective-permute-start | bytes 786440 | tf_op jit(solution)/shard_map/ppermute | solution.py:377
  31.1 24.5 %collective-permute-start.11 = (bf16[64,32,128]{2,1,0:T(8,128)(2,1)S(1)}, bf16[64,32,128]{2,1,0:T(8,128)(2,1)S(1)}, u32[]{:S(2)}, u32[]{:S(2)}) collective-permute-start(bf16[64,32,128]{2,1,0:T(8,128)(2,1)S(1)} %get-tuple-element.52), channel_id=1, source_target_pairs={{0,4},{1,5},{2,6},{3,7},{4,0},{5,1},{6,2},{7,3},{8,12},{9,13},{10,... | collective-permute-start | bytes 1572872 | tf_op jit(solution)/shard_map/ppermute | solution.py:377
  35.0 20.6 %collective-permute-start.12 = (bf16[64,32,128]{2,1,0:T(8,128)(2,1)S(1)}, bf16[64,32,128]{2,1,0:T(8,128)(2,1)S(1)}, u32[]{:S(2)}, u32[]{:S(2)}) collective-permute-start(bf16[64,32,128]{2,1,0:T(8,128)(2,1)S(1)} %get-tuple-element.51), channel_id=1, source_target_pairs={{0,6},{1,7},{2,4},{3,5},{4,2},{5,3},{6,0},{7,1},{8,14},{9,15},{10,... | collective-permute-start | bytes 1572872 | tf_op jit(solution)/shard_map/ppermute | solution.py:377
  36.3 8.2 %collective-permute-start.5 = (bf16[32,32,128]{2,1,0:T(8,128)(2,1)S(1)}, bf16[32,32,128]{2,1,0:T(8,128)(2,1)S(1)}, u32[]{:S(2)}, u32[]{:S(2)}) collective-permute-start(bf16[32,32,128]{2,1,0:T(8,128)(2,1)S(1)} %get-tuple-element.54), channel_id=1, source_target_pairs={{0,120},{1,121},{2,122},{3,123},{4,12},{5,13},{6,14},{7,15},{8,0},... | collective-permute-start | bytes 786440 | tf_op jit(solution)/shard_map/ppermute | solution.py:377
  40.1 14.7 %collective-permute-start.8 = (bf16[32,32,128]{2,1,0:T(8,128)(2,1)S(1)}, bf16[32,32,128]{2,1,0:T(8,128)(2,1)S(1)}, u32[]{:S(2)}, u32[]{:S(2)}) collective-permute-start(bf16[32,32,128]{2,1,0:T(8,128)(2,1)S(1)} %select_convert_fusion.1), channel_id=1, source_target_pairs={{0,2},{1,3},{2,0},{3,1},{4,6},{5,7},{6,4},{7,5},{8,10},{9,11},{10,... | collective-permute-start | bytes 786440 | tf_op jit(solution)/shard_map/ppermute | solution.py:377
  44.5 18.5 %collective-permute-start.6 = (bf16[64,32,128]{2,1,0:T(8,128)(2,1)S(1)}, bf16[64,32,128]{2,1,0:T(8,128)(2,1)S(1)}, u32[]{:S(2)}, u32[]{:S(2)}) collective-permute-start(bf16[64,32,128]{2,1,0:T(8,128)(2,1)S(1)} %add_convert_fusion.2), channel_id=1, source_target_pairs={{0,120},{1,121},{2,122},{3,123},{4,12},{5,13},{6,14},{7,15},{8,0},... | collective-permute-start | bytes 1572872 | tf_op jit(solution)/shard_map/ppermute | solution.py:377
  54.9 8.1 %collective-permute-start.9 = (bf16[32,32,128]{2,1,0:T(8,128)(2,1)S(1)}, bf16[32,32,128]{2,1,0:T(8,128)(2,1)S(1)}, u32[]{:S(2)}, u32[]{:S(2)}) collective-permute-start(bf16[32,32,128]{2,1,0:T(8,128)(2,1)S(1)} %select_convert_fusion), channel_id=1, source_target_pairs={{0,2},{1,3},{2,0},{3,1},{4,6},{5,7},{6,4},{7,5},{8,10},{9,11},{10,... | collective-permute-start | bytes 786440 | tf_op jit(solution)/shard_map/ppermute | solution.py:377
  67.4 12.9 %collective-permute-start.14 = (bf16[64,32,128]{2,1,0:T(8,128)(2,1)S(1)}, bf16[64,32,128]{2,1,0:T(8,128)(2,1)S(1)}, u32[]{:S(2)}, u32[]{:S(2)}) collective-permute-start(bf16[64,32,128]{2,1,0:T(8,128)(2,1)S(1)} %get-tuple-element.49.refs_4_), channel_id=1, source_target_pairs={{0,2},{1,3},{2,0},{3,1},{4,6},{5,7},{6,4},{7,5},{8,10},{9,11},{10,... | collective-permute-start | bytes 1572872 | tf_op jit(solution)/shard_map/ppermute | solution.py:377
  68.0 14.3 %collective-permute-start.13 = (bf16[64,32,128]{2,1,0:T(8,128)(2,1)S(1)}, bf16[64,32,128]{2,1,0:T(8,128)(2,1)S(1)}, u32[]{:S(2)}, u32[]{:S(2)}) collective-permute-start(bf16[64,32,128]{2,1,0:T(8,128)(2,1)S(1)} %get-tuple-element.49.refs_4_), channel_id=1, source_target_pairs={{0,8},{1,9},{2,10},{3,11},{4,124},{5,125},{6,126},{7,127},{8,16},{... | collective-permute-start | bytes 1572872 | tf_op jit(solution)/shard_map/ppermute | solution.py:377
  68.0 24.7 %collective-permute-start.20 = (bf16[64,32,128]{2,1,0:T(8,128)(2,1)S(1)}, bf16[64,32,128]{2,1,0:T(8,128)(2,1)S(1)}, u32[]{:S(2)}, u32[]{:S(2)}) collective-permute-start(bf16[64,32,128]{2,1,0:T(8,128)(2,1)S(1)} %get-tuple-element.50), channel_id=1, source_target_pairs={{0,4},{1,5},{2,6},{3,7},{4,0},{5,1},{6,2},{7,3},{8,12},{9,13},{10,... | collective-permute-start | bytes 1572872 | tf_op jit(solution)/shard_map/ppermute | solution.py:377
  71.6 24.2 %collective-permute-start.21 = (bf16[64,32,128]{2,1,0:T(8,128)(2,1)S(1)}, bf16[64,32,128]{2,1,0:T(8,128)(2,1)S(1)}, u32[]{:S(2)}, u32[]{:S(2)}) collective-permute-start(bf16[64,32,128]{2,1,0:T(8,128)(2,1)S(1)} %get-tuple-element.50), channel_id=1, source_target_pairs={{0,6},{1,7},{2,4},{3,5},{4,2},{5,3},{6,0},{7,1},{8,14},{9,15},{10,... | collective-permute-start | bytes 1572872 | tf_op jit(solution)/shard_map/ppermute | solution.py:377
  72.8 22.9 %collective-permute-start.18 = (bf16[64,32,128]{2,1,0:T(8,128)(2,1)S(1)}, bf16[64,32,128]{2,1,0:T(8,128)(2,1)S(1)}, u32[]{:S(2)}, u32[]{:S(2)}) collective-permute-start(bf16[64,32,128]{2,1,0:T(8,128)(2,1)S(1)} %get-tuple-element.49.refs_4_), channel_id=1, source_target_pairs={{0,1},{1,0},{2,3},{3,2},{4,5},{5,4},{6,7},{7,6},{8,9},{9,8},{10,11... | collective-permute-start | bytes 1572872 | tf_op jit(solution)/shard_map/ppermute | solution.py:377
  80.2 16.0 %collective-permute-start.15 = (bf16[64,32,128]{2,1,0:T(8,128)(2,1)S(1)}, bf16[64,32,128]{2,1,0:T(8,128)(2,1)S(1)}, u32[]{:S(2)}, u32[]{:S(2)}) collective-permute-start(bf16[64,32,128]{2,1,0:T(8,128)(2,1)S(1)} %collective-permute-done.14.refs_5_), channel_id=1, source_target_pairs={{0,8},{1,9},{2,10},{3,11},{4,124},{5,125},{6,126},{7,127},{8,16},{... | collective-permute-start | bytes 1572872 | tf_op jit(solution)/shard_map/ppermute | solution.py:377
  82.3 16.5 %collective-permute-start.19 = (bf16[64,32,128]{2,1,0:T(8,128)(2,1)S(1)}, bf16[64,32,128]{2,1,0:T(8,128)(2,1)S(1)}, u32[]{:S(2)}, u32[]{:S(2)}) collective-permute-start(bf16[64,32,128]{2,1,0:T(8,128)(2,1)S(1)} %collective-permute-done.14.refs_5_), channel_id=1, source_target_pairs={{0,1},{1,0},{2,3},{3,2},{4,5},{5,4},{6,7},{7,6},{8,9},{9,8},{10,11... | collective-permute-start | bytes 1572872 | tf_op jit(solution)/shard_map/ppermute | solution.py:377
  92.7 6.0 %collective-permute-start.16 = (bf16[64,32,128]{2,1,0:T(8,128)(2,1)S(1)}, bf16[64,32,128]{2,1,0:T(8,128)(2,1)S(1)}, u32[]{:S(2)}, u32[]{:S(2)}) collective-permute-start(bf16[64,32,128]{2,1,0:T(8,128)(2,1)S(1)} %collective-permute-done.13.refs_0_), channel_id=1, source_target_pairs={{0,1},{1,0},{2,3},{3,2},{4,5},{5,4},{6,7},{7,6},{8,9},{9,8},{10,11... | collective-permute-start | bytes 1572872 | tf_op jit(solution)/shard_map/ppermute | solution.py:377
  95.8 3.0 %collective-permute-start.22 = (bf16[64,32,128]{2,1,0:T(8,128)(2,1)S(1)}, bf16[64,32,128]{2,1,0:T(8,128)(2,1)S(1)}, u32[]{:S(2)}, u32[]{:S(2)}) collective-permute-start(bf16[64,32,128]{2,1,0:T(8,128)(2,1)S(1)} %collective-permute-done.20.refs_8_), channel_id=1, source_target_pairs={{0,1},{1,0},{2,3},{3,2},{4,5},{5,4},{6,7},{7,6},{8,9},{9,8},{10,11... | collective-permute-start | bytes 1572872 | tf_op jit(solution)/shard_map/ppermute | solution.py:377
  95.8 3.0 %collective-permute-start.23 = (bf16[64,32,128]{2,1,0:T(8,128)(2,1)S(1)}, bf16[64,32,128]{2,1,0:T(8,128)(2,1)S(1)}, u32[]{:S(2)}, u32[]{:S(2)}) collective-permute-start(bf16[64,32,128]{2,1,0:T(8,128)(2,1)S(1)} %collective-permute-done.21.refs_9_), channel_id=1, source_target_pairs={{0,1},{1,0},{2,3},{3,2},{4,5},{5,4},{6,7},{7,6},{8,9},{9,8},{10,11... | collective-permute-start | bytes 1572872 | tf_op jit(solution)/shard_map/ppermute | solution.py:377
  96.3 3.8 %collective-permute-start.17 = (bf16[64,32,128]{2,1,0:T(8,128)(2,1)S(1)}, bf16[64,32,128]{2,1,0:T(8,128)(2,1)S(1)}, u32[]{:S(2)}, u32[]{:S(2)}) collective-permute-start(bf16[64,32,128]{2,1,0:T(8,128)(2,1)S(1)} %collective-permute-done.15.refs_1_), channel_id=1, source_target_pairs={{0,1},{1,0},{2,3},{3,2},{4,5},{5,4},{6,7},{7,6},{8,9},{9,8},{10,11... | collective-permute-start | bytes 1572872 | tf_op jit(solution)/shard_map/ppermute | solution.py:377
